TPU v7x, 32 devices: a whole 2x2x4 slice. The times are simulated.
32 devices in a mesh: blk: 4 (over z), batch: 2 (over y), vocab: 4 (over x, core).
Axes of the slice: x: 2, y: 2, z: 4, core: 2. Of those that a mesh axis runs over, the one named last changes fastest.
Arguments:
- hidden: bfloat16 [8, 1024, 768], P(('batch', 'vocab'), 'blk'), may hold values from -6 to 6
- lengths: int32 [8], P(('batch', 'vocab')), may hold values from 64 to 1024, as said below
- student_first_gain: bfloat16 [768], P(('blk', 'batch', 'vocab')), may hold values from 0.5 to 1.5
- student_first_shift: bfloat16 [768], P(('blk', 'batch', 'vocab')), may hold values from -1.5 to 1.5
- student_attend_weight: bfloat16 [768, 2304], P(('blk', 'batch', 'vocab')), may hold values from -0.21875 to 0.21875
- student_attend_bias: bfloat16 [1536], P(('blk', 'batch', 'vocab')), may hold values from -1.5 to 1.5
- student_output_weight: bfloat16 [768, 768], P(('blk', 'batch', 'vocab')), may hold values from -0.625 to 0.625
- student_output_bias: bfloat16 [768], P(('blk', 'batch', 'vocab')), may hold values from -1.5 to 1.5
- student_second_gain: bfloat16 [768], P(('blk', 'batch', 'vocab')), may hold values from 0.5 to 1.5
- student_second_shift: bfloat16 [768], P(('blk', 'batch', 'vocab')), may hold values from -1.5 to 1.5
- student_expand_weight: bfloat16 [768, 3072], P(('blk', 'batch', 'vocab')), may hold values from -0.21875 to 0.21875
- student_expand_bias: bfloat16 [3072], P(('blk', 'batch', 'vocab')), may hold values from -1.5 to 1.5
- student_reduce_weight: bfloat16 [3072, 768], P(('blk', 'batch', 'vocab')), may hold values from -0.109375 to 0.109375
- student_reduce_bias: bfloat16 [768], P(('blk', 'batch', 'vocab')), may hold values from -1.5 to 1.5
- teacher_first_gain: bfloat16 [768], P(('blk', 'batch', 'vocab')), may hold values from 0.5 to 1.5
- teacher_first_shift: bfloat16 [768], P(('blk', 'batch', 'vocab')), may hold values from -1.5 to 1.5
- teacher_attend_weight: bfloat16 [768, 2304], P(('blk', 'batch', 'vocab')), may hold values from -0.21875 to 0.21875
- teacher_attend_bias: bfloat16 [1536], P(('blk', 'batch', 'vocab')), may hold values from -1.5 to 1.5
- teacher_output_weight: bfloat16 [768, 768], P(('blk', 'batch', 'vocab')), may hold values from -0.625 to 0.625
- teacher_output_bias: bfloat16 [768], P(('blk', 'batch', 'vocab')), may hold values from -1.5 to 1.5
- teacher_second_gain: bfloat16 [768], P(('blk', 'batch', 'vocab')), may hold values from 0.5 to 1.5
- teacher_second_shift: bfloat16 [768], P(('blk', 'batch', 'vocab')), may hold values from -1.5 to 1.5
- teacher_expand_weight: bfloat16 [768, 3072], P(('blk', 'batch', 'vocab')), may hold values from -0.21875 to 0.21875
- teacher_expand_bias: bfloat16 [3072], P(('blk', 'batch', 'vocab')), may hold values from -1.5 to 1.5
- teacher_reduce_weight: bfloat16 [3072, 768], P(('blk', 'batch', 'vocab')), may hold values from -0.109375 to 0.109375
- teacher_reduce_bias: bfloat16 [768], P(('blk', 'batch', 'vocab')), may hold values from -1.5 to 1.5
- final_gain: bfloat16 [768], replicated, may hold values from 0.5 to 1.5
- final_shift: bfloat16 [768], replicated, may hold values from -1.5 to 1.5
- embedding: bfloat16 [50304, 768], P('vocab'), may hold values from -0.59765625 to 0.59765625
Outputs:
- grad_student_first_gain: float32 [768], P(('blk', 'batch', 'vocab'))
- grad_student_first_shift: float32 [768], P(('blk', 'batch', 'vocab'))
- grad_student_attend_weight: float32 [768, 2304], P(('blk', 'batch', 'vocab'))
- grad_student_attend_bias: float32 [1536], P(('blk', 'batch', 'vocab'))
- grad_student_output_weight: float32 [768, 768], P(('blk', 'batch', 'vocab'))
- grad_student_output_bias: float32 [768], P(('blk', 'batch', 'vocab'))
- grad_student_second_gain: float32 [768], P(('blk', 'batch', 'vocab'))
- grad_student_second_shift: float32 [768], P(('blk', 'batch', 'vocab'))
- grad_student_expand_weight: float32 [768, 3072], P(('blk', 'batch', 'vocab'))
- grad_student_expand_bias: float32 [3072], P(('blk', 'batch', 'vocab'))
- grad_student_reduce_weight: float32 [3072, 768], P(('blk', 'batch', 'vocab'))
- grad_student_reduce_bias: float32 [768], P(('blk', 'batch', 'vocab'))
- grad_teacher_first_gain: float32 [768], P(('blk', 'batch', 'vocab'))
- grad_teacher_first_shift: float32 [768], P(('blk', 'batch', 'vocab'))
- grad_teacher_attend_weight: float32 [768, 2304], P(('blk', 'batch', 'vocab'))
- grad_teacher_attend_bias: float32 [1536], P(('blk', 'batch', 'vocab'))
- grad_teacher_output_weight: float32 [768, 768], P(('blk', 'batch', 'vocab'))
- grad_teacher_output_bias: float32 [768], P(('blk', 'batch', 'vocab'))
- grad_teacher_second_gain: float32 [768], P(('blk', 'batch', 'vocab'))
- grad_teacher_second_shift: float32 [768], P(('blk', 'batch', 'vocab'))
- grad_teacher_expand_weight: float32 [768, 3072], P(('blk', 'batch', 'vocab'))
- grad_teacher_expand_bias: float32 [3072], P(('blk', 'batch', 'vocab'))
- grad_teacher_reduce_weight: float32 [3072, 768], P(('blk', 'batch', 'vocab'))
- grad_teacher_reduce_bias: float32 [768], P(('blk', 'batch', 'vocab'))
- input_grad: float32 [8, 1024, 768], P(('batch', 'vocab'), 'blk')
- kl: float32 [8, 1024], P(('batch', 'vocab'), 'blk')
Inputs may be any that keep to these rules, and one draw needn't show every extreme that they name: `lengths`: in each run of 4 consecutive sequences counted from the first, at least one sequence has length 1024.
All inputs are finite; a program needn't handle non-finite values.
Results may differ from a plain program's by a relative error of at most 0.025.
Values may be sent and summed in bfloat16 or wider, within the bound.
No kernel may reach another device: no remote copies, remote signals or barrier semaphores. Data moves between devices by JAX's collectives and lax.ppermute only.
A program may use at most 256 MiB of HBM per device.

v0:
```python
import functools
import math

import jax
import jax.numpy as jnp
from jax import lax
from jax.experimental import pallas as pl
from jax.experimental.pallas import tpu as pltpu
from jax.sharding import PartitionSpec as P

HEADS = 12
HEAD = 64
VOCAB_REAL = 50257
BLK, BATCH, VOCAB = "blk", "batch", "vocab"
EVERY = (BLK, BATCH, VOCAB)


def for_sending(shard):
    return jax.tree.map(lambda a: a.astype(jnp.bfloat16) if a.dtype == jnp.float32 else a, shard)


def layer_norm(inputs, gain_row, shift_row):
    centred = inputs - jnp.mean(inputs, axis=-1, keepdims=True)
    spread = jnp.mean(centred * centred, axis=-1, keepdims=True)
    return centred * lax.rsqrt(spread + 1e-05) * gain_row + shift_row


def gelu_tanh(inputs):
    return jax.nn.gelu(inputs, approximate=True)


def matmul_plain(left_side, right_side):
    return jnp.dot(left_side, right_side, preferred_element_type=jnp.float32)


def matmul_right_t(left_side, right_side):
    return lax.dot_general(
        left_side, right_side, (((1,), (1,)), ((), ())), preferred_element_type=jnp.float32
    )


def matmul_left_t(left_side, right_side):
    return lax.dot_general(
        left_side, right_side, (((0,), (0,)), ((), ())), preferred_element_type=jnp.float32
    )


def column_sums(rows_low):
    return jnp.sum(rows_low.astype(jnp.float32), axis=0)


def split_heads(rows_flat):
    return rows_flat.reshape(rows_flat.shape[0], rows_flat.shape[1], HEADS, HEAD)


def front_half(inputs, params):
    model_width = inputs.shape[-1]
    normed_one = layer_norm(
        inputs, params[0].astype(jnp.float32), params[1].astype(jnp.float32)
    ).astype(jnp.bfloat16)
    joined = matmul_plain(normed_one.reshape(-1, model_width), params[2])
    bias_row = params[3].astype(jnp.float32)
    query_rows = (
        (joined[:, :model_width] + bias_row[:model_width])
        .astype(jnp.bfloat16)
        .reshape(inputs.shape)
    )
    key_rows = joined[:, model_width : 2 * model_width].astype(jnp.bfloat16).reshape(inputs.shape)
    value_rows = (
        (joined[:, 2 * model_width :] + bias_row[model_width:])
        .astype(jnp.bfloat16)
        .reshape(inputs.shape)
    )
    return (normed_one.reshape(-1, model_width), query_rows, key_rows, value_rows)


def attend_block(carried, block_in, first_row, queries, query_pos, seq_lengths):
    head_scale = HEAD ** (-0.5)
    key_count = block_in[0].shape[1]
    key_pos = jnp.arange(key_count, dtype=jnp.int32)
    allowed = (
        (key_pos[None, None, :] <= query_pos[None, :, None])
        & (key_pos[None, None, :] < seq_lengths[:, None, None])
    )[:, None]
    skipped = (first_row > query_pos[-1]) | (first_row >= jnp.max(seq_lengths))

    def attend_update():
        results = []
        for model_index in range(2):
            running, row_max, row_total = carried[model_index]
            key_rows = split_heads(block_in[2 * model_index])
            value_rows = split_heads(block_in[2 * model_index + 1])
            scores = (
                jnp.einsum(
                    "sqhd,skhd->shqk",
                    queries[model_index],
                    key_rows,
                    preferred_element_type=jnp.float32,
                )
                * head_scale
            )
            new_max = jnp.maximum(row_max, jnp.max(jnp.where(allowed, scores, -1e30), axis=-1))
            weights = jnp.where(allowed, jnp.exp(scores - new_max[..., None]), 0.0)
            row_total = jnp.sum(weights, axis=-1)
            running = jnp.einsum(
                "shqk,skhd->shqd",
                weights.astype(jnp.bfloat16),
                value_rows,
                preferred_element_type=jnp.float32,
            )
            results.append((running, new_max, row_total))
        return tuple(results)

    return lax.cond(skipped, lambda: carried, attend_update)


def query_grad_block(
    carried, block_in, first_row, queries, grads_heads, log_totals, deltas, query_pos, seq_lengths
):
    head_scale = HEAD ** (-0.5)
    key_count = block_in[0].shape[1]
    key_pos = jnp.arange(key_count, dtype=jnp.int32)
    allowed = (
        (key_pos[None, None, :] <= query_pos[None, :, None])
        & (key_pos[None, None, :] < seq_lengths[:, None, None])
    )[:, None]
    skipped = (first_row > query_pos[-1]) | (first_row >= jnp.max(seq_lengths))

    def query_update():
        results = []
        for model_index in range(2):
            key_rows = split_heads(block_in[2 * model_index])
            value_rows = split_heads(block_in[2 * model_index + 1])
            scores = (
                jnp.einsum(
                    "sqhd,skhd->shqk",
                    queries[model_index],
                    key_rows,
                    preferred_element_type=jnp.float32,
                )
                * head_scale
            )
            prob_rows = jnp.where(
                allowed, jnp.exp(scores - log_totals[model_index][..., None]), 0.0
            )
            grad_prob = jnp.einsum(
                "sqhd,skhd->shqk",
                grads_heads[model_index],
                value_rows,
                preferred_element_type=jnp.float32,
            )
            grad_scores = (prob_rows * (grad_prob - deltas[model_index][..., None])).astype(
                jnp.bfloat16
            )
            results.append(
                carried[model_index]
                + jnp.einsum(
                    "shqk,skhd->shqd", grad_scores, key_rows, preferred_element_type=jnp.float32
                )
                * head_scale
            )
        return tuple(results)

    return lax.cond(skipped, lambda: carried, query_update)


def key_grad_block(carried, block_in, first_row, keys_local, values_local, key_pos, seq_lengths):
    head_scale = HEAD ** (-0.5)
    query_count = block_in[0].shape[1]
    query_pos = jnp.arange(query_count, dtype=jnp.int32)
    allowed = (
        (key_pos[None, None, :] <= query_pos[None, :, None])
        & (key_pos[None, None, :] < seq_lengths[:, None, None])
    )[:, None]
    skipped = (first_row + query_count - 1 < key_pos[0]) | (key_pos[0] >= jnp.max(seq_lengths))

    def key_update():
        results = []
        for model_index in range(2):
            grad_keys, grad_values = carried[model_index]
            query_rows = split_heads(block_in[4 * model_index])
            grad_rows = split_heads(block_in[4 * model_index + 1])
            log_rows = jnp.transpose(block_in[4 * model_index + 2], (0, 2, 1))
            delta_rows = jnp.transpose(block_in[4 * model_index + 3], (0, 2, 1))
            scores = (
                jnp.einsum(
                    "sqhd,skhd->shqk",
                    query_rows,
                    keys_local[model_index],
                    preferred_element_type=jnp.float32,
                )
                * head_scale
            )
            prob_rows = jnp.where(allowed, jnp.exp(scores - log_rows[..., None]), 0.0)
            grad_values = grad_values + jnp.einsum(
                "shqk,sqhd->shkd",
                prob_rows.astype(jnp.bfloat16),
                grad_rows,
                preferred_element_type=jnp.float32,
            )
            grad_prob = jnp.einsum(
                "sqhd,skhd->shqk",
                grad_rows,
                values_local[model_index],
                preferred_element_type=jnp.float32,
            )
            grad_scores = (prob_rows * (grad_prob - delta_rows[..., None])).astype(jnp.bfloat16)
            grad_keys = (
                grad_keys
                + jnp.einsum(
                    "shqk,sqhd->shkd", grad_scores, query_rows, preferred_element_type=jnp.float32
                )
                * head_scale
            )
            results.append((grad_keys, grad_values))
        return tuple(results)

    return lax.cond(skipped, lambda: carried, key_update)


def shards(
    hidden,
    lengths,
    student_first_gain,
    student_first_shift,
    student_attend_weight,
    student_attend_bias,
    student_output_weight,
    student_output_bias,
    student_second_gain,
    student_second_shift,
    student_expand_weight,
    student_expand_bias,
    student_reduce_weight,
    student_reduce_bias,
    teacher_first_gain,
    teacher_first_shift,
    teacher_attend_weight,
    teacher_attend_bias,
    teacher_output_weight,
    teacher_output_bias,
    teacher_second_gain,
    teacher_second_shift,
    teacher_expand_weight,
    teacher_expand_bias,
    teacher_reduce_weight,
    teacher_reduce_bias,
    final_gain,
    final_shift,
    embedding,
):
    gathered = (
        lax.all_gather(student_first_gain, EVERY, axis=0, tiled=True),
        lax.all_gather(student_first_shift, EVERY, axis=0, tiled=True),
        lax.all_gather(student_attend_weight, EVERY, axis=0, tiled=True),
        lax.all_gather(student_attend_bias, EVERY, axis=0, tiled=True),
        lax.all_gather(student_output_weight, EVERY, axis=0, tiled=True),
        lax.all_gather(student_output_bias, EVERY, axis=0, tiled=True),
        lax.all_gather(student_second_gain, EVERY, axis=0, tiled=True),
        lax.all_gather(student_second_shift, EVERY, axis=0, tiled=True),
        lax.all_gather(student_expand_weight, EVERY, axis=0, tiled=True),
        lax.all_gather(student_expand_bias, EVERY, axis=0, tiled=True),
        lax.all_gather(student_reduce_weight, EVERY, axis=0, tiled=True),
        lax.all_gather(student_reduce_bias, EVERY, axis=0, tiled=True),
        lax.all_gather(teacher_first_gain, EVERY, axis=0, tiled=True),
        lax.all_gather(teacher_first_shift, EVERY, axis=0, tiled=True),
        lax.all_gather(teacher_attend_weight, EVERY, axis=0, tiled=True),
        lax.all_gather(teacher_attend_bias, EVERY, axis=0, tiled=True),
        lax.all_gather(teacher_output_weight, EVERY, axis=0, tiled=True),
        lax.all_gather(teacher_output_bias, EVERY, axis=0, tiled=True),
        lax.all_gather(teacher_second_gain, EVERY, axis=0, tiled=True),
        lax.all_gather(teacher_second_shift, EVERY, axis=0, tiled=True),
        lax.all_gather(teacher_expand_weight, EVERY, axis=0, tiled=True),
        lax.all_gather(teacher_expand_bias, EVERY, axis=0, tiled=True),
        lax.all_gather(teacher_reduce_weight, EVERY, axis=0, tiled=True),
        lax.all_gather(teacher_reduce_bias, EVERY, axis=0, tiled=True),
    )
    models = (tuple(gathered[:12]), tuple(gathered[12:]))
    batch_seqs, rows_local, model_width = hidden.shape
    row_count = batch_seqs * rows_local
    inputs = hidden.astype(jnp.float32)
    inputs_flat = inputs.reshape(row_count, model_width)
    query_pos = lax.axis_index(BLK) * rows_local + jnp.arange(rows_local, dtype=jnp.int32)
    fronts = [front_half(inputs, params) for params in models]
    queries = (split_heads(fronts[0][1]), split_heads(fronts[1][1]))
    zero_heads = jnp.zeros((batch_seqs, HEADS, rows_local, HEAD), jnp.float32)
    zero_rows = jnp.zeros((batch_seqs, HEADS, rows_local), jnp.float32)
    start_state = (
        zero_heads,
        jnp.full((batch_seqs, HEADS, rows_local), -1e30, jnp.float32),
        zero_rows,
    )
    folded = attend_block(
        (start_state, start_state),
        (
            lax.all_gather(fronts[0][2], BLK, axis=1, tiled=True),
            lax.all_gather(fronts[0][3], BLK, axis=1, tiled=True),
            lax.all_gather(fronts[1][2], BLK, axis=1, tiled=True),
            lax.all_gather(fronts[1][3], BLK, axis=1, tiled=True),
        ),
        jnp.int32(0),
        queries,
        query_pos,
        lengths,
    )
    gain_final = final_gain.astype(jnp.float32)
    shift_final = final_shift.astype(jnp.float32)
    caches = []
    final_rows = []
    for model_index in range(2):
        params = models[model_index]
        running, row_max, row_total = folded[model_index]
        mixed_rows = (
            jnp.transpose(running / row_total[..., None], (0, 2, 1, 3))
            .reshape(row_count, model_width)
            .astype(jnp.bfloat16)
        )
        log_total = row_max + jnp.log(row_total)
        middle = inputs_flat + matmul_plain(mixed_rows, params[4]) + params[5].astype(jnp.float32)
        normed_two = layer_norm(
            middle, params[6].astype(jnp.float32), params[7].astype(jnp.float32)
        ).astype(jnp.bfloat16)
        inner_rows = matmul_plain(normed_two, params[8]) + params[9].astype(jnp.float32)
        active = gelu_tanh(inner_rows).astype(jnp.bfloat16)
        block_out = middle + matmul_plain(active, params[10]) + params[11].astype(jnp.float32)
        final_rows.append(layer_norm(block_out, gain_final, shift_final).astype(jnp.bfloat16))
        caches.append((mixed_rows, log_total, middle, normed_two, inner_rows, active, block_out))
    all_rows = lax.all_gather(jnp.stack(final_rows), VOCAB, axis=1, tiled=True)
    vocab_local = embedding.shape[0]
    vocab_index = lax.axis_index(VOCAB)
    column_valid = (
        vocab_index * vocab_local + jnp.arange(vocab_local, dtype=jnp.int32) < VOCAB_REAL
    )[None, :]
    total_rows = all_rows.shape[1]

    def scaled_logits(rows_pair):
        scaled_student = jnp.where(
            column_valid, matmul_right_t(rows_pair[0], embedding) * 0.5, -1e30
        )
        scaled_teacher = jnp.where(
            column_valid, matmul_right_t(rows_pair[1], embedding) * 0.5, -1e30
        )
        return (scaled_student, scaled_teacher)

    stat_rows = math.gcd(total_rows, 512)

    def local_stats(block_index):
        rows_pair = lax.dynamic_slice_in_dim(all_rows, block_index * stat_rows, stat_rows, 1)
        scaled_student, scaled_teacher = scaled_logits(rows_pair)
        max_student = jnp.max(scaled_student, axis=-1)
        max_teacher = jnp.max(scaled_teacher, axis=-1)
        exp_student = jnp.where(column_valid, jnp.exp(scaled_student - max_student[:, None]), 0.0)
        exp_teacher = jnp.where(column_valid, jnp.exp(scaled_teacher - max_teacher[:, None]), 0.0)
        cross_sum = jnp.sum(exp_teacher * (scaled_teacher - scaled_student), axis=-1)
        return (
            max_student,
            jnp.sum(exp_student, axis=-1),
            max_teacher,
            jnp.sum(exp_teacher, axis=-1),
            cross_sum,
        )

    stat_blocks = lax.map(local_stats, jnp.arange(total_rows // stat_rows))
    max_student, sum_student, max_teacher, sum_teacher, cross_sum = [
        stat_block.reshape(total_rows) for stat_block in stat_blocks
    ]
    top_student, top_teacher = lax.pmax((max_student, max_teacher), VOCAB)
    factor_student = jnp.exp(max_student - top_student)
    factor_teacher = jnp.exp(max_teacher - top_teacher)
    sum_student, sum_teacher, cross_sum = lax.psum(
        (sum_student * factor_student, sum_teacher * factor_teacher, cross_sum * factor_teacher),
        VOCAB,
    )
    max_student, max_teacher = (top_student, top_teacher)
    lse_student = max_student + jnp.log(sum_student)
    lse_teacher = max_teacher + jnp.log(sum_teacher)
    divergence_rows = cross_sum / sum_teacher - lse_teacher + lse_student
    valid_rows = (query_pos[None, :] < lengths[:, None]).astype(jnp.float32)
    own_start = vocab_index * row_count
    kl_out = (
        4.0
        * lax.dynamic_slice_in_dim(divergence_rows, own_start, row_count).reshape(
            batch_seqs, rows_local
        )
        * valid_rows
    )
    step_rows = math.gcd(row_count * lax.axis_size(VOCAB), 512)

    def one_block(block_index):
        begin = block_index * step_rows
        rows_pair = lax.dynamic_slice_in_dim(all_rows, begin, step_rows, 1)
        scaled_student, scaled_teacher = scaled_logits(rows_pair)
        log_student = (
            scaled_student - lax.dynamic_slice_in_dim(lse_student, begin, step_rows)[:, None]
        )
        log_teacher = (
            scaled_teacher - lax.dynamic_slice_in_dim(lse_teacher, begin, step_rows)[:, None]
        )
        row_kl = lax.dynamic_slice_in_dim(divergence_rows, begin, step_rows)[:, None]
        prob_student = jnp.where(column_valid, jnp.exp(log_student), 0.0)
        prob_teacher = jnp.where(column_valid, jnp.exp(log_teacher), 0.0)
        grad_student = (2.0 * (prob_student - prob_teacher)).astype(jnp.bfloat16)
        grad_teacher = (2.0 * prob_teacher * (log_teacher - log_student - row_kl)).astype(
            jnp.bfloat16
        )
        return jnp.concatenate(
            [matmul_plain(grad_student, embedding), matmul_plain(grad_teacher, embedding)], axis=1
        )

    grad_final = (
        lax.psum_scatter(
            lax.map(one_block, jnp.arange(row_count * lax.axis_size(VOCAB) // step_rows))
            .reshape(row_count * lax.axis_size(VOCAB), 2 * model_width)
            .astype(jnp.bfloat16),
            VOCAB,
            scatter_dimension=0,
            tiled=True,
        ).astype(jnp.float32)
        * valid_rows.reshape(row_count)[:, None]
    )
    regathered = (
        lax.all_gather(student_first_gain, EVERY, axis=0, tiled=True),
        lax.all_gather(student_first_shift, EVERY, axis=0, tiled=True),
        lax.all_gather(student_attend_weight, EVERY, axis=0, tiled=True),
        lax.all_gather(student_attend_bias, EVERY, axis=0, tiled=True),
        lax.all_gather(student_output_weight, EVERY, axis=0, tiled=True),
        lax.all_gather(student_output_bias, EVERY, axis=0, tiled=True),
        lax.all_gather(student_second_gain, EVERY, axis=0, tiled=True),
        lax.all_gather(student_second_shift, EVERY, axis=0, tiled=True),
        lax.all_gather(student_expand_weight, EVERY, axis=0, tiled=True),
        lax.all_gather(student_expand_bias, EVERY, axis=0, tiled=True),
        lax.all_gather(student_reduce_weight, EVERY, axis=0, tiled=True),
        lax.all_gather(student_reduce_bias, EVERY, axis=0, tiled=True),
        lax.all_gather(teacher_first_gain, EVERY, axis=0, tiled=True),
        lax.all_gather(teacher_first_shift, EVERY, axis=0, tiled=True),
        lax.all_gather(teacher_attend_weight, EVERY, axis=0, tiled=True),
        lax.all_gather(teacher_attend_bias, EVERY, axis=0, tiled=True),
        lax.all_gather(teacher_output_weight, EVERY, axis=0, tiled=True),
        lax.all_gather(teacher_output_bias, EVERY, axis=0, tiled=True),
        lax.all_gather(teacher_second_gain, EVERY, axis=0, tiled=True),
        lax.all_gather(teacher_second_shift, EVERY, axis=0, tiled=True),
        lax.all_gather(teacher_expand_weight, EVERY, axis=0, tiled=True),
        lax.all_gather(teacher_expand_bias, EVERY, axis=0, tiled=True),
        lax.all_gather(teacher_reduce_weight, EVERY, axis=0, tiled=True),
        lax.all_gather(teacher_reduce_bias, EVERY, axis=0, tiled=True),
    )
    back_models = (tuple(regathered[:12]), tuple(regathered[12:]))
    uppers = []
    middle_pairs = []
    for model_index in range(2):
        params = back_models[model_index]
        mixed_rows, log_total, middle, normed_two, inner_rows, active, block_out = caches[
            model_index
        ]
        _, final_pull = jax.vjp(
            lambda rows_in: layer_norm(rows_in, gain_final, shift_final), block_out
        )
        grad_out = final_pull(
            grad_final[:, model_index * model_width : (model_index + 1) * model_width]
        )[0]
        branch_low = grad_out.astype(jnp.bfloat16)
        grad_reduce_bias = column_sums(branch_low)
        grad_active = matmul_right_t(branch_low, params[10])
        _, gelu_pull = jax.vjp(gelu_tanh, inner_rows)
        inner_grad = gelu_pull(grad_active)[0].astype(jnp.bfloat16)
        grad_expand_bias = column_sums(inner_grad)
        grad_normed_two = matmul_right_t(inner_grad, params[8])
        _, second_pull = jax.vjp(
            layer_norm, middle, params[6].astype(jnp.float32), params[7].astype(jnp.float32)
        )
        middle_part, grad_second_gain, grad_second_shift = second_pull(grad_normed_two)
        grad_middle = grad_out + middle_part
        attn_low = grad_middle.astype(jnp.bfloat16)
        grad_output_bias = column_sums(attn_low)
        grad_mixed = matmul_right_t(attn_low, params[4]).astype(jnp.bfloat16)
        delta_rows = jnp.sum(
            (grad_mixed.astype(jnp.float32) * mixed_rows.astype(jnp.float32)).reshape(
                batch_seqs, rows_local, HEADS, HEAD
            ),
            axis=-1,
        )
        uppers.append(
            (
                grad_output_bias,
                grad_second_gain,
                grad_second_shift,
                grad_expand_bias,
                grad_reduce_bias,
                grad_middle,
                grad_mixed.reshape(batch_seqs, rows_local, model_width),
                delta_rows,
            )
        )
        middle_pairs.append(
            ((mixed_rows, attn_low), (normed_two, inner_grad), (active, branch_low))
        )
    grads_heads = (split_heads(uppers[0][6]), split_heads(uppers[1][6]))
    log_totals = (caches[0][1], caches[1][1])
    deltas = (jnp.transpose(uppers[0][7], (0, 2, 1)), jnp.transpose(uppers[1][7], (0, 2, 1)))
    query_grads = query_grad_block(
        (zero_heads, zero_heads),
        (
            lax.all_gather(fronts[0][2], BLK, axis=1, tiled=True),
            lax.all_gather(fronts[0][3], BLK, axis=1, tiled=True),
            lax.all_gather(fronts[1][2], BLK, axis=1, tiled=True),
            lax.all_gather(fronts[1][3], BLK, axis=1, tiled=True),
        ),
        jnp.int32(0),
        queries,
        grads_heads,
        log_totals,
        deltas,
        query_pos,
        lengths,
    )
    keys_local = (split_heads(fronts[0][2]), split_heads(fronts[1][2]))
    values_local = (split_heads(fronts[0][3]), split_heads(fronts[1][3]))
    key_grads = key_grad_block(
        ((zero_heads, zero_heads), (zero_heads, zero_heads)),
        (
            lax.all_gather(fronts[0][1], BLK, axis=1, tiled=True),
            lax.all_gather(uppers[0][6], BLK, axis=1, tiled=True),
            lax.all_gather(
                for_sending(jnp.transpose(log_totals[0], (0, 2, 1))), BLK, axis=1, tiled=True
            ),
            lax.all_gather(uppers[0][7].astype(jnp.bfloat16), BLK, axis=1, tiled=True).astype(
                jnp.float32
            ),
            lax.all_gather(fronts[1][1], BLK, axis=1, tiled=True),
            lax.all_gather(uppers[1][6], BLK, axis=1, tiled=True),
            lax.all_gather(
                for_sending(jnp.transpose(log_totals[1], (0, 2, 1))), BLK, axis=1, tiled=True
            ),
            lax.all_gather(uppers[1][7].astype(jnp.bfloat16), BLK, axis=1, tiled=True).astype(
                jnp.float32
            ),
        ),
        jnp.int32(0),
        keys_local,
        values_local,
        query_pos,
        lengths,
    )
    vectors = []
    pairs = []
    input_grad = jnp.zeros((row_count, model_width), jnp.float32)
    for model_index in range(2):
        params = back_models[model_index]
        upper = uppers[model_index]
        grad_keys, grad_values = key_grads[model_index]
        joined_grad = jnp.concatenate(
            [
                jnp.transpose(query_grads[model_index], (0, 2, 1, 3)).reshape(
                    row_count, model_width
                ),
                jnp.transpose(grad_keys, (0, 2, 1, 3)).reshape(row_count, model_width),
                jnp.transpose(grad_values, (0, 2, 1, 3)).reshape(row_count, model_width),
            ],
            axis=1,
        ).astype(jnp.bfloat16)
        bias_sums = column_sums(joined_grad)
        grad_attend_bias = jnp.concatenate([bias_sums[:model_width], bias_sums[2 * model_width :]])
        grad_normed_one = matmul_right_t(joined_grad, params[2])
        _, first_pull = jax.vjp(
            layer_norm, inputs_flat, params[0].astype(jnp.float32), params[1].astype(jnp.float32)
        )
        input_part, grad_first_gain, grad_first_shift = first_pull(grad_normed_one)
        input_grad = input_grad + upper[5] + input_part
        vectors.append(
            [
                grad_first_gain,
                grad_first_shift,
                grad_attend_bias,
                upper[0],
                upper[1],
                upper[2],
                upper[3],
                upper[4],
            ]
        )
        pairs.append(
            [
                (fronts[model_index][0], joined_grad),
                middle_pairs[model_index][0],
                middle_pairs[model_index][1],
                middle_pairs[model_index][2],
            ]
        )
    grads = []
    for model_index in range(2):
        matrix_list = [matmul_left_t(pair[0], pair[1]) for pair in pairs[model_index]]
        vector_list = vectors[model_index]
        grads.extend(
            [
                vector_list[0],
                vector_list[1],
                matrix_list[0],
                vector_list[2],
                matrix_list[1],
                vector_list[3],
                vector_list[4],
                vector_list[5],
                matrix_list[2],
                vector_list[6],
                matrix_list[3],
                vector_list[7],
            ]
        )
    summed = (
        lax.psum_scatter(grads[0], EVERY, scatter_dimension=0, tiled=True),
        lax.psum_scatter(grads[1], EVERY, scatter_dimension=0, tiled=True),
        lax.psum_scatter(grads[2], EVERY, scatter_dimension=0, tiled=True),
        lax.psum_scatter(grads[3], EVERY, scatter_dimension=0, tiled=True),
        lax.psum_scatter(grads[4], EVERY, scatter_dimension=0, tiled=True),
        lax.psum_scatter(grads[5], EVERY, scatter_dimension=0, tiled=True),
        lax.psum_scatter(grads[6], EVERY, scatter_dimension=0, tiled=True),
        lax.psum_scatter(grads[7], EVERY, scatter_dimension=0, tiled=True),
        lax.psum_scatter(grads[8], EVERY, scatter_dimension=0, tiled=True),
        lax.psum_scatter(grads[9], EVERY, scatter_dimension=0, tiled=True),
        lax.psum_scatter(grads[10], EVERY, scatter_dimension=0, tiled=True),
        lax.psum_scatter(grads[11], EVERY, scatter_dimension=0, tiled=True),
        lax.psum_scatter(grads[12], EVERY, scatter_dimension=0, tiled=True),
        lax.psum_scatter(grads[13], EVERY, scatter_dimension=0, tiled=True),
        lax.psum_scatter(grads[14], EVERY, scatter_dimension=0, tiled=True),
        lax.psum_scatter(grads[15], EVERY, scatter_dimension=0, tiled=True),
        lax.psum_scatter(grads[16], EVERY, scatter_dimension=0, tiled=True),
        lax.psum_scatter(grads[17], EVERY, scatter_dimension=0, tiled=True),
        lax.psum_scatter(grads[18], EVERY, scatter_dimension=0, tiled=True),
        lax.psum_scatter(grads[19], EVERY, scatter_dimension=0, tiled=True),
        lax.psum_scatter(grads[20], EVERY, scatter_dimension=0, tiled=True),
        lax.psum_scatter(grads[21], EVERY, scatter_dimension=0, tiled=True),
        lax.psum_scatter(grads[22], EVERY, scatter_dimension=0, tiled=True),
        lax.psum_scatter(grads[23], EVERY, scatter_dimension=0, tiled=True),
    )
    return tuple(summed) + (input_grad.reshape(batch_seqs, rows_local, model_width), kl_out)


LANES = 128
MARGIN = 16.0
VMEM_BYTES = 60 * 1024 * 1024


def lane_fold(tile_in, combine):
    folded = tile_in[:, :LANES]
    for start in range(LANES, tile_in.shape[1], LANES):
        folded = combine(folded, tile_in[:, start : start + LANES])
    return folded


def whole_block(shape):
    return pl.BlockSpec(shape, lambda *_: (0,) * len(shape))


def vocab_stats_kernel(
    scalars_ref,
    student_low_ref,
    student_high_ref,
    teacher_low_ref,
    teacher_high_ref,
    embed_ref,
    logit_student_ref,
    logit_teacher_ref,
    stats_ref,
    tile_max_s,
    tile_max_t,
    max_s,
    max_t,
    sum_s,
    sum_t,
    cross,
    part_s,
    part_t,
    part_x,
    *,
    tile,
    rows_block,
):
    step_index = pl.program_id(0)
    steps = pl.num_programs(0)
    half_rows = student_low_ref.shape[1]
    rows = 2 * half_rows

    @pl.when(step_index == 0)
    def _():
        max_s[...] = jnp.full_like(max_s, -1e30)
        max_t[...] = jnp.full_like(max_t, -1e30)
        for total in (sum_s, sum_t, cross):
            total[...] = jnp.zeros_like(total)

    def sums(scaled_s, scaled_t, top_s, top_t):
        shifted_s = scaled_s - top_s
        shifted_t = scaled_t - top_t
        exp_s = jnp.exp(shifted_s)
        exp_t = jnp.exp(shifted_t)
        return (
            lane_fold(exp_s, jnp.add),
            lane_fold(exp_t, jnp.add),
            lane_fold(exp_t * (shifted_t - shifted_s), jnp.add),
        )

    def one_tile(masked):
        embed_tile = embed_ref[...]
        excess = None
        for start in range(0, rows, rows_block):
            here = pl.ds(start, rows_block)
            source = pl.ds(start % half_rows, rows_block)
            student_ref = student_low_ref if start < half_rows else student_high_ref
            teacher_ref = teacher_low_ref if start < half_rows else teacher_high_ref
            scaled_s = matmul_right_t(student_ref[0, source, :], embed_tile)
            scaled_t = matmul_right_t(teacher_ref[0, source, :], embed_tile)
            if masked:
                column = lax.broadcasted_iota(jnp.int32, (1, tile), 1) + step_index * tile
                scaled_s = jnp.where(column < scalars_ref[0], scaled_s, -1e30)
                scaled_t = jnp.where(column < scalars_ref[0], scaled_t, -1e30)
            logit_student_ref[here, :] = scaled_s
            logit_teacher_ref[here, :] = scaled_t
            tops_s = lane_fold(scaled_s, jnp.maximum)
            tops_t = lane_fold(scaled_t, jnp.maximum)
            tile_max_s[here, :] = tops_s
            tile_max_t[here, :] = tops_t
            old_s = max_s[here, :]
            old_t = max_t[here, :]
            part_s[here, :], part_t[here, :], part_x[here, :] = sums(
                scaled_s, scaled_t, old_s[:, :1], old_t[:, :1]
            )
            over = jnp.maximum(tops_s - old_s, tops_t - old_t)
            excess = over if excess is None else jnp.maximum(excess, over)

        @pl.when(jnp.max(excess) > MARGIN)
        def _():
            def rescale(chunk, _):
                here = pl.ds(pl.multiple_of(chunk * 64, 64), 64)
                old_s = max_s[here, :]
                old_t = max_t[here, :]
                new_s = jnp.maximum(old_s, jnp.max(tile_max_s[here, :], axis=1, keepdims=True))
                new_t = jnp.maximum(old_t, jnp.max(tile_max_t[here, :], axis=1, keepdims=True))
                factor_t = jnp.exp(old_t - new_t)
                moved = (old_t - old_s) - (new_t - new_s)
                max_s[here, :] = new_s
                max_t[here, :] = new_t
                sum_s[here, :] = sum_s[here, :] * jnp.exp(old_s - new_s)
                cross[here, :] = (cross[here, :] + moved * sum_t[here, :]) * factor_t
                sum_t[here, :] = sum_t[here, :] * factor_t
                part_s[here, :], part_t[here, :], part_x[here, :] = sums(
                    logit_student_ref[here, :],
                    logit_teacher_ref[here, :],
                    new_s[:, :1],
                    new_t[:, :1],
                )
                return 0

            lax.fori_loop(0, rows // 64, rescale, 0)

        sum_s[...] += part_s[...]
        sum_t[...] += part_t[...]
        cross[...] += part_x[...]

    @pl.when(step_index < steps - 1)
    def _():
        one_tile(False)

    @pl.when(step_index == steps - 1)
    def _():
        one_tile(True)
        lane = lax.broadcasted_iota(jnp.int32, (rows, LANES), 1)
        result = jnp.sum(cross[...], axis=1, keepdims=True)
        result = jnp.where(lane == 3, jnp.sum(sum_t[...], axis=1, keepdims=True), result)
        result = jnp.where(lane == 2, jnp.sum(sum_s[...], axis=1, keepdims=True), result)
        result = jnp.where(lane == 0, max_s[...], jnp.where(lane == 1, max_t[...], result))
        stats_ref[...] = result.T[:8, :]


def vocab_stats(final_parts, is_teacher, embedding, valid_columns, tile=1280, rows_block=256):
    _, half_rows, width = final_parts.shape
    rows = 2 * half_rows
    steps = pl.cdiv(embedding.shape[0], tile)
    logits = jax.ShapeDtypeStruct((rows, steps * tile), jnp.float32)
    part_spec = lambda teacher, second: pl.BlockSpec(
        (1, half_rows, width),
        lambda j, scalars: (2 * (scalars[1] ^ teacher) + second, 0, 0),
    )
    return pl.pallas_call(
        functools.partial(vocab_stats_kernel, tile=tile, rows_block=rows_block),
        grid_spec=pltpu.PrefetchScalarGridSpec(
            num_scalar_prefetch=1,
            grid=(steps,),
            in_specs=[part_spec(0, 0), part_spec(0, 1), part_spec(1, 0), part_spec(1, 1)]
            + [pl.BlockSpec((tile, width), lambda j, *_: (j, 0))],
            out_specs=[
                pl.BlockSpec((rows, tile), lambda j, *_: (0, j)),
                pl.BlockSpec((rows, tile), lambda j, *_: (0, j)),
                whole_block((8, rows)),
            ],
            scratch_shapes=[pltpu.VMEM((rows, LANES), jnp.float32)] * 10,
        ),
        out_shape=[logits, logits, jax.ShapeDtypeStruct((8, rows), jnp.float32)],
        compiler_params=pltpu.CompilerParams(vmem_limit_bytes=VMEM_BYTES),
        name="vocab_stats",
    )(
        jnp.stack([valid_columns, is_teacher.astype(jnp.int32)]),
        *[final_parts] * 4,
        embedding,
    )


def vocab_grads_kernel(
    logit_student_ref,
    logit_teacher_ref,
    embed_ref,
    *refs,
    tile,
    columns,
    rows_block,
    count,
):
    stat_refs = refs[:count]
    own_ref, send_ref, divergence_ref, row_ref, student_ref, teacher_ref = refs[count:]
    step_index = pl.program_id(0)
    rows = student_ref.shape[0]
    half_rows = rows // 2

    @pl.when(step_index == 0)
    def _():
        student_ref[...] = jnp.zeros_like(student_ref)
        teacher_ref[...] = jnp.zeros_like(teacher_ref)
        parts = []
        for index in range(count):
            part = stat_refs[index][...]
            if index % 2:
                part = jnp.concatenate([part[:, half_rows:], part[:, :half_rows]], axis=1)
            parts.append([part[k : k + 1, :] for k in range(5)])
        top_s = functools.reduce(jnp.maximum, [p[0] for p in parts])
        top_t = functools.reduce(jnp.maximum, [p[1] for p in parts])
        sum_s = sum(p[2] * jnp.exp(p[0] - top_s) for p in parts)
        sum_t = sum(p[3] * jnp.exp(p[1] - top_t) for p in parts)
        cross = sum((p[4] + (p[1] - p[0]) * p[3]) * jnp.exp(p[1] - top_t) for p in parts)
        lse_s = top_s + jnp.log(sum_s)
        lse_t = top_t + jnp.log(sum_t)
        mean_gap = cross / sum_t
        divergence_ref[...] = jnp.broadcast_to(mean_gap - lse_t + lse_s, divergence_ref.shape)
        line = lax.broadcasted_iota(jnp.int32, (LANES, rows), 0)
        row_ref[...] = jnp.where(line == 0, lse_s, jnp.where(line == 1, lse_t, mean_gap)).T

    def one_tile(masked):
        embed_tile = embed_ref[...]
        if masked:
            row = lax.broadcasted_iota(jnp.int32, (tile, 1), 0) + step_index * tile
            embed_tile = jnp.where(row < columns, embed_tile, jnp.zeros_like(embed_tile))
        for start in range(0, rows, rows_block):
            here = pl.ds(start, rows_block)
            scaled_s = logit_student_ref[here, :]
            scaled_t = logit_teacher_ref[here, :]
            prob_s = jnp.exp(scaled_s - row_ref[here, 0:1])
            prob_t = jnp.exp(scaled_t - row_ref[here, 1:2])
            grad_s = (prob_s - prob_t).astype(jnp.bfloat16)
            grad_t = (prob_t * ((scaled_t - scaled_s) - row_ref[here, 2:3])).astype(jnp.bfloat16)
            student_ref[here, :] += matmul_plain(grad_s, embed_tile)
            teacher_ref[here, :] += matmul_plain(grad_t, embed_tile)

    last = pl.num_programs(0) - 1

    @pl.when(step_index < last)
    def _():
        one_tile(False)

    @pl.when(step_index == last)
    def _():
        one_tile(True)
        for index, sums in enumerate((student_ref, teacher_ref)):
            own_ref[index] = sums[:half_rows, :]
            send_ref[index] = sums[half_rows:, :].astype(jnp.bfloat16)


def vocab_grads(logit_student, logit_teacher, embedding, stat_parts, tile=1280, rows_block=256):
    rows = logit_student.shape[0]
    columns, width = embedding.shape
    halves = (2, rows // 2, width)
    return pl.pallas_call(
        functools.partial(
            vocab_grads_kernel,
            tile=tile,
            columns=columns,
            rows_block=rows_block,
            count=len(stat_parts),
        ),
        grid=(pl.cdiv(columns, tile),),
        in_specs=[
            pl.BlockSpec((rows, tile), lambda j: (0, j)),
            pl.BlockSpec((rows, tile), lambda j: (0, j)),
            pl.BlockSpec((tile, width), lambda j: (j, 0)),
        ]
        + [whole_block((8, rows))] * len(stat_parts),
        out_specs=[whole_block(halves), whole_block(halves), whole_block((8, rows))],
        out_shape=[
            jax.ShapeDtypeStruct(halves, jnp.float32),
            jax.ShapeDtypeStruct(halves, jnp.bfloat16),
            jax.ShapeDtypeStruct((8, rows), jnp.float32),
        ],
        scratch_shapes=[
            pltpu.VMEM((rows, LANES), jnp.float32),
            pltpu.VMEM((rows, width), jnp.float32),
            pltpu.VMEM((rows, width), jnp.float32),
        ],
        compiler_params=pltpu.CompilerParams(vmem_limit_bytes=VMEM_BYTES),
        name="vocab_grads",
    )(logit_student, logit_teacher, embedding, *stat_parts)


def attend_kernel(length_ref, query_ref, key_ref, value_ref, mixed_ref, *, block):
    rows = query_ref.shape[0]
    lane = lax.broadcasted_iota(jnp.int32, (1, LANES), 1)
    for start in range(0, rows, block):
        keys = start + block
        key_pos = lax.broadcasted_iota(jnp.int32, (block, keys), 1)
        query_pos = lax.broadcasted_iota(jnp.int32, (block, keys), 0) + start
        allowed = (key_pos <= query_pos) & (key_pos < length_ref[0])
        outs = []
        for head in range(LANES // HEAD):
            own = (lane // HEAD) == head
            queries = query_ref[start : start + block, :] * HEAD**-0.5
            queries = jnp.where(own, queries, jnp.zeros_like(queries))
            scores = matmul_right_t(queries, key_ref[:keys, :])
            scores = jnp.where(allowed, scores, -1e30)
            weights = jnp.exp(scores - jnp.max(scores, axis=1, keepdims=True))
            total = jnp.sum(weights, axis=1, keepdims=True)
            outs.append(
                matmul_plain(weights.astype(jnp.bfloat16), value_ref[:keys, :]) / total
            )
        mixed_ref[start : start + block, :] = jnp.where(lane < HEAD, outs[0], outs[1]).astype(
            jnp.bfloat16
        )


def attend_rows(joined, seq_length, block):
    rows, width = joined.shape
    third = width // 3
    pairs = third // LANES
    spec = lambda part: pl.BlockSpec((rows, LANES), lambda p, *_: (0, part * pairs + p))
    return pl.pallas_call(
        functools.partial(attend_kernel, block=block),
        grid_spec=pltpu.PrefetchScalarGridSpec(
            num_scalar_prefetch=1,
            grid=(pairs,),
            in_specs=[spec(0), spec(1), spec(2)],
            out_specs=spec(0),
        ),
        out_shape=jax.ShapeDtypeStruct((rows, third), jnp.bfloat16),
        compiler_params=pltpu.CompilerParams(vmem_limit_bytes=VMEM_BYTES),
        name="attend",
    )(seq_length.reshape(1), joined, joined, joined)


def attend_grads_kernel(
    length_ref,
    query_ref,
    key_ref,
    value_ref,
    grad_ref,
    grad_query_ref,
    grad_key_ref,
    grad_value_ref,
    sum_key,
    sum_value,
    *,
    block,
):
    rows = query_ref.shape[0]
    lane = lax.broadcasted_iota(jnp.int32, (1, LANES), 1)
    sum_key[...] = jnp.zeros_like(sum_key)
    sum_value[...] = jnp.zeros_like(sum_value)
    keys_turned = key_ref[...].T
    for start in range(0, rows, block):
        keys = start + block
        key_pos = lax.broadcasted_iota(jnp.int32, (keys, block), 0)
        query_pos = lax.broadcasted_iota(jnp.int32, (keys, block), 1) + start
        allowed = (key_pos <= query_pos) & (key_pos < length_ref[0])
        outs = []
        for head in range(LANES // HEAD):
            own = (lane // HEAD) == head
            queries = query_ref[start : start + block, :] * HEAD**-0.5
            queries = jnp.where(own, queries, jnp.zeros_like(queries))
            grads = grad_ref[start : start + block, :]
            grads = jnp.where(own, grads, jnp.zeros_like(grads))
            scores = matmul_right_t(key_ref[:keys, :], queries)
            scores = jnp.where(allowed, scores, -1e30)
            weights = jnp.exp(scores - jnp.max(scores, axis=0, keepdims=True))
            soft = weights * (1.0 / jnp.sum(weights, axis=0, keepdims=True))
            grad_soft = matmul_right_t(value_ref[:keys, :], grads)
            soft_grad = soft * grad_soft
            delta = jnp.sum(soft_grad, axis=0, keepdims=True)
            grad_scores = (soft_grad - soft * delta).astype(jnp.bfloat16)
            sum_value[:keys, :] += matmul_plain(soft.astype(jnp.bfloat16), grads)
            sum_key[:keys, :] += matmul_plain(grad_scores, queries)
            outs.append(matmul_plain(keys_turned[:, :keys], grad_scores))
        head_row = lax.broadcasted_iota(jnp.int32, (LANES, 1), 0)
        turned = jnp.where(head_row < HEAD, outs[0], outs[1]) * HEAD**-0.5
        grad_query_ref[start : start + block, :] = turned.T.astype(jnp.bfloat16)
    grad_key_ref[...] = sum_key[...].astype(jnp.bfloat16)
    grad_value_ref[...] = sum_value[...].astype(jnp.bfloat16)


def attend_grads(joined, grad_mixed, seq_length, block):
    rows, width = joined.shape
    third = width // 3
    pairs = third // LANES
    spec = lambda part: pl.BlockSpec((rows, LANES), lambda p, *_: (0, part * pairs + p))
    out = jax.ShapeDtypeStruct((rows, third), jnp.bfloat16)
    return pl.pallas_call(
        functools.partial(attend_grads_kernel, block=block),
        grid_spec=pltpu.PrefetchScalarGridSpec(
            num_scalar_prefetch=1,
            grid=(pairs,),
            in_specs=[spec(0), spec(1), spec(2), spec(0)],
            out_specs=[spec(0)] * 3,
            scratch_shapes=[pltpu.VMEM((rows, LANES), jnp.float32)] * 2,
        ),
        out_shape=[out] * 3,
        compiler_params=pltpu.CompilerParams(vmem_limit_bytes=VMEM_BYTES),
        name="attend_grads",
    )(seq_length.reshape(1), joined, joined, joined, grad_mixed)


def place_kernel(own_ref, *refs, count, cuts):
    for index in range(count):
        target = own_ref[0] ^ index
        for (first_row, rows, first_lane, lanes), out in zip(cuts, refs[count:]):
            out[pl.ds(pl.multiple_of(target * rows, 16), rows), :] = refs[index][
                first_row : first_row + rows, first_lane : first_lane + lanes
            ]


def place_blocks(blocks, own, cuts):
    count = len(blocks)
    return pl.pallas_call(
        functools.partial(place_kernel, count=count, cuts=cuts),
        in_specs=[pl.BlockSpec(memory_space=pltpu.SMEM)]
        + [pl.BlockSpec(memory_space=pltpu.VMEM)] * count,
        out_specs=[pl.BlockSpec(memory_space=pltpu.VMEM)] * len(cuts),
        out_shape=[
            jax.ShapeDtypeStruct((count * rows, lanes), jnp.bfloat16)
            for _, rows, _, lanes in cuts
        ],
        compiler_params=pltpu.CompilerParams(vmem_limit_bytes=VMEM_BYTES),
        name="place_blocks",
    )(own.reshape(1), *blocks)


def swap(rows, axis, distance):
    count = lax.axis_size(axis)
    return lax.ppermute(rows, axis, [(index, index ^ distance) for index in range(count)])


def in_pair(second, mine, other, axis=0):
    return jnp.where(
        second,
        jnp.concatenate([other, mine], axis=axis),
        jnp.concatenate([mine, other], axis=axis),
    )


def in_order(index, parts):
    low = (index & 1) == 1
    high = (index & 2) == 2
    pairs = [
        [jnp.where(low, parts[k + 1], parts[k]), jnp.where(low, parts[k], parts[k + 1])]
        for k in (0, 2)
    ]
    return [
        jnp.where(high, pairs[1][0], pairs[0][0]),
        jnp.where(high, pairs[1][1], pairs[0][1]),
        jnp.where(high, pairs[0][0], pairs[1][0]),
        jnp.where(high, pairs[0][1], pairs[1][1]),
    ]


def norm_back(inputs, gain_row, grad):
    centred = inputs - jnp.mean(inputs, axis=-1, keepdims=True)
    inverse = lax.rsqrt(jnp.mean(centred * centred, axis=-1, keepdims=True) + 1e-05)
    normal = centred * inverse
    scaled = grad * gain_row
    along = jnp.mean(scaled * normal, axis=-1, keepdims=True)
    result = inverse * (scaled - jnp.mean(scaled, axis=-1, keepdims=True) - normal * along)
    return result, jnp.sum(grad * normal, axis=0), jnp.sum(grad, axis=0)


def gelu_slope(inputs):
    root = math.sqrt(2.0 / math.pi)
    square = inputs * inputs
    bent = jnp.tanh(root * inputs * (1.0 + 0.044715 * square))
    return 0.5 * (1.0 + bent) + 0.5 * inputs * (1.0 - bent * bent) * root * (
        1.0 + 3 * 0.044715 * square
    )


def rows_of(array_in, start, count):
    return lax.dynamic_slice_in_dim(array_in, start, count, 0)


def columns_of(array_in, start, count):
    return lax.dynamic_slice_in_dim(array_in, start, count, 1)


def pack_weights(params, half, seq_length):
    attend, output, expand, reduce = params[2], params[4], params[8], params[10]
    width = output.shape[1]
    part = width // 2
    wide = expand.shape[1] // 2
    begin = half * part
    front = jnp.concatenate(
        [attend[:, k * width + begin : k * width + begin + part] for k in range(3)], axis=1
    )
    length_parts = jnp.stack([seq_length // 32, seq_length % 32]).astype(jnp.bfloat16)
    lines = [params[k] for k in (0, 1, 5, 6, 7, 11, 3, 9)]
    lines[0] = jnp.concatenate(
        [lines[0], jnp.zeros((LANES - lines[0].shape[0],), jnp.bfloat16), length_parts]
    )
    lines = [jnp.pad(line[None], ((0, 0), (0, 3 * part - line.shape[0]))) for line in lines]
    return (
        jnp.concatenate([front] + lines, axis=0),
        jnp.concatenate(
            [expand[:, half * wide : (half + 1) * wide], output[:, begin : begin + part]], axis=1
        ),
        reduce[:, begin : begin + part],
    )


def exchange_models(slabs):
    index = lax.axis_index(VOCAB)
    stacked = jnp.stack(slabs)
    parts = [lax.dynamic_index_in_dim(stacked, index, 0, keepdims=False)]
    for distance in (1, 2, 3):
        parts.append(
            swap(
                lax.dynamic_index_in_dim(stacked, index ^ distance, 0, keepdims=False),
                VOCAB,
                distance,
            )
        )
    return in_order(index, parts)


def after(value, *others):
    return lax.optimization_barrier((value, others))[0]


def along_blk(block):
    return [block] + [swap(block, BLK, dz) for dz in range(1, lax.axis_size(BLK))]


def along_batch(blocks):
    result = []
    for block in blocks:
        result.append(block)
        result += [swap(block, BATCH, dy) for dy in range(1, lax.axis_size(BATCH))]
    return result


def sum_batch(block_of):
    blk, batch = lax.axis_index(BLK), lax.axis_index(BATCH)
    sums = []
    for dz in list(range(1, lax.axis_size(BLK))) + [0]:
        total = block_of(blk ^ dz, batch).astype(jnp.float32)
        for dy in range(1, lax.axis_size(BATCH)):
            total += swap(block_of(blk ^ dz, batch ^ dy), BATCH, dy).astype(jnp.float32)
        sums.append(total.astype(jnp.bfloat16) if dz else total)
    return sums


def sum_blk(sums):
    total = sums[-1]
    for dz in range(1, lax.axis_size(BLK)):
        total += swap(sums[dz - 1], BLK, dz).astype(jnp.float32)
    return total


def shards_by_model(hidden, lengths, *rest):
    embedding = rest[26]
    gain_final = rest[24].astype(jnp.float32)
    shift_final = rest[25].astype(jnp.float32)
    params = (rest[:12], rest[12:24])
    blk, batch, member = (lax.axis_index(name) for name in EVERY)
    size_blk, size_batch, size_vocab = (lax.axis_size(name) for name in EVERY)
    plane = blk * size_batch + batch
    model, half = member // 2, member % 2
    is_teacher, is_second = model == 1, half == 1
    rows_local, width = hidden.shape[1:]
    rows = rows_local * size_vocab
    own_rows = rows // 2
    part = width // 2
    ff_part = rest[8].shape[1] // 2
    shard_rows = rest[2].shape[0]
    plane_rows = shard_rows * size_vocab
    crossing = (BLK, VOCAB)

    front_slabs, middle_slabs, back_slabs = zip(
        *[pack_weights(params[m], h, lengths[0]) for m in (0, 1) for h in (0, 1)]
    )
    front = exchange_models(front_slabs)
    length_parts = sum(
        jnp.where(blk == source, front[source][shard_rows, LANES : LANES + 2], 0)
        for source in range(size_vocab)
    ).astype(jnp.int32)
    seq_length = 32 * length_parts[0] + length_parts[1]
    front_block = jnp.concatenate(
        [source[:shard_rows] for source in front] + [source[shard_rows:] for source in front],
        axis=0,
    )
    vector_lines = front_block.shape[0] - plane_rows
    front_along = along_blk(front_block)
    middle_block = jnp.concatenate(exchange_models(middle_slabs), axis=0)
    reduce_block = jnp.concatenate(exchange_models(back_slabs), axis=0)
    middle_along = along_blk(middle_block)
    reduce_along = along_blk(reduce_block)

    turn = [
        (a * size_vocab + b, b * size_vocab + a) for a in range(size_blk) for b in range(size_vocab)
    ]
    quarter = lax.ppermute(hidden[0], crossing, turn)
    quarter_far = swap(quarter, VOCAB, 2)
    quarters = in_order(
        member, [quarter, swap(quarter, VOCAB, 1), quarter_far, swap(quarter_far, VOCAB, 1)]
    )
    attend_weight, vectors = place_blocks(
        along_batch(front_along),
        plane,
        ((0, plane_rows, 0, 3 * part), (plane_rows, vector_lines, 0, LANES)),
    )
    middle_blocks = along_batch(middle_along)
    reduce_blocks = along_batch(reduce_along)

    shards_all = size_blk * size_batch * size_vocab
    vectors = vectors.reshape(shards_all, vector_lines // size_vocab, LANES).astype(jnp.float32)
    first_gain, first_shift, output_bias, second_gain, second_shift, reduce_bias = [
        vectors[:, k, :shard_rows].reshape(width) for k in range(6)
    ]
    attend_bias = vectors[:, 6, : 2 * shard_rows].reshape(2 * width)
    expand_bias = vectors[:, 7, : 4 * shard_rows].reshape(2 * ff_part)
    query_bias = rows_of(attend_bias, half * part, part)
    value_bias = rows_of(attend_bias, width + half * part, part)
    joined_bias = jnp.concatenate([query_bias, jnp.zeros((part,), jnp.float32), value_bias])
    expand_bias = rows_of(expand_bias, half * ff_part, ff_part)

    inputs_low = jnp.concatenate(quarters, axis=0)
    inputs = inputs_low.astype(jnp.float32)
    inputs_own = rows_of(inputs_low, half * own_rows, own_rows).astype(jnp.float32)
    normed_one = layer_norm(inputs, first_gain, first_shift).astype(jnp.bfloat16)
    normed_one = after(normed_one, middle_along, reduce_along)
    joined = (matmul_plain(normed_one, attend_weight) + joined_bias).astype(jnp.bfloat16)
    joined = after(joined, middle_blocks[:4])
    block = math.gcd(rows, 256)
    mixed_rows = attend_rows(joined, seq_length, block)
    mixed_rows = after(mixed_rows, middle_blocks)
    expand_weight, output_columns = place_blocks(
        middle_blocks, plane, ((0, plane_rows, 0, ff_part), (0, plane_rows, ff_part, part))
    )
    output_weight = in_pair(
        is_second,
        rows_of(output_columns, half * part, part),
        swap(rows_of(output_columns, (1 - half) * part, part), VOCAB, 1),
        axis=1,
    )
    attended = matmul_plain(mixed_rows, output_weight)
    middle = (
        inputs_own
        + rows_of(attended, half * own_rows, own_rows)
        + swap(rows_of(attended, (1 - half) * own_rows, own_rows), VOCAB, 1)
        + output_bias
    )
    normed_own = layer_norm(middle, second_gain, second_shift).astype(jnp.bfloat16)
    normed_two = jnp.concatenate([normed_own, swap(normed_own, VOCAB, 1)], axis=0)
    inner_rows = matmul_plain(normed_two, expand_weight) + expand_bias
    active = gelu_tanh(inner_rows).astype(jnp.bfloat16)
    active, slope = lax.optimization_barrier((active, gelu_slope(inner_rows)))
    reduce_rows = reduce_block.shape[0]
    (reduce_columns,) = place_blocks(reduce_blocks, plane, ((0, reduce_rows, 0, part),))
    reduce_weight = in_pair(
        is_second,
        rows_of(reduce_columns, half * ff_part, ff_part),
        swap(rows_of(reduce_columns, (1 - half) * ff_part, ff_part), VOCAB, 1),
        axis=1,
    )
    reduced = matmul_plain(active, reduce_weight)
    block_out = middle + reduced[:own_rows] + swap(reduced[own_rows:], VOCAB, 1) + reduce_bias
    final_rows = (0.5 * layer_norm(block_out, gain_final, shift_final)).astype(jnp.bfloat16)

    final_far = swap(final_rows, VOCAB, 2)
    final_parts = jnp.stack(
        [final_rows, swap(final_rows, VOCAB, 1), final_far, swap(final_far, VOCAB, 1)]
    )
    vocab_local = embedding.shape[0]
    valid_columns = jnp.clip(VOCAB_REAL - member * vocab_local, 0, vocab_local)
    logit_student, logit_teacher, stats = vocab_stats(
        final_parts, is_teacher, embedding, valid_columns
    )
    stat_parts = [stats] + [swap(stats, VOCAB, distance) for distance in (1, 2, 3)]
    own_sums, core_sums, divergence_rows = vocab_grads(
        logit_student, logit_teacher, embedding, stat_parts
    )
    positions = jnp.arange(rows, dtype=jnp.int32)
    kl_rows = in_pair(is_second, divergence_rows[0, :own_rows], divergence_rows[0, own_rows:])
    kl_rows = 4.0 * kl_rows * (positions < seq_length).astype(jnp.float32)
    kl_out = lax.ppermute(rows_of(kl_rows, member * rows_local, rows_local), crossing, turn)

    both = own_sums + swap(core_sums, VOCAB, 1).astype(jnp.float32)
    grad_final = jnp.where(is_teacher, both[1], both[0]) + swap(
        jnp.where(is_teacher, both[0], both[1]).astype(jnp.bfloat16), VOCAB, 2
    ).astype(jnp.float32)
    own_valid = (half * own_rows + positions[:own_rows] < seq_length).astype(jnp.float32)
    grad_final = grad_final * (2.0 * own_valid)[:, None]

    grad_out, _, _ = norm_back(block_out, gain_final, grad_final)
    branch_own = grad_out.astype(jnp.bfloat16)
    branch_low = jnp.concatenate([branch_own, swap(branch_own, VOCAB, 1)], axis=0)
    grad_reduce = matmul_left_t(active, branch_low).astype(jnp.bfloat16)
    grad_reduce = in_pair(
        is_second,
        columns_of(grad_reduce, half * part, part),
        swap(columns_of(grad_reduce, (1 - half) * part, part), VOCAB, 1),
    )
    reduce_pairs = sum_batch(
        lambda z, y: rows_of(grad_reduce, (z * size_batch + y) * reduce_rows, reduce_rows)
    )
    grad_active = matmul_right_t(branch_low, reduce_weight)
    inner_grad = (grad_active * slope).astype(jnp.bfloat16)
    grad_normed = matmul_right_t(inner_grad, expand_weight)
    grad_normed_own = grad_normed[:own_rows] + swap(grad_normed[own_rows:], VOCAB, 1)
    middle_part, grad_second_gain, grad_second_shift = norm_back(
        middle, second_gain, grad_normed_own
    )
    grad_middle = grad_out + middle_part
    attn_own = grad_middle.astype(jnp.bfloat16)
    attn_low = in_pair(is_second, attn_own, swap(attn_own, VOCAB, 1))
    grad_mixed = matmul_right_t(attn_low, output_weight).astype(jnp.bfloat16)
    grad_expand = matmul_left_t(normed_two, inner_grad).astype(jnp.bfloat16)
    grad_output = matmul_left_t(mixed_rows, attn_low).astype(jnp.bfloat16)
    grad_output = in_pair(
        is_second,
        columns_of(grad_output, half * part, part),
        swap(columns_of(grad_output, (1 - half) * part, part), VOCAB, 1),
    )
    grad_output = jnp.concatenate([grad_expand, grad_output], axis=1)
    middle_pairs = sum_batch(
        lambda z, y: rows_of(grad_output, (z * size_batch + y) * plane_rows, plane_rows)
    )
    grad_mixed = after(grad_mixed, reduce_pairs[:-1], grad_output)
    joined_grad = jnp.concatenate(attend_grads(joined, grad_mixed, seq_length, block), axis=1)
    reduce_sum = sum_blk(reduce_pairs)
    joined_grad = after(joined_grad, middle_pairs[:-1], reduce_sum)
    middle_sum = sum_blk(middle_pairs)
    grad_normed = matmul_right_t(joined_grad, attend_weight)
    grad_attend = matmul_left_t(normed_one, joined_grad).astype(jnp.bfloat16)
    grad_normed_own = rows_of(grad_normed, half * own_rows, own_rows) + swap(
        rows_of(grad_normed, (1 - half) * own_rows, own_rows), VOCAB, 1
    )
    input_part, grad_first_gain, grad_first_shift = norm_back(
        inputs_own, first_gain, grad_normed_own
    )
    grad_inputs = (grad_middle + input_part).reshape(2, rows_local, width)
    input_sum = jnp.where(is_teacher, grad_inputs[1], grad_inputs[0]) + swap(
        jnp.where(is_teacher, grad_inputs[0], grad_inputs[1]).astype(jnp.bfloat16), VOCAB, 2
    ).astype(jnp.float32)
    home = [
        (a * size_vocab + 2 * m + h, (2 * h + m) * size_vocab + a)
        for a in range(size_blk)
        for m in (0, 1)
        for h in (0, 1)
    ]
    input_grad = lax.ppermute(input_sum.astype(jnp.bfloat16), crossing, home).astype(jnp.float32)

    bias_sums = column_sums(joined_grad)

    def spread_half(values, count):
        return jnp.where(
            jnp.arange(2)[:, None] == half, values.reshape(1, count), 0.0
        ).reshape(2 * count)

    vector_parts = [
        grad_first_gain,
        grad_first_shift,
        column_sums(attn_own),
        grad_second_gain,
        grad_second_shift,
        column_sums(branch_own),
        jnp.concatenate(
            [spread_half(bias_sums[:part], part), spread_half(bias_sums[2 * part :], part)]
        ),
        spread_half(column_sums(inner_grad), ff_part),
    ]
    vector_grads = jnp.concatenate([v.reshape(shards_all, -1) for v in vector_parts], axis=1)
    vector_grads = jnp.pad(
        vector_grads.reshape(size_blk * size_batch, size_vocab, -1),
        ((0, 0), (0, 4), (0, 3 * part - vector_grads.shape[1])),
    ).astype(jnp.bfloat16)
    grad_front = jnp.concatenate(
        [grad_attend.reshape(size_blk * size_batch, plane_rows, 3 * part), vector_grads], axis=1
    )
    front_sum = sum_blk(
        sum_batch(
            lambda z, y: lax.dynamic_index_in_dim(grad_front, z * size_batch + y, 0, keepdims=False)
        )
    )

    share = reduce_rows // size_vocab
    back = exchange_models(
        [reduce_sum[t * share : (t + 1) * share].astype(jnp.bfloat16) for t in range(size_vocab)]
    )
    middles = exchange_models(
        [
            middle_sum[t * shard_rows : (t + 1) * shard_rows].astype(jnp.bfloat16)
            for t in range(size_vocab)
        ]
    )
    front = exchange_models(
        [
            jnp.concatenate(
                [
                    front_sum[t * shard_rows : (t + 1) * shard_rows],
                    jnp.pad(front_sum[plane_rows + t][None], ((0, 7), (0, 0))),
                ],
                axis=0,
            ).astype(jnp.bfloat16)
            for t in range(size_vocab)
        ]
    )
    results = []
    for m in (0, 1):
        sides = front[2 * m : 2 * m + 2]
        vector = sum(side[shard_rows].astype(jnp.float32) for side in sides)
        pieces = [vector[k * shard_rows : (k + 1) * shard_rows] for k in range(6)]
        attend = jnp.concatenate(
            [side[:shard_rows, k * part : (k + 1) * part] for k in range(3) for side in sides],
            axis=1,
        ).astype(jnp.float32)
        sides = middles[2 * m : 2 * m + 2]
        output = jnp.concatenate([side[:, ff_part:] for side in sides], axis=1)
        output = output.astype(jnp.float32)
        expand = jnp.concatenate([side[:, :ff_part] for side in sides], axis=1)
        expand = expand.astype(jnp.float32)
        reduce = jnp.concatenate(back[2 * m : 2 * m + 2], axis=1).astype(jnp.float32)
        results += [
            pieces[0],
            pieces[1],
            attend,
            vector[6 * shard_rows : 8 * shard_rows],
            output,
            pieces[2],
            pieces[3],
            pieces[4],
            expand,
            vector[8 * shard_rows : 12 * shard_rows],
            reduce,
            pieces[5],
        ]
    return tuple(results) + (input_grad[None], kl_out[None])


def solution(mesh):
    by_model = mesh.shape[VOCAB] == 4 and mesh.shape[BLK] == 4 and mesh.shape[BATCH] == 2
    return jax.shard_map(
        shards_by_model if by_model else shards,
        mesh=mesh,
        in_specs=(
            P((BATCH, VOCAB), BLK, None),
            P((BATCH, VOCAB)),
            P(EVERY),
            P(EVERY),
            P(EVERY, None),
            P(EVERY),
            P(EVERY, None),
            P(EVERY),
            P(EVERY),
            P(EVERY),
            P(EVERY, None),
            P(EVERY),
            P(EVERY, None),
            P(EVERY),
            P(EVERY),
            P(EVERY),
            P(EVERY, None),
            P(EVERY),
            P(EVERY, None),
            P(EVERY),
            P(EVERY),
            P(EVERY),
            P(EVERY, None),
            P(EVERY),
            P(EVERY, None),
            P(EVERY),
            P(),
            P(),
            P(VOCAB, None),
        ),
        out_specs=(
            P(EVERY),
            P(EVERY),
            P(EVERY, None),
            P(EVERY),
            P(EVERY, None),
            P(EVERY),
            P(EVERY),
            P(EVERY),
            P(EVERY, None),
            P(EVERY),
            P(EVERY, None),
            P(EVERY),
            P(EVERY),
            P(EVERY),
            P(EVERY, None),
            P(EVERY),
            P(EVERY, None),
            P(EVERY),
            P(EVERY),
            P(EVERY),
            P(EVERY, None),
            P(EVERY),
            P(EVERY, None),
            P(EVERY),
            P((BATCH, VOCAB), BLK, None),
            P((BATCH, VOCAB), BLK),
        ),
        check_vma=False,
    )
```

profile of v0, /device:TPU:1, one launch (start us, length us, event | category | flops | bytes accessed | tf_op | source)
XLA Modules:
  0.0 658.0 jit_solution(11335480787232526129)
XLA Ops:
  25.8 35.3 %collective-permute-done.10.refs_4_ = bf16[128,1152]{1,0:T(8,128)(2,1)} collective-permute-done((bf16[128,1152]{1,0:T(8,128)(2,1)S(1)}, bf16[128,1152]{1,0:T(8,128)(2,1)}, u32[]{:S(2)}, u32[]{:S(2)}) %collective-permute-start.10) | collective-permute-done | bytes 294944 | tf_op jit(solution)/shard_map/ppermute | solution.py:1050
  74.6 16.4 %collective-permute-done.18.refs_4_ = bf16[96,1920]{1,0:T(8,128)(2,1)S(1)} collective-permute-done((bf16[96,1920]{1,0:T(8,128)(2,1)S(1)}, bf16[96,1920]{1,0:T(8,128)(2,1)S(1)}, u32[]{:S(2)}, u32[]{:S(2)}) %collective-permute-start.18) | collective-permute-done | bytes 368672 | tf_op jit(solution)/shard_map/ppermute | solution.py:1050
  141.3 11.8 %attend.1 = bf16[1024,384]{1,0:T(8,128)(2,1)} custom-call(s32[1]{0:T(128)} %bitcast.45.length_ref, bf16[1024,1152]{1,0:T(8,128)(2,1)} %add_convert_fusion.query_ref.key_ref.value_ref, bf16[1024,1152]{1,0:T(8,128)(2,1)} %add_convert_fusion.query_ref.key_ref.value_ref, bf16[1024,1152]{1,0:T(8,128)(2,1)} %add_convert_fusion.query_ref.key_ref.value_ref), custom_call_target="tpu_custom_call" | custom-call | tf_op jit(solution)/shard_map/attend/pallas_call | solution.py:939
  178.2 6.3 collective-permute-done.34.refs_3_
  184.5 6.3 collective-permute-done.35.refs_5_
  190.8 6.3 collective-permute-done.36.refs_7_
  206.1 10.9 %fusion.13 = (f32[1024,1536]{1,0:T(8,128)}, bf16[1024,1536]{1,0:T(8,128)(2,1)S(1)}) fusion(f32[1536]{0:T(1024)S(1)} %dynamic_slice.218, bf16[768,1536]{1,0:T(8,128)(2,1)} %get-tuple-element.52, bf16[512,768]{1,0:T(8,128)(2,1)} %collective-permute-done.32, bf16[512,768]{1,0:T(8,128)(2,1)} %add_convert_fusion.1), kind=kOutput, calls=%fused_computation.25 | convolution fusion | flops 2458386432 | bytes 13375488 | tf_op jit(solution)/shard_map/dot_general | solution.py:33
  232.0 18.9 %collective-permute-done.40 = bf16[512,768]{1,0:T(8,128)(2,1)} collective-permute-done((bf16[512,768]{1,0:T(8,128)(2,1)}, bf16[512,768]{1,0:T(8,128)(2,1)}, u32[]{:S(2)}, u32[]{:S(2)}) %collective-permute-start.40) | collective-permute-done | bytes 786464 | tf_op jit(solution)/shard_map/ppermute | solution.py:1050
  257.2 63.5 %vocab_stats.1 = (f32[1024,12800]{1,0:T(8,128)}, f32[1024,12800]{1,0:T(8,128)}, f32[8,1024]{1,0:T(8,128)}) custom-call(s32[2]{0:T(128)} %pad_add_fusion.scalars_ref, bf16[4,512,768]{2,1,0:T(8,128)(2,1)} %pad_maximum_fusion.1.student_low_ref.student_high_ref.teacher_low_ref.teacher_high_ref, ...), custom_call_target="tpu_custom_call" | custom-call | tf_op jit(solution)/shard_map/vocab_stats/pallas_call | solution.py:782
  325.7 53.4 %vocab_grads.1 = (f32[2,512,768]{2,1,0:T(8,128)}, bf16[2,512,768]{2,1,0:T(8,128)(2,1)}, f32[8,1024]{1,0:T(8,128)}) custom-call(f32[1024,12800]{1,0:T(8,128)} %get-tuple-element.54.logit_student_ref, f32[1024,12800]{1,0:T(8,128)} %get-tuple-element.55.logit_teacher_ref, bf16[12576,768]{1,0:T(8,128)(2,1)} %embed_ref.3, f32[8,1024]{1,0:T(8,128)} %get-tuple-element.56.refs_0_, ...), custom_call_target="tpu_custom_call" | custom-call | tf_op jit(solution)/shard_map/vocab_grads/pallas_call | solution.py:878
  388.9 17.9 %collective-permute-done.46 = bf16[512,768]{1,0:T(8,128)(2,1)} collective-permute-done((bf16[512,768]{1,0:T(8,128)(2,1)}, bf16[512,768]{1,0:T(8,128)(2,1)}, u32[]{:S(2)}, u32[]{:S(2)}) %collective-permute-start.46) | collective-permute-done | bytes 786464 | tf_op jit(solution)/shard_map/ppermute | solution.py:1050
  416.5 7.4 %collective-permute-start.85 = (f32[256]{0:T(256)S(1)}, f32[256]{0:T(256)S(1)}, u32[]{:S(2)}, u32[]{:S(2)}) collective-permute-start(f32[256]{0:T(256)S(1)} %dynamic_slice.263), channel_id=1, source_target_pairs={{0,0},{1,8},{2,16},{3,24},{8,1},{9,9},{10,17},{11,25},{16,2},{17,1... | collective-permute-start | bytes 3080 | tf_op jit(solution)/shard_map/ppermute | solution.py:1302
  431.5 6.5 convert_reduce_fusion
  450.9 5.7 convolution_convert_fusion
  456.8 5.7 collective-permute-done.52
  462.5 6.3 collective-permute-done.53
  491.8 8.4 %collective-permute-start.80 = (bf16[96,384]{1,0:T(8,128)(2,1)S(1)}, bf16[96,384]{1,0:T(8,128)(2,1)S(1)}, u32[]{:S(2)}, u32[]{:S(2)}) collective-permute-start(bf16[96,384]{1,0:T(8,128)(2,1)S(1)} %get-tuple-element.163), channel_id=1, source_target_pairs={{0,3},{1,2},{2,1},{3,0},{4,7},{5,6},{6,5},{7,4},{8,11},{9,10},{10,... | collective-permute-start | bytes 221192 | tf_op jit(solution)/shard_map/ppermute | solution.py:1050
  512.9 21.0 %attend_grads.1 = (bf16[1024,384]{1,0:T(8,128)(2,1)}, bf16[1024,384]{1,0:T(8,128)(2,1)}, bf16[1024,384]{1,0:T(8,128)(2,1)}) custom-call(s32[1]{0:T(128)} %bitcast.45.length_ref, bf16[1024,1152]{1,0:T(8,128)(2,1)} %add_convert_fusion.query_ref.key_ref.value_ref, bf16[1024,1152]{1,0:T(8,128)(2,1)} %add_convert_fusion.query_ref.key_ref.value_ref, ...), custom_call_target="tpu_custom_call" | custom-call | tf_op jit(solution)/shard_map/attend_grads/pallas_call | solution.py:1008
  559.0 9.6 %collective-permute-done.76 = bf16[96,1920]{1,0:T(8,128)(2,1)} collective-permute-done((bf16[96,1920]{1,0:T(8,128)(2,1)}, bf16[96,1920]{1,0:T(8,128)(2,1)}, u32[]{:S(2)}, u32[]{:S(2)}) %collective-permute-start.76) | collective-permute-done | bytes 368672 | tf_op jit(solution)/shard_map/ppermute | solution.py:1050
  570.4 6.7 %collective-permute-start.77 = (bf16[24,1920]{1,0:T(8,128)(2,1)S(1)}, bf16[24,1920]{1,0:T(8,128)(2,1)S(1)}, u32[]{:S(2)}, u32[]{:S(2)}) collective-permute-start(bf16[24,1920]{1,0:T(8,128)(2,1)S(1)} %get-tuple-element.153), channel_id=1, source_target_pairs={{0,3},{1,2},{2,1},{3,0},{4,7},{5,6},{6,5},{7,4},{8,11},{9,10},{10,... | collective-permute-start | bytes 276488 | tf_op jit(solution)/shard_map/ppermute | solution.py:1050
  606.9 6.6 collective-permute-start.65
  621.9 6.2 collective-permute-done.69
  628.5 7.5 %collective-permute-start.70 = (bf16[32,1152]{1,0:T(8,128)(2,1)S(1)}, bf16[32,1152]{1,0:T(8,128)(2,1)S(1)}, u32[]{:S(2)}, u32[]{:S(2)}) collective-permute-start(bf16[32,1152]{1,0:T(8,128)(2,1)S(1)} %get-tuple-element.170), channel_id=1, source_target_pairs={{0,3},{1,2},{2,1},{3,0},{4,7},{5,6},{6,5},{7,4},{8,11},{9,10},{10,... | collective-permute-start | bytes 221192 | tf_op jit(solution)/shard_map/ppermute | solution.py:1050
  647.6 8.7 %collective-permute-done.84 = bf16[256,768]{1,0:T(8,128)(2,1)S(1)} collective-permute-done((bf16[256,768]{1,0:T(8,128)(2,1)S(1)}, bf16[256,768]{1,0:T(8,128)(2,1)S(1)}, u32[]{:S(2)}, u32[]{:S(2)}) %collective-permute-start.84) | collective-permute-done | bytes 393248 | tf_op jit(solution)/shard_map/ppermute | solution.py:1368
  (553 shorter events, 299.9 us)
Async XLA Ops:
  18.2 54.8 %collective-permute-start = (bf16[256,768]{1,0:T(8,128)(2,1)}, bf16[256,768]{1,0:T(8,128)(2,1)S(1)}, u32[]{:S(2)}, u32[]{:S(2)}) collective-permute-start(bf16[256,768]{1,0:T(8,128)(2,1)} %bitcast), channel_id=1, source_target_pairs={{0,0},{1,8},{2,16},{3,24},{8,1},{9,9},{10,17},{11,25},{16,2},{17,1... | collective-permute-start | bytes 1179656 | tf_op jit(solution)/shard_map/ppermute | solution.py:1218
  22.0 39.1 %collective-permute-start.10 = (bf16[128,1152]{1,0:T(8,128)(2,1)S(1)}, bf16[128,1152]{1,0:T(8,128)(2,1)}, u32[]{:S(2)}, u32[]{:S(2)}) collective-permute-start(bf16[128,1152]{1,0:T(8,128)(2,1)S(1)} %constant_dynamic-update-slice_fusion.refs_0_), channel_id=1, source_target_pairs={{0,16},{8,24},{16,0},{24,8},{1,17},{9,25},{17,1},{25,9},{2,18},{10... | collective-permute-start | bytes 884744 | tf_op jit(solution)/shard_map/ppermute | solution.py:1050
  24.0 38.3 %collective-permute-start.12 = (bf16[128,1152]{1,0:T(8,128)(2,1)S(1)}, bf16[128,1152]{1,0:T(8,128)(2,1)}, u32[]{:S(2)}, u32[]{:S(2)}) collective-permute-start(bf16[128,1152]{1,0:T(8,128)(2,1)S(1)} %constant_dynamic-update-slice_fusion.refs_0_), channel_id=1, source_target_pairs={{0,24},{8,16},{16,8},{24,0},{1,25},{9,17},{17,9},{25,1},{2,26},{10... | collective-permute-start | bytes 884744 | tf_op jit(solution)/shard_map/ppermute | solution.py:1050
  24.1 42.4 %collective-permute-start.8 = (bf16[128,1152]{1,0:T(8,128)(2,1)S(1)}, bf16[128,1152]{1,0:T(8,128)(2,1)}, u32[]{:S(2)}, u32[]{:S(2)}) collective-permute-start(bf16[128,1152]{1,0:T(8,128)(2,1)S(1)} %constant_dynamic-update-slice_fusion.refs_0_), channel_id=1, source_target_pairs={{0,8},{8,0},{16,24},{24,16},{1,9},{9,1},{17,25},{25,17},{2,10},{10... | collective-permute-start | bytes 884744 | tf_op jit(solution)/shard_map/ppermute | solution.py:1050
  24.9 48.3 %collective-permute-start.17 = (bf16[96,1920]{1,0:T(8,128)(2,1)S(1)}, bf16[96,1920]{1,0:T(8,128)(2,1)S(1)}, u32[]{:S(2)}, u32[]{:S(2)}) collective-permute-start(bf16[96,1920]{1,0:T(8,128)(2,1)S(1)} %pad_maximum_fusion.11.refs_0_), channel_id=1, source_target_pairs={{0,8},{8,0},{16,24},{24,16},{1,9},{9,1},{17,25},{25,17},{2,10},{10... | collective-permute-start | bytes 1105928 | tf_op jit(solution)/shard_map/ppermute | solution.py:1050
  62.3 28.6 %collective-permute-start.18 = (bf16[96,1920]{1,0:T(8,128)(2,1)S(1)}, bf16[96,1920]{1,0:T(8,128)(2,1)S(1)}, u32[]{:S(2)}, u32[]{:S(2)}) collective-permute-start(bf16[96,1920]{1,0:T(8,128)(2,1)S(1)} %pad_maximum_fusion.11.refs_0_), channel_id=1, source_target_pairs={{0,16},{8,24},{16,0},{24,8},{1,17},{9,25},{17,1},{25,9},{2,18},{10... | collective-permute-start | bytes 1105928 | tf_op jit(solution)/shard_map/ppermute | solution.py:1050
  66.6 25.6 %collective-permute-start.19 = (bf16[96,1920]{1,0:T(8,128)(2,1)S(1)}, bf16[96,1920]{1,0:T(8,128)(2,1)}, u32[]{:S(2)}, u32[]{:S(2)}) collective-permute-start(bf16[96,1920]{1,0:T(8,128)(2,1)S(1)} %pad_maximum_fusion.11.refs_0_), channel_id=1, source_target_pairs={{0,24},{8,16},{16,8},{24,0},{1,25},{9,17},{17,9},{25,1},{2,26},{10... | collective-permute-start | bytes 1105928 | tf_op jit(solution)/shard_map/ppermute | solution.py:1050
  71.7 22.7 %collective-permute-start.11 = (bf16[128,1152]{1,0:T(8,128)(2,1)}, bf16[128,1152]{1,0:T(8,128)(2,1)S(1)}, u32[]{:S(2)}, u32[]{:S(2)}) collective-permute-start(bf16[128,1152]{1,0:T(8,128)(2,1)} %collective-permute-done.10.refs_4_), channel_id=1, source_target_pairs={{0,4},{4,0},{1,5},{5,1},{2,6},{6,2},{3,7},{7,3},{8,12},{12,8},{9,1... | collective-permute-start | bytes 884744 | tf_op jit(solution)/shard_map/ppermute | solution.py:1050
  73.2 23.4 %collective-permute-start.9 = (bf16[128,1152]{1,0:T(8,128)(2,1)}, bf16[128,1152]{1,0:T(8,128)(2,1)}, u32[]{:S(2)}, u32[]{:S(2)}) collective-permute-start(bf16[128,1152]{1,0:T(8,128)(2,1)} %collective-permute-done.8.refs_2_), channel_id=1, source_target_pairs={{0,4},{4,0},{1,5},{5,1},{2,6},{6,2},{3,7},{7,3},{8,12},{12,8},{9,1... | collective-permute-start | bytes 884744 | tf_op jit(solution)/shard_map/ppermute | solution.py:1050
  96.6 26.6 %collective-permute-start.29 = (bf16[96,1920]{1,0:T(8,128)(2,1)}, bf16[96,1920]{1,0:T(8,128)(2,1)}, u32[]{:S(2)}, u32[]{:S(2)}) collective-permute-start(bf16[96,1920]{1,0:T(8,128)(2,1)} %collective-permute-done.19.refs_6_), channel_id=1, source_target_pairs={{0,4},{4,0},{1,5},{5,1},{2,6},{6,2},{3,7},{7,3},{8,12},{12,8},{9,1... | collective-permute-start | bytes 1105928 | tf_op jit(solution)/shard_map/ppermute | solution.py:1050
  101.2 31.9 %collective-permute-start.3 = (bf16[256,768]{1,0:T(8,128)(2,1)S(1)}, bf16[256,768]{1,0:T(8,128)(2,1)S(1)}, u32[]{:S(2)}, u32[]{:S(2)}) collective-permute-start(bf16[256,768]{1,0:T(8,128)(2,1)S(1)} %collective-permute-done), channel_id=1, source_target_pairs={{0,1},{1,0},{2,3},{3,2},{4,5},{5,4},{6,7},{7,6},{8,9},{9,8},{10,11... | collective-permute-start | bytes 1179656 | tf_op jit(solution)/shard_map/ppermute | solution.py:1050
  104.0 31.1 %collective-permute-start.2 = (bf16[256,768]{1,0:T(8,128)(2,1)S(1)}, bf16[256,768]{1,0:T(8,128)(2,1)S(1)}, u32[]{:S(2)}, u32[]{:S(2)}) collective-permute-start(bf16[256,768]{1,0:T(8,128)(2,1)S(1)} %collective-permute-done.1), channel_id=1, source_target_pairs={{0,1},{1,0},{2,3},{3,2},{4,5},{5,4},{6,7},{7,6},{8,9},{9,8},{10,11... | collective-permute-start | bytes 1179656 | tf_op jit(solution)/shard_map/ppermute | solution.py:1050
  107.4 29.4 %collective-permute-start.23 = (bf16[384,384]{1,0:T(8,128)(2,1)S(1)}, bf16[384,384]{1,0:T(8,128)(2,1)S(1)}, u32[]{:S(2)}, u32[]{:S(2)}) collective-permute-start(bf16[384,384]{1,0:T(8,128)(2,1)S(1)} %pad_maximum_fusion.15.refs_0_), channel_id=1, source_target_pairs={{0,8},{8,0},{16,24},{24,16},{1,9},{9,1},{17,25},{25,17},{2,10},{10... | collective-permute-start | bytes 884744 | tf_op jit(solution)/shard_map/ppermute | solution.py:1050
  169.4 36.7 %collective-permute-start.32 = (bf16[512,768]{1,0:T(8,128)(2,1)}, bf16[512,768]{1,0:T(8,128)(2,1)}, u32[]{:S(2)}, u32[]{:S(2)}) collective-permute-start(bf16[512,768]{1,0:T(8,128)(2,1)} %add_convert_fusion.1), channel_id=1, source_target_pairs={{0,1},{1,0},{2,3},{3,2},{4,5},{5,4},{6,7},{7,6},{8,9},{9,8},{10,11... | collective-permute-start | bytes 2359304 | tf_op jit(solution)/shard_map/ppermute | solution.py:1050
  172.4 24.7 %collective-permute-start.36 = (bf16[384,384]{1,0:T(8,128)(2,1)}, bf16[384,384]{1,0:T(8,128)(2,1)S(1)}, u32[]{:S(2)}, u32[]{:S(2)}) collective-permute-start(bf16[384,384]{1,0:T(8,128)(2,1)} %collective-permute-done.25.refs_6_), channel_id=1, source_target_pairs={{0,4},{4,0},{1,5},{5,1},{2,6},{6,2},{3,7},{7,3},{8,12},{12,8},{9,1... | collective-permute-start | bytes 884744 | tf_op jit(solution)/shard_map/ppermute | solution.py:1050
  416.5 27.7 %collective-permute-start.85 = (f32[256]{0:T(256)S(1)}, f32[256]{0:T(256)S(1)}, u32[]{:S(2)}, u32[]{:S(2)}) collective-permute-start(f32[256]{0:T(256)S(1)} %dynamic_slice.263), channel_id=1, source_target_pairs={{0,0},{1,8},{2,16},{3,24},{8,1},{9,9},{10,17},{11,25},{16,2},{17,1... | collective-permute-start | bytes 3080 | tf_op jit(solution)/shard_map/ppermute | solution.py:1302
  443.6 29.9 %collective-permute-start.48 = (f32[512,768]{1,0:T(8,128)}, f32[512,768]{1,0:T(8,128)}, u32[]{:S(2)}, u32[]{:S(2)}) collective-permute-start(f32[512,768]{1,0:T(8,128)} %slice.585), channel_id=1, source_target_pairs={{0,1},{1,0},{2,3},{3,2},{4,5},{5,4},{6,7},{7,6},{8,9},{9,8},{10,11... | collective-permute-start | bytes 4718600 | tf_op jit(solution)/shard_map/ppermute | solution.py:1050
  456.6 30.1 %collective-permute-start.58 = (bf16[384,384]{1,0:T(8,128)(2,1)S(1)}, bf16[384,384]{1,0:T(8,128)(2,1)S(1)}, u32[]{:S(2)}, u32[]{:S(2)}) collective-permute-start(bf16[384,384]{1,0:T(8,128)(2,1)S(1)} %get-tuple-element.100), channel_id=1, source_target_pairs={{0,4},{4,0},{1,5},{5,1},{2,6},{6,2},{3,7},{7,3},{8,12},{12,8},{9,1... | collective-permute-start | bytes 884744 | tf_op jit(solution)/shard_map/ppermute | solution.py:1050
  506.8 29.3 %collective-permute-start.55 = (bf16[96,1920]{1,0:T(8,128)(2,1)}, bf16[96,1920]{1,0:T(8,128)(2,1)S(1)}, u32[]{:S(2)}, u32[]{:S(2)}) collective-permute-start(bf16[96,1920]{1,0:T(8,128)(2,1)} %get-tuple-element.94), channel_id=1, source_target_pairs={{0,4},{4,0},{1,5},{5,1},{2,6},{6,2},{3,7},{7,3},{8,12},{12,8},{9,1... | collective-permute-start | bytes 1105928 | tf_op jit(solution)/shard_map/ppermute | solution.py:1050
  508.0 28.0 %collective-permute-start.56 = (bf16[96,1920]{1,0:T(8,128)(2,1)}, bf16[96,1920]{1,0:T(8,128)(2,1)}, u32[]{:S(2)}, u32[]{:S(2)}) collective-permute-start(bf16[96,1920]{1,0:T(8,128)(2,1)} %get-tuple-element.95), channel_id=1, source_target_pairs={{0,4},{4,0},{1,5},{5,1},{2,6},{6,2},{3,7},{7,3},{8,12},{12,8},{9,1... | collective-permute-start | bytes 1105928 | tf_op jit(solution)/shard_map/ppermute | solution.py:1050
  508.3 27.8 %collective-permute-start.57 = (bf16[96,1920]{1,0:T(8,128)(2,1)}, bf16[96,1920]{1,0:T(8,128)(2,1)}, u32[]{:S(2)}, u32[]{:S(2)}) collective-permute-start(bf16[96,1920]{1,0:T(8,128)(2,1)} %get-tuple-element.96), channel_id=1, source_target_pairs={{0,4},{4,0},{1,5},{5,1},{2,6},{6,2},{3,7},{7,3},{8,12},{12,8},{9,1... | collective-permute-start | bytes 1105928 | tf_op jit(solution)/shard_map/ppermute | solution.py:1050
  544.0 24.6 %collective-permute-start.76 = (bf16[96,1920]{1,0:T(8,128)(2,1)}, bf16[96,1920]{1,0:T(8,128)(2,1)}, u32[]{:S(2)}, u32[]{:S(2)}) collective-permute-start(bf16[96,1920]{1,0:T(8,128)(2,1)} %get-tuple-element.97), channel_id=1, source_target_pairs={{0,24},{8,16},{16,8},{24,0},{1,25},{9,17},{17,9},{25,1},{2,26},{10... | collective-permute-start | bytes 1105928 | tf_op jit(solution)/shard_map/ppermute | solution.py:1050
  550.6 34.5 %collective-permute-start.62 = (f32[512,768]{1,0:T(8,128)}, f32[512,768]{1,0:T(8,128)}, u32[]{:S(2)}, u32[]{:S(2)}) collective-permute-start(f32[512,768]{1,0:T(8,128)} %constant_dynamic-slice_fusion), channel_id=1, source_target_pairs={{0,1},{1,0},{2,3},{3,2},{4,5},{5,4},{6,7},{7,6},{8,9},{9,8},{10,11... | collective-permute-start | bytes 4718600 | tf_op jit(solution)/shard_map/ppermute | solution.py:1050
  591.6 24.5 %collective-permute-start.63 = (bf16[104,1152]{1,0:T(8,128)(2,1)S(1)}, bf16[104,1152]{1,0:T(8,128)(2,1)S(1)}, u32[]{:S(2)}, u32[]{:S(2)}) collective-permute-start(bf16[104,1152]{1,0:T(8,128)(2,1)S(1)} %get-tuple-element.111), channel_id=1, source_target_pairs={{0,4},{4,0},{1,5},{5,1},{2,6},{6,2},{3,7},{7,3},{8,12},{12,8},{9,1... | collective-permute-start | bytes 718856 | tf_op jit(solution)/shard_map/ppermute | solution.py:1050
  (148 other events, 1675.0 us)
where the time goes:
time: 666 us; the launch traced here: 658 us
  waiting for transfers between devices  207 us (31%)
  Pallas kernels  159 us (24%)
  starting transfers between devices  136 us (20%)
  other arithmetic  56.7 us (9%)
  matrix products  55.3 us (8%)
  local copies, waits for them, and re-layouts  38.9 us (6%)
    ppermute x83, waiting for transfers between devices, swap(): lax.ppermute(rows, axis, [(index, index ^ distance) for index in range(co...  198 us
    ppermute x83, starting transfers between devices, swap(): lax.ppermute(rows, axis, [(index, index ^ distance) for index in range(co...  120 us
    pallas_call x1, Pallas kernels, vocab_stats(): pl.pallas_call(functools.partial(vocab_stats_kernel, tile=tile, rows_bloc...  63.5 us
    pallas_call x1, Pallas kernels, vocab_grads(): pl.pallas_call(functools.partial(vocab_grads_kernel, tile=tile, columns=c...  53.4 us
    dot_general x4, matrix products, matmul_plain(): return jnp.dot(left_side, right_side, preferred_element_type=jnp.float32)  22.1 us
    pallas_call x1, Pallas kernels, attend_grads(): pl.pallas_call(functools.partial(attend_grads_kernel, block=block), grid_...  21 us
    dot_general x4, matrix products, matmul_left_t(): lax.dot_general(left_side, right_side, (((0,), (0,)), ((), ())), preferre...  18.5 us
    dot_general x4, matrix products, matmul_right_t(): lax.dot_general(left_side, right_side, (((1,), (1,)), ((), ())), preferre...  14.7 us
  transfers between devices with their start and end apart: 86, of which 38 were waited for; matrix products, arithmetic and copies ran while one was open for 16% of the time, Pallas kernels for 6%

commit v1 on v0

--- a/solution.py
+++ b/solution.py
@@ -1020,29 +1020,32 @@
     )(seq_length.reshape(1), joined, joined, joined, grad_mixed)
 
 
-def place_kernel(own_ref, *refs, count, cuts):
-    for index in range(count):
-        target = own_ref[0] ^ index
-        for (first_row, rows, first_lane, lanes), out in zip(cuts, refs[count:]):
-            out[pl.ds(pl.multiple_of(target * rows, 16), rows), :] = refs[index][
-                first_row : first_row + rows, first_lane : first_lane + lanes
-            ]
-
-
-def place_blocks(blocks, own, cuts):
-    count = len(blocks)
+def place_kernel(own_ref, *refs, order, cuts):
+    count = len(order)
+    for block_ref, indices in zip(refs, order):
+        height = block_ref.shape[0] // len(indices)
+        for place, index in enumerate(indices):
+            target = own_ref[0] ^ index
+            for (first_row, rows, first_lane, lanes), out in zip(cuts, refs[count:]):
+                first = place * height + first_row
+                out[pl.ds(pl.multiple_of(target * rows, 16), rows), :] = block_ref[
+                    first : first + rows, first_lane : first_lane + lanes
+                ]
+
+
+def place_blocks(gathered, own, cuts):
+    gathered, order = gathered
     return pl.pallas_call(
-        functools.partial(place_kernel, count=count, cuts=cuts),
+        functools.partial(place_kernel, order=order, cuts=cuts),
         in_specs=[pl.BlockSpec(memory_space=pltpu.SMEM)]
-        + [pl.BlockSpec(memory_space=pltpu.VMEM)] * count,
+        + [pl.BlockSpec(memory_space=pltpu.VMEM)] * len(order),
         out_specs=[pl.BlockSpec(memory_space=pltpu.VMEM)] * len(cuts),
         out_shape=[
-            jax.ShapeDtypeStruct((count * rows, lanes), jnp.bfloat16)
-            for _, rows, _, lanes in cuts
+            jax.ShapeDtypeStruct((8 * rows, lanes), jnp.bfloat16) for _, rows, _, lanes in cuts
         ],
         compiler_params=pltpu.CompilerParams(vmem_limit_bytes=VMEM_BYTES),
         name="place_blocks",
-    )(own.reshape(1), *blocks)
+    )(own.reshape(1), *gathered)
 
 
 def swap(rows, axis, distance):
@@ -1100,7 +1103,25 @@
     return lax.dynamic_slice_in_dim(array_in, start, count, 1)
 
 
-def pack_weights(params, half, seq_length):
+def vector_lines_of(params, seq_length, width):
+    short, middle, wide = [
+        jnp.stack([jnp.stack([p[k] for k in numbers]) for p in params])
+        for numbers in ((0, 1, 5, 6, 7, 11), (3,), (9,))
+    ]
+    lines = jnp.concatenate(
+        [
+            jnp.pad(group, ((0, 0), (0, 0), (0, LANES - group.shape[2])))
+            for group in (short, middle, wide)
+        ],
+        axis=1,
+    )
+    length_parts = jnp.stack([seq_length // 32, seq_length % 32]).astype(jnp.bfloat16)
+    length_parts = jnp.broadcast_to(length_parts, lines.shape[:2] + (2,))
+    lines = jnp.concatenate([lines, length_parts], axis=2)
+    return jnp.pad(lines, ((0, 0), (0, 0), (0, width - lines.shape[2])))
+
+
+def pack_weights(params, half, lines):
     attend, output, expand, reduce = params[2], params[4], params[8], params[10]
     width = output.shape[1]
     part = width // 2
@@ -1109,18 +1130,16 @@
     front = jnp.concatenate(
         [attend[:, k * width + begin : k * width + begin + part] for k in range(3)], axis=1
     )
-    length_parts = jnp.stack([seq_length // 32, seq_length % 32]).astype(jnp.bfloat16)
-    lines = [params[k] for k in (0, 1, 5, 6, 7, 11, 3, 9)]
-    lines[0] = jnp.concatenate(
-        [lines[0], jnp.zeros((LANES - lines[0].shape[0],), jnp.bfloat16), length_parts]
-    )
-    lines = [jnp.pad(line[None], ((0, 0), (0, 3 * part - line.shape[0]))) for line in lines]
     return (
-        jnp.concatenate([front] + lines, axis=0),
+        jnp.concatenate([front, lines], axis=0),
         jnp.concatenate(
-            [expand[:, half * wide : (half + 1) * wide], output[:, begin : begin + part]], axis=1
+            [
+                expand[:, start : start + part]
+                for start in range(half * wide, (half + 1) * wide, part)
+            ]
+            + [output[:, begin : begin + part], reduce[:, begin : begin + part]],
+            axis=0,
         ),
-        reduce[:, begin : begin + part],
     )
 
 
@@ -1143,34 +1162,34 @@
     return lax.optimization_barrier((value, others))[0]
 
 
-def along_blk(block):
-    return [block] + [swap(block, BLK, dz) for dz in range(1, lax.axis_size(BLK))]
-
-
-def along_batch(blocks):
-    result = []
-    for block in blocks:
-        result.append(block)
-        result += [swap(block, BATCH, dy) for dy in range(1, lax.axis_size(BATCH))]
-    return result
-
-
-def sum_batch(block_of):
-    blk, batch = lax.axis_index(BLK), lax.axis_index(BATCH)
-    sums = []
-    for dz in list(range(1, lax.axis_size(BLK))) + [0]:
-        total = block_of(blk ^ dz, batch).astype(jnp.float32)
-        for dy in range(1, lax.axis_size(BATCH)):
-            total += swap(block_of(blk ^ dz, batch ^ dy), BATCH, dy).astype(jnp.float32)
-        sums.append(total.astype(jnp.bfloat16) if dz else total)
-    return sums
-
-
-def sum_blk(sums):
-    total = sums[-1]
-    for dz in range(1, lax.axis_size(BLK)):
-        total += swap(sums[dz - 1], BLK, dz).astype(jnp.float32)
-    return total
+def held_after(held, *others):
+    return after(held[0], *others), held[1]
+
+
+def halves_of(axis_name, bit):
+    distance = 1 << bit
+    return distance, distance * (lax.axis_size(BATCH) if axis_name == BLK else 1)
+
+
+def double(held, axis_name, bit):
+    arrays, order = held
+    distance, offset = halves_of(axis_name, bit)
+    sent = jnp.concatenate(arrays, axis=0) if len(arrays) > 1 else arrays[0]
+    sources = sum(order, ())
+    return (
+        arrays + (swap(sent, axis_name, distance),),
+        order + (tuple(source ^ offset for source in sources),),
+    )
+
+
+def halve(addends, axis_name, bit):
+    axis = 2 if axis_name == BATCH else 1 - bit
+    own = (lax.axis_index(axis_name) >> bit) & 1
+    mine = lax.dynamic_slice_in_dim(addends, own, 1, axis)
+    theirs = lax.dynamic_slice_in_dim(addends, 1 - own, 1, axis)
+    return mine.astype(jnp.float32) + swap(
+        theirs.astype(jnp.bfloat16), axis_name, 1 << bit
+    ).astype(jnp.float32)
 
 
 def shards_by_model(hidden, lengths, *rest):
@@ -1192,10 +1211,17 @@
     plane_rows = shard_rows * size_vocab
     crossing = (BLK, VOCAB)
 
-    front_slabs, middle_slabs, back_slabs = zip(
-        *[pack_weights(params[m], h, lengths[0]) for m in (0, 1) for h in (0, 1)]
+    turn = [
+        (a * size_vocab + b, b * size_vocab + a) for a in range(size_blk) for b in range(size_vocab)
+    ]
+    quarter = lax.ppermute(hidden[0], crossing, turn)
+
+    lines = vector_lines_of(params, lengths[0], 3 * part)
+    front_slabs, back_slabs = zip(
+        *[pack_weights(params[m], h, lines[m]) for m in (0, 1) for h in (0, 1)]
     )
     front = exchange_models(front_slabs)
+    back = exchange_models(after(back_slabs, front))
     length_parts = sum(
         jnp.where(blk == source, front[source][shard_rows, LANES : LANES + 2], 0)
         for source in range(size_vocab)
@@ -1205,28 +1231,36 @@
         [source[:shard_rows] for source in front] + [source[shard_rows:] for source in front],
         axis=0,
     )
+    units = (ff_part + part) // part
+    middle_block = jnp.concatenate(
+        [
+            jnp.concatenate(
+                [source[k * shard_rows : (k + 1) * shard_rows] for source in back], axis=0
+            )
+            for k in range(units)
+        ],
+        axis=1,
+    )
+    reduce_block = jnp.concatenate([source[units * shard_rows :] for source in back], axis=0)
     vector_lines = front_block.shape[0] - plane_rows
-    front_along = along_blk(front_block)
-    middle_block = jnp.concatenate(exchange_models(middle_slabs), axis=0)
-    reduce_block = jnp.concatenate(exchange_models(back_slabs), axis=0)
-    middle_along = along_blk(middle_block)
-    reduce_along = along_blk(reduce_block)
-
-    turn = [
-        (a * size_vocab + b, b * size_vocab + a) for a in range(size_blk) for b in range(size_vocab)
-    ]
-    quarter = lax.ppermute(hidden[0], crossing, turn)
-    quarter_far = swap(quarter, VOCAB, 2)
+    reduce_rows = reduce_block.shape[0]
+
+    front_held = double(((after(front_block, quarter),), ((0,),)), BLK, 1)
+    middle_held = double(((after(middle_block, front_held[0]),), ((0,),)), BLK, 1)
+    reduce_held = double(((after(reduce_block, middle_held[0]),), ((0,),)), BLK, 1)
+    quarter_far = swap(after(quarter, front), VOCAB, 2)
     quarters = in_order(
         member, [quarter, swap(quarter, VOCAB, 1), quarter_far, swap(quarter_far, VOCAB, 1)]
     )
+    front_held = double(front_held, BLK, 0)
+    front_held = double(held_after(front_held, middle_held[0]), BATCH, 0)
+    middle_held = double(middle_held, BATCH, 0)
+    reduce_held = double(reduce_held, BLK, 0)
     attend_weight, vectors = place_blocks(
-        along_batch(front_along),
+        front_held,
         plane,
         ((0, plane_rows, 0, 3 * part), (plane_rows, vector_lines, 0, LANES)),
     )
-    middle_blocks = along_batch(middle_along)
-    reduce_blocks = along_batch(reduce_along)
 
     shards_all = size_blk * size_batch * size_vocab
     vectors = vectors.reshape(shards_all, vector_lines // size_vocab, LANES).astype(jnp.float32)
@@ -1244,14 +1278,15 @@
     inputs = inputs_low.astype(jnp.float32)
     inputs_own = rows_of(inputs_low, half * own_rows, own_rows).astype(jnp.float32)
     normed_one = layer_norm(inputs, first_gain, first_shift).astype(jnp.bfloat16)
-    normed_one = after(normed_one, middle_along, reduce_along)
+    normed_one = after(normed_one, middle_held[0], reduce_held[0])
     joined = (matmul_plain(normed_one, attend_weight) + joined_bias).astype(jnp.bfloat16)
-    joined = after(joined, middle_blocks[:4])
     block = math.gcd(rows, 256)
     mixed_rows = attend_rows(joined, seq_length, block)
-    mixed_rows = after(mixed_rows, middle_blocks)
+    middle_held = held_after(double(middle_held, BLK, 0), mixed_rows)
+    reduce_held = double(reduce_held, BATCH, 0)
+    mixed_rows = after(mixed_rows, middle_held[0], reduce_held[0])
     expand_weight, output_columns = place_blocks(
-        middle_blocks, plane, ((0, plane_rows, 0, ff_part), (0, plane_rows, ff_part, part))
+        middle_held, plane, ((0, plane_rows, 0, ff_part), (0, plane_rows, ff_part, part))
     )
     output_weight = in_pair(
         is_second,
@@ -1271,8 +1306,7 @@
     inner_rows = matmul_plain(normed_two, expand_weight) + expand_bias
     active = gelu_tanh(inner_rows).astype(jnp.bfloat16)
     active, slope = lax.optimization_barrier((active, gelu_slope(inner_rows)))
-    reduce_rows = reduce_block.shape[0]
-    (reduce_columns,) = place_blocks(reduce_blocks, plane, ((0, reduce_rows, 0, part),))
+    (reduce_columns,) = place_blocks(reduce_held, plane, ((0, reduce_rows, 0, part),))
     reduce_weight = in_pair(
         is_second,
         rows_of(reduce_columns, half * ff_part, ff_part),
@@ -1299,7 +1333,6 @@
     positions = jnp.arange(rows, dtype=jnp.int32)
     kl_rows = in_pair(is_second, divergence_rows[0, :own_rows], divergence_rows[0, own_rows:])
     kl_rows = 4.0 * kl_rows * (positions < seq_length).astype(jnp.float32)
-    kl_out = lax.ppermute(rows_of(kl_rows, member * rows_local, rows_local), crossing, turn)
 
     both = own_sums + swap(core_sums, VOCAB, 1).astype(jnp.float32)
     grad_final = jnp.where(is_teacher, both[1], both[0]) + swap(
@@ -1317,9 +1350,8 @@
         columns_of(grad_reduce, half * part, part),
         swap(columns_of(grad_reduce, (1 - half) * part, part), VOCAB, 1),
     )
-    reduce_pairs = sum_batch(
-        lambda z, y: rows_of(grad_reduce, (z * size_batch + y) * reduce_rows, reduce_rows)
-    )
+    grid = (2, 2, 2)
+    reduce_sum = halve(grad_reduce.reshape(grid + (reduce_rows, part)), BATCH, 0)
     grad_active = matmul_right_t(branch_low, reduce_weight)
     inner_grad = (grad_active * slope).astype(jnp.bfloat16)
     grad_normed = matmul_right_t(inner_grad, expand_weight)
@@ -1338,15 +1370,12 @@
         columns_of(grad_output, half * part, part),
         swap(columns_of(grad_output, (1 - half) * part, part), VOCAB, 1),
     )
-    grad_output = jnp.concatenate([grad_expand, grad_output], axis=1)
-    middle_pairs = sum_batch(
-        lambda z, y: rows_of(grad_output, (z * size_batch + y) * plane_rows, plane_rows)
-    )
-    grad_mixed = after(grad_mixed, reduce_pairs[:-1], grad_output)
+    grad_middles = jnp.concatenate([grad_expand, grad_output], axis=1)
+    grad_middles = grad_middles.reshape(grid + (plane_rows, ff_part + part))
+    middle_sum = halve(grad_middles, BLK, 0)
     joined_grad = jnp.concatenate(attend_grads(joined, grad_mixed, seq_length, block), axis=1)
-    reduce_sum = sum_blk(reduce_pairs)
-    joined_grad = after(joined_grad, middle_pairs[:-1], reduce_sum)
-    middle_sum = sum_blk(middle_pairs)
+    reduce_sum = halve(after(reduce_sum, joined_grad), BLK, 0)
+    joined_grad = after(joined_grad, middle_sum)
     grad_normed = matmul_right_t(joined_grad, attend_weight)
     grad_attend = matmul_left_t(normed_one, joined_grad).astype(jnp.bfloat16)
     grad_normed_own = rows_of(grad_normed, half * own_rows, own_rows) + swap(
@@ -1366,6 +1395,8 @@
         for h in (0, 1)
     ]
     input_grad = lax.ppermute(input_sum.astype(jnp.bfloat16), crossing, home).astype(jnp.float32)
+    kl_rows = after(rows_of(kl_rows, member * rows_local, rows_local), input_sum)
+    kl_out = lax.ppermute(kl_rows, crossing, turn)
 
     bias_sums = column_sums(joined_grad)
 
@@ -1394,19 +1425,23 @@
     grad_front = jnp.concatenate(
         [grad_attend.reshape(size_blk * size_batch, plane_rows, 3 * part), vector_grads], axis=1
     )
-    front_sum = sum_blk(
-        sum_batch(
-            lambda z, y: lax.dynamic_index_in_dim(grad_front, z * size_batch + y, 0, keepdims=False)
-        )
-    )
+    middle_sum = halve(after(middle_sum, grad_front), BATCH, 0)
+    reduce_sum = halve(after(reduce_sum, grad_front), BLK, 1)[0, 0, 0]
+    front_sum = halve(grad_front.reshape(grid + grad_front.shape[1:]), BLK, 0)
+    middle_sum = halve(middle_sum, BLK, 1)[0, 0, 0]
+    front_sum = halve(halve(front_sum, BATCH, 0), BLK, 1)[0, 0, 0]
 
     share = reduce_rows // size_vocab
     back = exchange_models(
-        [reduce_sum[t * share : (t + 1) * share].astype(jnp.bfloat16) for t in range(size_vocab)]
-    )
-    middles = exchange_models(
         [
-            middle_sum[t * shard_rows : (t + 1) * shard_rows].astype(jnp.bfloat16)
+            jnp.concatenate(
+                [
+                    middle_sum[t * shard_rows : (t + 1) * shard_rows, k * part : (k + 1) * part]
+                    for k in range(units)
+                ]
+                + [reduce_sum[t * share : (t + 1) * share]],
+                axis=0,
+            ).astype(jnp.bfloat16)
             for t in range(size_vocab)
         ]
     )
@@ -1431,12 +1466,20 @@
             [side[:shard_rows, k * part : (k + 1) * part] for k in range(3) for side in sides],
             axis=1,
         ).astype(jnp.float32)
-        sides = middles[2 * m : 2 * m + 2]
-        output = jnp.concatenate([side[:, ff_part:] for side in sides], axis=1)
-        output = output.astype(jnp.float32)
-        expand = jnp.concatenate([side[:, :ff_part] for side in sides], axis=1)
-        expand = expand.astype(jnp.float32)
-        reduce = jnp.concatenate(back[2 * m : 2 * m + 2], axis=1).astype(jnp.float32)
+        sides = back[2 * m : 2 * m + 2]
+        output = jnp.concatenate(
+            [side[(units - 1) * shard_rows : units * shard_rows] for side in sides], axis=1
+        ).astype(jnp.float32)
+        expand = jnp.concatenate(
+            [
+                side[k * shard_rows : (k + 1) * shard_rows]
+                for side in sides
+                for k in range(units - 1)
+            ],
+            axis=1,
+        ).astype(jnp.float32)
+        reduce = jnp.concatenate([side[units * shard_rows :] for side in sides], axis=1)
+        reduce = reduce.astype(jnp.float32)
         results += [
             pieces[0],
             pieces[1],

time: 666 us -> 560 us (0.84)
  starting transfers between devices: 136 us -> 53 us
  waiting for transfers between devices: 207 us -> 193 us
  matrix products: 55.3 us -> 46 us
  local copies, waits for them, and re-layouts: 38.9 us -> 45.8 us
    ppermute x83 -> x53, starting transfers between devices: 120 us -> 42.8 us  [swap(): lax.ppermute(rows, axis, [(index, index ^ distance) for index in range(co...]
    ppermute x83 -> x53, waiting for transfers between devices: 198 us -> 163 us  [swap(): lax.ppermute(rows, axis, [(index, index ^ distance) for index in range(co...]
    ppermute x1, waiting for transfers between devices: 0.01 us -> 23.4 us  [shards_by_model(): kl_out = lax.ppermute(kl_rows, crossing, turn)]
    add x1 -> x7, other arithmetic: 1.33 us -> 8.58 us  [the longest x6 7.47 us: halve(): mine.astype(jnp.float32)]
    unnamed x190 -> x203, local copies, waits for them, and re-layouts: 13.2 us -> 16 us
  transfers between devices with their start and end apart: 86 -> 56, of which waited for: 38 -> 30; matrix products, arithmetic and copies ran while one was open for 16% -> 15% of each run, Pallas kernels for 6% -> 8%
where the time goes in v1:
time: 560 us; the launch traced here: 552 us
  waiting for transfers between devices  193 us (34%)
  Pallas kernels  159 us (28%)
  starting transfers between devices  53 us (9%)
  other arithmetic  51.1 us (9%)
  matrix products  46 us (8%)
  local copies, waits for them, and re-layouts  45.8 us (8%)
    ppermute x53, waiting for transfers between devices, swap(): lax.ppermute(rows, axis, [(index, index ^ distance) for index in range(co...  163 us
    pallas_call x1, Pallas kernels, vocab_stats(): pl.pallas_call(functools.partial(vocab_stats_kernel, tile=tile, rows_bloc...  63.4 us
    pallas_call x1, Pallas kernels, vocab_grads(): pl.pallas_call(functools.partial(vocab_grads_kernel, tile=tile, columns=c...  53.5 us
    ppermute x53, starting transfers between devices, swap(): lax.ppermute(rows, axis, [(index, index ^ distance) for index in range(co...  42.8 us
    ppermute x1, waiting for transfers between devices, shards_by_model(): kl_out = lax.ppermute(kl_rows, crossing, turn)  23.4 us
    pallas_call x1, Pallas kernels, attend_grads(): pl.pallas_call(functools.partial(attend_grads_kernel, block=block), grid_...  20.6 us
    dot_general x4, matrix products, matmul_left_t(): lax.dot_general(left_side, right_side, (((0,), (0,)), ((), ())), preferre...  17 us
    dot_general x4, matrix products, matmul_plain(): return jnp.dot(left_side, right_side, preferred_element_type=jnp.float32)  16.4 us
  transfers between devices with their start and end apart: 56, of which 30 were waited for; matrix products, arithmetic and copies ran while one was open for 15% of the time, Pallas kernels for 8%

profile of v1, /device:TPU:1, one launch (start us, length us, event | category | flops | bytes accessed | tf_op | source)
XLA Modules:
  0.0 552.4 jit_solution(2465835982480186320)
XLA Ops:
  18.6 4.8 collective-permute-done.10
  23.4 7.3 %collective-permute-done.9 = bf16[216,384]{1,0:T(8,128)(2,1)S(1)} collective-permute-done((bf16[216,384]{1,0:T(8,128)(2,1)S(1)}, bf16[216,384]{1,0:T(8,128)(2,1)S(1)}, u32[]{:S(2)}, u32[]{:S(2)}) %collective-permute-start.9) | collective-permute-done | bytes 165920 | tf_op jit(solution)/shard_map/ppermute | solution.py:1053
  33.6 13.3 %collective-permute-done.7.refs_1_ = bf16[128,1152]{1,0:T(8,128)(2,1)S(1)} collective-permute-done((bf16[128,1152]{1,0:T(8,128)(2,1)S(1)}, bf16[128,1152]{1,0:T(8,128)(2,1)S(1)}, u32[]{:S(2)}, u32[]{:S(2)}) %collective-permute-start.7) | collective-permute-done | bytes 294944 | tf_op jit(solution)/shard_map/ppermute | solution.py:1053
  50.5 15.6 %collective-permute-done.12.refs_1_ = bf16[96,1920]{1,0:T(8,128)(2,1)S(1)} collective-permute-done((bf16[96,1920]{1,0:T(8,128)(2,1)S(1)}, bf16[96,1920]{1,0:T(8,128)(2,1)S(1)}, u32[]{:S(2)}, u32[]{:S(2)}) %collective-permute-start.12) | collective-permute-done | bytes 368672 | tf_op jit(solution)/shard_map/ppermute | solution.py:1053
  68.0 5.2 collective-permute-done.8.refs_2_
  74.6 6.7 %collective-permute-done.15.refs_1_ = bf16[384,384]{1,0:T(8,128)(2,1)S(1)} collective-permute-done((bf16[384,384]{1,0:T(8,128)(2,1)S(1)}, bf16[384,384]{1,0:T(8,128)(2,1)S(1)}, u32[]{:S(2)}, u32[]{:S(2)}) %collective-permute-start.15) | collective-permute-done | bytes 294944 | tf_op jit(solution)/shard_map/ppermute | solution.py:1053
  86.2 8.5 %collective-permute-done.16.refs_2_ = bf16[768,384]{1,0:T(8,128)(2,1)S(1)} collective-permute-done((bf16[768,384]{1,0:T(8,128)(2,1)S(1)}, bf16[768,384]{1,0:T(8,128)(2,1)S(1)}, u32[]{:S(2)}, u32[]{:S(2)}) %collective-permute-start.16) | collective-permute-done | bytes 589856 | tf_op jit(solution)/shard_map/ppermute | solution.py:1053
  97.3 11.7 %collective-permute-done.13.refs_3_ = bf16[512,1152]{1,0:T(8,128)(2,1)S(1)} collective-permute-done((bf16[512,1152]{1,0:T(8,128)(2,1)S(1)}, bf16[512,1152]{1,0:T(8,128)(2,1)S(1)}, u32[]{:S(2)}, u32[]{:S(2)}) %collective-permute-start.13) | collective-permute-done | bytes 1179680 | tf_op jit(solution)/shard_map/ppermute | solution.py:1053
  119.4 11.8 %attend.1 = bf16[1024,384]{1,0:T(8,128)(2,1)} custom-call(s32[1]{0:T(128)} %bitcast.43.length_ref, bf16[1024,1152]{1,0:T(8,128)(2,1)} %add_convert_fusion.query_ref.key_ref.value_ref, bf16[1024,1152]{1,0:T(8,128)(2,1)} %add_convert_fusion.query_ref.key_ref.value_ref, bf16[1024,1152]{1,0:T(8,128)(2,1)} %add_convert_fusion.query_ref.key_ref.value_ref), custom_call_target="tpu_custom_call" | custom-call | tf_op jit(solution)/shard_map/attend/pallas_call | solution.py:939
  157.1 9.2 %fusion.13 = (f32[1024,1536]{1,0:T(8,128)}, bf16[1024,1536]{1,0:T(8,128)(2,1)S(1)}) fusion(f32[1536]{0:T(1024)S(1)} %dynamic_slice.170, bf16[768,1536]{1,0:T(8,128)(2,1)S(1)} %copy-done.65, bf16[512,768]{1,0:T(8,128)(2,1)} %collective-permute-done.21, bf16[512,768]{1,0:T(8,128)(2,1)S(1)} %add_convert_fusion.1), kind=kOutput, calls=%fused_computation.16 | convolution fusion | flops 2458386432 | bytes 13375488 | tf_op jit(solution)/shard_map/dot_general | solution.py:33
  178.3 18.9 %collective-permute-done.25 = bf16[512,768]{1,0:T(8,128)(2,1)} collective-permute-done((bf16[512,768]{1,0:T(8,128)(2,1)}, bf16[512,768]{1,0:T(8,128)(2,1)}, u32[]{:S(2)}, u32[]{:S(2)}) %collective-permute-start.25) | collective-permute-done | bytes 786464 | tf_op jit(solution)/shard_map/ppermute | solution.py:1053
  203.6 63.4 %vocab_stats.1 = (f32[1024,12800]{1,0:T(8,128)}, f32[1024,12800]{1,0:T(8,128)}, f32[8,1024]{1,0:T(8,128)}) custom-call(s32[2]{0:T(128)} %pad_add_fusion.scalars_ref, bf16[4,512,768]{2,1,0:T(8,128)(2,1)} %pad_maximum_fusion.student_low_ref.student_high_ref.teacher_low_ref.teacher_high_ref, ...), custom_call_target="tpu_custom_call" | custom-call | tf_op jit(solution)/shard_map/vocab_stats/pallas_call | solution.py:782
  272.0 53.5 %vocab_grads.1 = (f32[2,512,768]{2,1,0:T(8,128)}, bf16[2,512,768]{2,1,0:T(8,128)(2,1)}, f32[8,1024]{1,0:T(8,128)}) custom-call(f32[1024,12800]{1,0:T(8,128)} %get-tuple-element.85.logit_student_ref, f32[1024,12800]{1,0:T(8,128)} %get-tuple-element.86.logit_teacher_ref, bf16[12576,768]{1,0:T(8,128)(2,1)} %embed_ref.3, f32[8,1024]{1,0:T(8,128)} %get-tuple-element.87.refs_0_, ...), custom_call_target="tpu_custom_call" | custom-call | tf_op jit(solution)/shard_map/vocab_grads/pallas_call | solution.py:878
  332.8 17.6 %collective-permute-done.31 = bf16[512,768]{1,0:T(8,128)(2,1)S(1)} collective-permute-done((bf16[512,768]{1,0:T(8,128)(2,1)S(1)}, bf16[512,768]{1,0:T(8,128)(2,1)S(1)}, u32[]{:S(2)}, u32[]{:S(2)}) %collective-permute-start.31) | collective-permute-done | bytes 786464 | tf_op jit(solution)/shard_map/ppermute | solution.py:1053
  365.4 5.1 convolution_convert_fusion
  380.7 5.1 convolution_convert_fusion.1
  403.0 20.6 %attend_grads.1 = (bf16[1024,384]{1,0:T(8,128)(2,1)}, bf16[1024,384]{1,0:T(8,128)(2,1)}, bf16[1024,384]{1,0:T(8,128)(2,1)}) custom-call(s32[1]{0:T(128)} %bitcast.43.length_ref, bf16[1024,1152]{1,0:T(8,128)(2,1)} %add_convert_fusion.query_ref.key_ref.value_ref, bf16[1024,1152]{1,0:T(8,128)(2,1)} %add_convert_fusion.query_ref.key_ref.value_ref, ...), custom_call_target="tpu_custom_call" | custom-call | tf_op jit(solution)/shard_map/attend_grads/pallas_call | solution.py:1008
  448.0 4.1 convolution_convert_fusion.2
  466.2 4.9 collective-permute-start.55
  476.9 23.4 %collective-permute-done.55 = f32[256]{0:T(256)S(1)} collective-permute-done((f32[256]{0:T(256)S(1)}, f32[256]{0:T(256)S(1)}, u32[]{:S(2)}, u32[]{:S(2)}) %collective-permute-start.55) | collective-permute-done | bytes 1056 | tf_op jit(solution)/shard_map/ppermute | solution.py:1399
  500.6 6.1 %collective-permute-done.54 = bf16[256,768]{1,0:T(8,128)(2,1)S(1)} collective-permute-done((bf16[256,768]{1,0:T(8,128)(2,1)S(1)}, bf16[256,768]{1,0:T(8,128)(2,1)S(1)}, u32[]{:S(2)}, u32[]{:S(2)}) %collective-permute-start.54) | collective-permute-done | bytes 393248 | tf_op jit(solution)/shard_map/ppermute | solution.py:1397
  507.8 5.4 collective-permute-done.45
  520.4 8.2 %collective-permute-done.39 = bf16[2,1,1,104,1152]{4,3,2,1,0:T(8,128)(2,1)S(1)} collective-permute-done((bf16[2,1,1,104,1152]{4,3,2,1,0:T(8,128)(2,1)S(1)}, bf16[2,1,1,104,1152]{4,3,2,1,0:T(8,128)(2,1)S(1)}, u32[]{:S(2)}, u32[]{:S(2)}) %collective-permute-start.39) | collective-permute-done | bytes 479264 | tf_op jit(solution)/shard_map/ppermute | solution.py:1053
  532.5 7.7 %collective-permute-done.40 = bf16[1,1,1,104,1152]{4,3,2,1,0:T(8,128)(2,1)S(1)} collective-permute-done((bf16[1,1,1,104,1152]{4,3,2,1,0:T(8,128)(2,1)S(1)}, bf16[1,1,1,104,1152]{4,3,2,1,0:T(8,128)(2,1)S(1)}, u32[]{:S(2)}, u32[]{:S(2)}) %collective-permute-start.40) | collective-permute-done | bytes 239648 | tf_op jit(solution)/shard_map/ppermute | solution.py:1053
  (503 shorter events, 209.5 us)
Async XLA Ops:
  8.8 22.1 %collective-permute-start = (bf16[256,768]{1,0:T(8,128)(2,1)S(1)}, bf16[256,768]{1,0:T(8,128)(2,1)S(1)}, u32[]{:S(2)}, u32[]{:S(2)}) collective-permute-start(bf16[256,768]{1,0:T(8,128)(2,1)S(1)} %bitcast.380), channel_id=1, source_target_pairs={{0,0},{1,8},{2,16},{3,24},{8,1},{9,9},{10,17},{11,25},{16,2},{17,1... | collective-permute-start | bytes 1179656 | tf_op jit(solution)/shard_map/ppermute | solution.py:1217
  16.1 14.6 %collective-permute-start.9 = (bf16[216,384]{1,0:T(8,128)(2,1)S(1)}, bf16[216,384]{1,0:T(8,128)(2,1)S(1)}, u32[]{:S(2)}, u32[]{:S(2)}) collective-permute-start(bf16[216,384]{1,0:T(8,128)(2,1)S(1)} %get-tuple-element.149), channel_id=1, source_target_pairs={{0,3},{1,2},{2,1},{3,0},{4,7},{5,6},{6,5},{7,4},{8,11},{9,10},{10,... | collective-permute-start | bytes 497672 | tf_op jit(solution)/shard_map/ppermute | solution.py:1053
  31.0 16.0 %collective-permute-start.7 = (bf16[128,1152]{1,0:T(8,128)(2,1)S(1)}, bf16[128,1152]{1,0:T(8,128)(2,1)S(1)}, u32[]{:S(2)}, u32[]{:S(2)}) collective-permute-start(bf16[128,1152]{1,0:T(8,128)(2,1)S(1)} %constant_dynamic-update-slice_fusion.refs_0_), channel_id=1, source_target_pairs={{0,16},{8,24},{16,0},{24,8},{1,17},{9,25},{17,1},{25,9},{2,18},{10... | collective-permute-start | bytes 884744 | tf_op jit(solution)/shard_map/ppermute | solution.py:1053
  33.4 14.4 %collective-permute-start.4 = (bf16[256,768]{1,0:T(8,128)(2,1)S(1)}, bf16[256,768]{1,0:T(8,128)(2,1)S(1)}, u32[]{:S(2)}, u32[]{:S(2)}) collective-permute-start(bf16[256,768]{1,0:T(8,128)(2,1)S(1)} %collective-permute-done), channel_id=1, source_target_pairs={{0,2},{1,3},{2,0},{3,1},{4,6},{5,7},{6,4},{7,5},{8,10},{9,11},{10,... | collective-permute-start | bytes 1179656 | tf_op jit(solution)/shard_map/ppermute | solution.py:1053
  47.0 19.2 %collective-permute-start.12 = (bf16[96,1920]{1,0:T(8,128)(2,1)S(1)}, bf16[96,1920]{1,0:T(8,128)(2,1)S(1)}, u32[]{:S(2)}, u32[]{:S(2)}) collective-permute-start(bf16[96,1920]{1,0:T(8,128)(2,1)S(1)} %constant_dynamic-update-slice_fusion.32.refs_0_), channel_id=1, source_target_pairs={{0,16},{8,24},{16,0},{24,8},{1,17},{9,25},{17,1},{25,9},{2,18},{10... | collective-permute-start | bytes 1105928 | tf_op jit(solution)/shard_map/ppermute | solution.py:1053
  47.0 20.5 %collective-permute-start.6 = (bf16[256,768]{1,0:T(8,128)(2,1)S(1)}, bf16[256,768]{1,0:T(8,128)(2,1)S(1)}, u32[]{:S(2)}, u32[]{:S(2)}) collective-permute-start(bf16[256,768]{1,0:T(8,128)(2,1)S(1)} %collective-permute-done), channel_id=1, source_target_pairs={{0,1},{1,0},{2,3},{3,2},{4,5},{5,4},{6,7},{7,6},{8,9},{9,8},{10,11... | collective-permute-start | bytes 1179656 | tf_op jit(solution)/shard_map/ppermute | solution.py:1053
  47.8 19.7 %collective-permute-start.5 = (bf16[256,768]{1,0:T(8,128)(2,1)S(1)}, bf16[256,768]{1,0:T(8,128)(2,1)S(1)}, u32[]{:S(2)}, u32[]{:S(2)}) collective-permute-start(bf16[256,768]{1,0:T(8,128)(2,1)S(1)} %collective-permute-done.4), channel_id=1, source_target_pairs={{0,1},{1,0},{2,3},{3,2},{4,5},{5,4},{6,7},{7,6},{8,9},{9,8},{10,11... | collective-permute-start | bytes 1179656 | tf_op jit(solution)/shard_map/ppermute | solution.py:1053
  47.9 25.2 %collective-permute-start.8 = (bf16[256,1152]{1,0:T(8,128)(2,1)S(1)}, bf16[256,1152]{1,0:T(8,128)(2,1)S(1)}, u32[]{:S(2)}, u32[]{:S(2)}) collective-permute-start(bf16[256,1152]{1,0:T(8,128)(2,1)S(1)} %pad_maximum_fusion.16), channel_id=1, source_target_pairs={{0,8},{8,0},{16,24},{24,16},{1,9},{9,1},{17,25},{25,17},{2,10},{10... | collective-permute-start | bytes 1769480 | tf_op jit(solution)/shard_map/ppermute | solution.py:1053
  66.2 15.1 %collective-permute-start.15 = (bf16[384,384]{1,0:T(8,128)(2,1)S(1)}, bf16[384,384]{1,0:T(8,128)(2,1)S(1)}, u32[]{:S(2)}, u32[]{:S(2)}) collective-permute-start(bf16[384,384]{1,0:T(8,128)(2,1)S(1)} %pad_maximum_fusion.19.refs_0_), channel_id=1, source_target_pairs={{0,16},{8,24},{16,0},{24,8},{1,17},{9,25},{17,1},{25,9},{2,18},{10... | collective-permute-start | bytes 884744 | tf_op jit(solution)/shard_map/ppermute | solution.py:1053
  66.2 17.4 %collective-permute-start.14 = (bf16[192,1920]{1,0:T(8,128)(2,1)S(1)}, bf16[192,1920]{1,0:T(8,128)(2,1)S(1)}, u32[]{:S(2)}, u32[]{:S(2)}) collective-permute-start(bf16[192,1920]{1,0:T(8,128)(2,1)S(1)} %pad_maximum_fusion.13), channel_id=1, source_target_pairs={{0,4},{4,0},{1,5},{5,1},{2,6},{6,2},{3,7},{7,3},{8,12},{12,8},{9,1... | collective-permute-start | bytes 2211848 | tf_op jit(solution)/shard_map/ppermute | solution.py:1053
  73.3 35.7 %collective-permute-start.13 = (bf16[512,1152]{1,0:T(8,128)(2,1)S(1)}, bf16[512,1152]{1,0:T(8,128)(2,1)S(1)}, u32[]{:S(2)}, u32[]{:S(2)}) collective-permute-start(bf16[512,1152]{1,0:T(8,128)(2,1)S(1)} %pad_maximum_fusion.7), channel_id=1, source_target_pairs={{0,4},{4,0},{1,5},{5,1},{2,6},{6,2},{3,7},{7,3},{8,12},{12,8},{9,1... | collective-permute-start | bytes 3538952 | tf_op jit(solution)/shard_map/ppermute | solution.py:1053
  84.9 46.3 %collective-permute-start.17 = (bf16[384,1920]{1,0:T(8,128)(2,1)}, bf16[384,1920]{1,0:T(8,128)(2,1)}, u32[]{:S(2)}, u32[]{:S(2)}) collective-permute-start(bf16[384,1920]{1,0:T(8,128)(2,1)} %pad_maximum_fusion.6), channel_id=1, source_target_pairs={{0,8},{8,0},{16,24},{24,16},{1,9},{9,1},{17,25},{25,17},{2,10},{10... | collective-permute-start | bytes 4423688 | tf_op jit(solution)/shard_map/ppermute | solution.py:1053
  96.0 43.4 %collective-permute-start.18 = (bf16[1536,384]{1,0:T(8,128)(2,1)}, bf16[1536,384]{1,0:T(8,128)(2,1)}, u32[]{:S(2)}, u32[]{:S(2)}) collective-permute-start(bf16[1536,384]{1,0:T(8,128)(2,1)} %pad_maximum_fusion.8), channel_id=1, source_target_pairs={{0,4},{4,0},{1,5},{5,1},{2,6},{6,2},{3,7},{7,3},{8,12},{12,8},{9,1... | collective-permute-start | bytes 3538952 | tf_op jit(solution)/shard_map/ppermute | solution.py:1053
  178.0 19.2 %collective-permute-start.25 = (bf16[512,768]{1,0:T(8,128)(2,1)}, bf16[512,768]{1,0:T(8,128)(2,1)}, u32[]{:S(2)}, u32[]{:S(2)}) collective-permute-start(bf16[512,768]{1,0:T(8,128)(2,1)} %multiply_convert_fusion.1), channel_id=1, source_target_pairs={{0,2},{1,3},{2,0},{3,1},{4,6},{5,7},{6,4},{7,5},{8,10},{9,11},{10,... | collective-permute-start | bytes 2359304 | tf_op jit(solution)/shard_map/ppermute | solution.py:1053
  178.0 21.2 %collective-permute-start.24 = (bf16[512,768]{1,0:T(8,128)(2,1)}, bf16[512,768]{1,0:T(8,128)(2,1)}, u32[]{:S(2)}, u32[]{:S(2)}) collective-permute-start(bf16[512,768]{1,0:T(8,128)(2,1)} %multiply_convert_fusion.1), channel_id=1, source_target_pairs={{0,1},{1,0},{2,3},{3,2},{4,5},{5,4},{6,7},{7,6},{8,9},{9,8},{10,11... | collective-permute-start | bytes 2359304 | tf_op jit(solution)/shard_map/ppermute | solution.py:1053
  331.6 18.8 %collective-permute-start.31 = (bf16[512,768]{1,0:T(8,128)(2,1)S(1)}, bf16[512,768]{1,0:T(8,128)(2,1)S(1)}, u32[]{:S(2)}, u32[]{:S(2)}) collective-permute-start(bf16[512,768]{1,0:T(8,128)(2,1)S(1)} %fusion.40), channel_id=1, source_target_pairs={{0,2},{1,3},{2,0},{3,1},{4,6},{5,7},{6,4},{7,5},{8,10},{9,11},{10,... | collective-permute-start | bytes 2359304 | tf_op jit(solution)/shard_map/ppermute | solution.py:1053
  390.6 34.8 %collective-permute-start.47 = (bf16[2,2,1,384,384]{4,3,2,1,0:T(8,128)(2,1)}, bf16[2,2,1,384,384]{4,3,2,1,0:T(8,128)(2,1)}, u32[]{:S(2)}, u32[]{:S(2)}) collective-permute-start(bf16[2,2,1,384,384]{4,3,2,1,0:T(8,128)(2,1)} %constant_dynamic-slice_fusion), channel_id=1, source_target_pairs={{0,4},{4,0},{1,5},{5,1},{2,6},{6,2},{3,7},{7,3},{8,12},{12,8},{9,1... | collective-permute-start | bytes 3538952 | tf_op jit(solution)/shard_map/ppermute | solution.py:1053
  393.5 37.0 %collective-permute-start.36 = (bf16[2,1,2,96,1920]{4,3,2,1,0:T(8,128)(2,1)}, bf16[2,1,2,96,1920]{4,3,2,1,0:T(8,128)(2,1)}, u32[]{:S(2)}, u32[]{:S(2)}) collective-permute-start(bf16[2,1,2,96,1920]{4,3,2,1,0:T(8,128)(2,1)} %constant_dynamic-slice_fusion.4), channel_id=1, source_target_pairs={{0,8},{8,0},{16,24},{24,16},{1,9},{9,1},{17,25},{25,17},{2,10},{10... | collective-permute-start | bytes 4423688 | tf_op jit(solution)/shard_map/ppermute | solution.py:1053
  430.4 14.0 %collective-permute-start.48 = (bf16[2,1,1,384,384]{4,3,2,1,0:T(8,128)(2,1)S(1)}, bf16[2,1,1,384,384]{4,3,2,1,0:T(8,128)(2,1)}, u32[]{:S(2)}, u32[]{:S(2)}) collective-permute-start(bf16[2,1,1,384,384]{4,3,2,1,0:T(8,128)(2,1)S(1)} %dynamic-slice_convert_fusion.1), channel_id=1, source_target_pairs={{0,8},{8,0},{16,24},{24,16},{1,9},{9,1},{17,25},{25,17},{2,10},{10... | collective-permute-start | bytes 1769480 | tf_op jit(solution)/shard_map/ppermute | solution.py:1053
  458.7 16.2 %collective-permute-start.49 = (bf16[1,1,1,384,384]{4,3,2,1,0:T(8,128)(2,1)S(1)}, bf16[1,1,1,384,384]{4,3,2,1,0:T(8,128)(2,1)S(1)}, u32[]{:S(2)}, u32[]{:S(2)}) collective-permute-start(bf16[1,1,1,384,384]{4,3,2,1,0:T(8,128)(2,1)S(1)} %dynamic-slice_convert_fusion.4), channel_id=1, source_target_pairs={{0,16},{8,24},{16,0},{24,8},{1,17},{9,25},{17,1},{25,9},{2,18},{10... | collective-permute-start | bytes 884744 | tf_op jit(solution)/shard_map/ppermute | solution.py:1053
  461.7 38.6 %collective-permute-start.44 = (bf16[2,1,1,96,1920]{4,3,2,1,0:T(8,128)(2,1)S(1)}, bf16[2,1,1,96,1920]{4,3,2,1,0:T(8,128)(2,1)S(1)}, u32[]{:S(2)}, u32[]{:S(2)}) collective-permute-start(bf16[2,1,1,96,1920]{4,3,2,1,0:T(8,128)(2,1)S(1)} %dynamic-slice_convert_fusion), channel_id=1, source_target_pairs={{0,4},{4,0},{1,5},{5,1},{2,6},{6,2},{3,7},{7,3},{8,12},{12,8},{9,1... | collective-permute-start | bytes 2211848 | tf_op jit(solution)/shard_map/ppermute | solution.py:1053
  462.2 45.4 %collective-permute-start.38 = (bf16[2,1,2,104,1152]{4,3,2,1,0:T(8,128)(2,1)S(1)}, bf16[2,1,2,104,1152]{4,3,2,1,0:T(8,128)(2,1)S(1)}, u32[]{:S(2)}, u32[]{:S(2)}) collective-permute-start(bf16[2,1,2,104,1152]{4,3,2,1,0:T(8,128)(2,1)S(1)} %fusion.38), channel_id=1, source_target_pairs={{0,8},{8,0},{16,24},{24,16},{1,9},{9,1},{17,25},{25,17},{2,10},{10... | collective-permute-start | bytes 2875400 | tf_op jit(solution)/shard_map/ppermute | solution.py:1053
  466.2 34.1 %collective-permute-start.55 = (f32[256]{0:T(256)S(1)}, f32[256]{0:T(256)S(1)}, u32[]{:S(2)}, u32[]{:S(2)}) collective-permute-start(f32[256]{0:T(256)S(1)} %copy-done.62), channel_id=1, source_target_pairs={{0,0},{1,8},{2,16},{3,24},{8,1},{9,9},{10,17},{11,25},{16,2},{17,1... | collective-permute-start | bytes 3080 | tf_op jit(solution)/shard_map/ppermute | solution.py:1399
  474.9 31.7 %collective-permute-start.54 = (bf16[256,768]{1,0:T(8,128)(2,1)S(1)}, bf16[256,768]{1,0:T(8,128)(2,1)S(1)}, u32[]{:S(2)}, u32[]{:S(2)}) collective-permute-start(bf16[256,768]{1,0:T(8,128)(2,1)S(1)} %convert_add_fusion.8), channel_id=1, source_target_pairs={{0,0},{1,16},{2,8},{3,24},{8,1},{9,17},{10,9},{11,25},{16,2},{17,1... | collective-permute-start | bytes 1179656 | tf_op jit(solution)/shard_map/ppermute | solution.py:1397
  (109 other events, 914.7 us)

commit v2 on v1

--- a/solution.py
+++ b/solution.py
@@ -1053,6 +1053,10 @@
     return lax.ppermute(rows, axis, [(index, index ^ distance) for index in range(count)])
 
 
+def swap_low(rows):
+    return swap(rows.astype(jnp.bfloat16), VOCAB, 1).astype(jnp.float32)
+
+
 def in_pair(second, mine, other, axis=0):
     return jnp.where(
         second,
@@ -1182,14 +1186,18 @@
     )
 
 
-def halve(addends, axis_name, bit):
+def halve_and_see(addends, axis_name, bit, *waits):
     axis = 2 if axis_name == BATCH else 1 - bit
     own = (lax.axis_index(axis_name) >> bit) & 1
     mine = lax.dynamic_slice_in_dim(addends, own, 1, axis)
     theirs = lax.dynamic_slice_in_dim(addends, 1 - own, 1, axis)
-    return mine.astype(jnp.float32) + swap(
-        theirs.astype(jnp.bfloat16), axis_name, 1 << bit
-    ).astype(jnp.float32)
+    received = swap(theirs.astype(jnp.bfloat16), axis_name, 1 << bit)
+    seen = after(received, *waits) if waits else received
+    return mine.astype(jnp.float32) + seen.astype(jnp.float32), received
+
+
+def halve(addends, axis_name, bit, *waits):
+    return halve_and_see(addends, axis_name, bit, *waits)[0]
 
 
 def shards_by_model(hidden, lengths, *rest):
@@ -1211,11 +1219,6 @@
     plane_rows = shard_rows * size_vocab
     crossing = (BLK, VOCAB)
 
-    turn = [
-        (a * size_vocab + b, b * size_vocab + a) for a in range(size_blk) for b in range(size_vocab)
-    ]
-    quarter = lax.ppermute(hidden[0], crossing, turn)
-
     lines = vector_lines_of(params, lengths[0], 3 * part)
     front_slabs, back_slabs = zip(
         *[pack_weights(params[m], h, lines[m]) for m in (0, 1) for h in (0, 1)]
@@ -1245,10 +1248,14 @@
     vector_lines = front_block.shape[0] - plane_rows
     reduce_rows = reduce_block.shape[0]
 
-    front_held = double(((after(front_block, quarter),), ((0,),)), BLK, 1)
+    front_held = double(((front_block,), ((0,),)), BLK, 1)
     middle_held = double(((after(middle_block, front_held[0]),), ((0,),)), BLK, 1)
     reduce_held = double(((after(reduce_block, middle_held[0]),), ((0,),)), BLK, 1)
-    quarter_far = swap(after(quarter, front), VOCAB, 2)
+    turn = [
+        (a * size_vocab + b, b * size_vocab + a) for a in range(size_blk) for b in range(size_vocab)
+    ]
+    quarter = lax.ppermute(after(hidden[0], front_held[0]), crossing, turn)
+    quarter_far = swap(quarter, VOCAB, 2)
     quarters = in_order(
         member, [quarter, swap(quarter, VOCAB, 1), quarter_far, swap(quarter_far, VOCAB, 1)]
     )
@@ -1298,7 +1305,7 @@
     middle = (
         inputs_own
         + rows_of(attended, half * own_rows, own_rows)
-        + swap(rows_of(attended, (1 - half) * own_rows, own_rows), VOCAB, 1)
+        + swap_low(rows_of(attended, (1 - half) * own_rows, own_rows))
         + output_bias
     )
     normed_own = layer_norm(middle, second_gain, second_shift).astype(jnp.bfloat16)
@@ -1314,7 +1321,7 @@
         axis=1,
     )
     reduced = matmul_plain(active, reduce_weight)
-    block_out = middle + reduced[:own_rows] + swap(reduced[own_rows:], VOCAB, 1) + reduce_bias
+    block_out = middle + reduced[:own_rows] + swap_low(reduced[own_rows:]) + reduce_bias
     final_rows = (0.5 * layer_norm(block_out, gain_final, shift_final)).astype(jnp.bfloat16)
 
     final_far = swap(final_rows, VOCAB, 2)
@@ -1345,17 +1352,15 @@
     branch_own = grad_out.astype(jnp.bfloat16)
     branch_low = jnp.concatenate([branch_own, swap(branch_own, VOCAB, 1)], axis=0)
     grad_reduce = matmul_left_t(active, branch_low).astype(jnp.bfloat16)
-    grad_reduce = in_pair(
-        is_second,
-        columns_of(grad_reduce, half * part, part),
-        swap(columns_of(grad_reduce, (1 - half) * part, part), VOCAB, 1),
-    )
+    branch_low = after(branch_low, grad_reduce)
+    reduce_other = swap(columns_of(grad_reduce, (1 - half) * part, part), VOCAB, 1)
+    grad_reduce = in_pair(is_second, columns_of(grad_reduce, half * part, part), reduce_other)
     grid = (2, 2, 2)
-    reduce_sum = halve(grad_reduce.reshape(grid + (reduce_rows, part)), BATCH, 0)
+    grad_reduce = grad_reduce.reshape(grid + (reduce_rows, part))
     grad_active = matmul_right_t(branch_low, reduce_weight)
     inner_grad = (grad_active * slope).astype(jnp.bfloat16)
-    grad_normed = matmul_right_t(inner_grad, expand_weight)
-    grad_normed_own = grad_normed[:own_rows] + swap(grad_normed[own_rows:], VOCAB, 1)
+    grad_normed = matmul_right_t(after(inner_grad, reduce_other), expand_weight)
+    grad_normed_own = grad_normed[:own_rows] + swap_low(grad_normed[own_rows:])
     middle_part, grad_second_gain, grad_second_shift = norm_back(
         middle, second_gain, grad_normed_own
     )
@@ -1370,33 +1375,43 @@
         columns_of(grad_output, half * part, part),
         swap(columns_of(grad_output, (1 - half) * part, part), VOCAB, 1),
     )
-    grad_middles = jnp.concatenate([grad_expand, grad_output], axis=1)
-    grad_middles = grad_middles.reshape(grid + (plane_rows, ff_part + part))
-    middle_sum = halve(grad_middles, BLK, 0)
-    joined_grad = jnp.concatenate(attend_grads(joined, grad_mixed, seq_length, block), axis=1)
-    reduce_sum = halve(after(reduce_sum, joined_grad), BLK, 0)
-    joined_grad = after(joined_grad, middle_sum)
+    grad_expand = grad_expand.reshape(grid + (plane_rows, ff_part))
+    joined_parts = attend_grads(joined, grad_mixed, seq_length, block)
+    reduce_sum = halve(grad_reduce, BATCH, 0, joined_parts[0])
+    expand_sum = halve(grad_expand, BLK, 0, joined_parts[0])
+    joined_grad = after(jnp.concatenate(joined_parts, axis=1), reduce_sum, expand_sum)
     grad_normed = matmul_right_t(joined_grad, attend_weight)
     grad_attend = matmul_left_t(normed_one, joined_grad).astype(jnp.bfloat16)
-    grad_normed_own = rows_of(grad_normed, half * own_rows, own_rows) + swap(
-        rows_of(grad_normed, (1 - half) * own_rows, own_rows), VOCAB, 1
-    )
+    reduce_sum, reduce_seen = halve_and_see(reduce_sum, BLK, 0)
+    expand_sum, expand_seen = halve_and_see(expand_sum, BATCH, 0)
+    normed_other = after(rows_of(grad_normed, (1 - half) * own_rows, own_rows), reduce_seen, expand_seen)
+    normed_other = swap_low(normed_other)
+    grad_normed_own = rows_of(grad_normed, half * own_rows, own_rows) + normed_other
     input_part, grad_first_gain, grad_first_shift = norm_back(
         inputs_own, first_gain, grad_normed_own
     )
     grad_inputs = (grad_middle + input_part).reshape(2, rows_local, width)
-    input_sum = jnp.where(is_teacher, grad_inputs[1], grad_inputs[0]) + swap(
+    input_other = swap(
         jnp.where(is_teacher, grad_inputs[0], grad_inputs[1]).astype(jnp.bfloat16), VOCAB, 2
-    ).astype(jnp.float32)
+    )
+    input_sum = jnp.where(is_teacher, grad_inputs[1], grad_inputs[0])
+    input_sum += input_other.astype(jnp.float32)
     home = [
         (a * size_vocab + 2 * m + h, (2 * h + m) * size_vocab + a)
         for a in range(size_blk)
         for m in (0, 1)
         for h in (0, 1)
     ]
-    input_grad = lax.ppermute(input_sum.astype(jnp.bfloat16), crossing, home).astype(jnp.float32)
-    kl_rows = after(rows_of(kl_rows, member * rows_local, rows_local), input_sum)
-    kl_out = lax.ppermute(kl_rows, crossing, turn)
+    kl_rows = rows_of(kl_rows, (2 * half + model) * rows_local, rows_local)
+    kl_high = kl_rows.astype(jnp.bfloat16)
+    kl_low = (kl_rows - kl_high.astype(jnp.float32)).astype(jnp.bfloat16)
+    kl_line = jnp.concatenate([kl_high, kl_low])
+    kl_line = jnp.pad(kl_line[None], ((0, 7), (0, width - kl_line.shape[0])))
+    home_rows = lax.ppermute(
+        jnp.concatenate([input_sum.astype(jnp.bfloat16), kl_line], axis=0), crossing, home
+    ).astype(jnp.float32)
+    input_grad = home_rows[:rows_local]
+    kl_out = home_rows[rows_local, :rows_local] + home_rows[rows_local, rows_local : 2 * rows_local]
 
     bias_sums = column_sums(joined_grad)
 
@@ -1425,20 +1440,25 @@
     grad_front = jnp.concatenate(
         [grad_attend.reshape(size_blk * size_batch, plane_rows, 3 * part), vector_grads], axis=1
     )
-    middle_sum = halve(after(middle_sum, grad_front), BATCH, 0)
-    reduce_sum = halve(after(reduce_sum, grad_front), BLK, 1)[0, 0, 0]
-    front_sum = halve(grad_front.reshape(grid + grad_front.shape[1:]), BLK, 0)
-    middle_sum = halve(middle_sum, BLK, 1)[0, 0, 0]
-    front_sum = halve(halve(front_sum, BATCH, 0), BLK, 1)[0, 0, 0]
-
+    front_sum, seen = halve_and_see(grad_front.reshape(grid + grad_front.shape[1:]), BATCH, 0)
+    output_sum = halve(grad_output.reshape(grid + (plane_rows, part)), BLK, 0, input_other)
+    output_sum = halve(output_sum, BATCH, 0, seen)
+    front_sum, seen = halve_and_see(front_sum, BLK, 0)
+    reduce_sum = halve(reduce_sum, BLK, 1, seen)[0, 0, 0]
+    expand_sum = halve(expand_sum, BLK, 1, seen)[0, 0, 0]
+    output_sum = halve(output_sum, BLK, 1, seen)[0, 0, 0]
+    front_sum = halve(front_sum, BLK, 1)[0, 0, 0]
+
+    units = (ff_part + part) // part
     share = reduce_rows // size_vocab
     back = exchange_models(
         [
             jnp.concatenate(
                 [
-                    middle_sum[t * shard_rows : (t + 1) * shard_rows, k * part : (k + 1) * part]
-                    for k in range(units)
+                    expand_sum[t * shard_rows : (t + 1) * shard_rows, k * part : (k + 1) * part]
+                    for k in range(units - 1)
                 ]
+                + [output_sum[t * shard_rows : (t + 1) * shard_rows]]
                 + [reduce_sum[t * share : (t + 1) * share]],
                 axis=0,
             ).astype(jnp.bfloat16)

time: 560 us -> 528 us (0.943)
  waiting for transfers between devices: 193 us -> 157 us
  starting transfers between devices: 53 us -> 74.2 us
  local copies, waits for them, and re-layouts: 45.8 us -> 33 us
    ppermute x3 -> x2, waiting for transfers between devices: 29.6 us -> 9.04 us  [the longest x1 9.04 us: shards_by_model(): lax.ppermute(jnp.concatenate([input_sum.astype(jnp.bfloat16), kl_line], a...]
    ppermute x53 -> x56, starting transfers between devices: 42.8 us -> 62.2 us  [swap(): lax.ppermute(rows, axis, [(index, index ^ distance) for index in range(co...]
    ppermute x53 -> x56, waiting for transfers between devices: 163 us -> 148 us  [swap(): lax.ppermute(rows, axis, [(index, index ^ distance) for index in range(co...]
    unnamed x203 -> x175, local copies, waits for them, and re-layouts: 16 us -> 10.4 us
    ppermute x3 -> x2, starting transfers between devices: 10.2 us -> 12 us  [the longest x1 6.64 us: shards_by_model(): quarter = lax.ppermute(after(hidden[0], front_held[0]), crossing, turn)]
  transfers between devices with their start and end apart: 56 -> 58, of which waited for: 30 -> 31; matrix products, arithmetic and copies ran while one was open for 15% -> 13% of each run, Pallas kernels for 8% -> 8%
where the time goes in v2:
time: 528 us; the launch traced here: 521 us
  Pallas kernels  159 us (30%)
  waiting for transfers between devices  157 us (30%)
  starting transfers between devices  74.2 us (14%)
  matrix products  46.6 us (9%)
  other arithmetic  46.4 us (9%)
  local copies, waits for them, and re-layouts  33 us (6%)
    ppermute x56, waiting for transfers between devices, swap(): lax.ppermute(rows, axis, [(index, index ^ distance) for index in range(co...  148 us
    pallas_call x1, Pallas kernels, vocab_stats(): pl.pallas_call(functools.partial(vocab_stats_kernel, tile=tile, rows_bloc...  63.3 us
    ppermute x56, starting transfers between devices, swap(): lax.ppermute(rows, axis, [(index, index ^ distance) for index in range(co...  62.2 us
    pallas_call x1, Pallas kernels, vocab_grads(): pl.pallas_call(functools.partial(vocab_grads_kernel, tile=tile, columns=c...  53.6 us
    pallas_call x1, Pallas kernels, attend_grads(): pl.pallas_call(functools.partial(attend_grads_kernel, block=block), grid_...  20.8 us
    dot_general x4, matrix products, matmul_plain(): return jnp.dot(left_side, right_side, preferred_element_type=jnp.float32)  16.5 us
    dot_general x4, matrix products, matmul_left_t(): lax.dot_general(left_side, right_side, (((0,), (0,)), ((), ())), preferre...  15.5 us
    dot_general x4, matrix products, matmul_right_t(): lax.dot_general(left_side, right_side, (((1,), (1,)), ((), ())), preferre...  14.7 us
  transfers between devices with their start and end apart: 58, of which 31 were waited for; matrix products, arithmetic and copies ran while one was open for 13% of the time, Pallas kernels for 8%

profile of v2, /device:TPU:1, one launch (start us, length us, event | category | flops | bytes accessed | tf_op | source)
XLA Modules:
  0.0 521.2 jit_solution(1998311562575453723)
XLA Ops:
  23.2 7.9 %collective-permute-done.3.refs_1_ = bf16[128,1152]{1,0:T(8,128)(2,1)S(1)} collective-permute-done((bf16[128,1152]{1,0:T(8,128)(2,1)S(1)}, bf16[128,1152]{1,0:T(8,128)(2,1)S(1)}, u32[]{:S(2)}, u32[]{:S(2)}) %collective-permute-start.3) | collective-permute-done | bytes 294944 | tf_op jit(solution)/shard_map/ppermute | solution.py:1053
  31.1 6.6 %collective-permute-start.4 = (bf16[256,768]{1,0:T(8,128)(2,1)S(1)}, bf16[256,768]{1,0:T(8,128)(2,1)S(1)}, u32[]{:S(2)}, u32[]{:S(2)}) collective-permute-start(bf16[256,768]{1,0:T(8,128)(2,1)S(1)} %bitcast.380), channel_id=1, source_target_pairs={{0,0},{1,8},{2,16},{3,24},{8,1},{9,9},{10,17},{11,25},{16,2},{17,1... | collective-permute-start | bytes 1179656 | tf_op jit(solution)/shard_map/ppermute | solution.py:1257
  37.9 19.5 %collective-permute-done.12.refs_1_ = bf16[96,1920]{1,0:T(8,128)(2,1)S(1)} collective-permute-done((bf16[96,1920]{1,0:T(8,128)(2,1)S(1)}, bf16[96,1920]{1,0:T(8,128)(2,1)S(1)}, u32[]{:S(2)}, u32[]{:S(2)}) %collective-permute-start.12) | collective-permute-done | bytes 368672 | tf_op jit(solution)/shard_map/ppermute | solution.py:1053
  58.3 9.6 %collective-permute-start.15 = (bf16[384,384]{1,0:T(8,128)(2,1)S(1)}, bf16[384,384]{1,0:T(8,128)(2,1)S(1)}, u32[]{:S(2)}, u32[]{:S(2)}) collective-permute-start(bf16[384,384]{1,0:T(8,128)(2,1)S(1)} %pad_maximum_fusion.15.refs_0_), channel_id=1, source_target_pairs={{0,16},{8,24},{16,0},{24,8},{1,17},{9,25},{17,1},{25,9},{2,18},{10... | collective-permute-start | bytes 884744 | tf_op jit(solution)/shard_map/ppermute | solution.py:1053
  76.3 4.6 collective-permute-done.15.refs_1_
  84.9 9.7 %collective-permute-done.16.refs_2_ = bf16[768,384]{1,0:T(8,128)(2,1)S(1)} collective-permute-done((bf16[768,384]{1,0:T(8,128)(2,1)S(1)}, bf16[768,384]{1,0:T(8,128)(2,1)S(1)}, u32[]{:S(2)}, u32[]{:S(2)}) %collective-permute-start.16) | collective-permute-done | bytes 589856 | tf_op jit(solution)/shard_map/ppermute | solution.py:1053
  97.1 5.9 %collective-permute-done.13.refs_3_ = bf16[512,1152]{1,0:T(8,128)(2,1)} collective-permute-done((bf16[512,1152]{1,0:T(8,128)(2,1)S(1)}, bf16[512,1152]{1,0:T(8,128)(2,1)}, u32[]{:S(2)}, u32[]{:S(2)}) %collective-permute-start.13) | collective-permute-done | bytes 1179680 | tf_op jit(solution)/shard_map/ppermute | solution.py:1053
  112.4 11.8 %attend.1 = bf16[1024,384]{1,0:T(8,128)(2,1)} custom-call(s32[1]{0:T(128)} %bitcast.43.length_ref, bf16[1024,1152]{1,0:T(8,128)(2,1)} %add_convert_fusion.query_ref.key_ref.value_ref, bf16[1024,1152]{1,0:T(8,128)(2,1)} %add_convert_fusion.query_ref.key_ref.value_ref, bf16[1024,1152]{1,0:T(8,128)(2,1)} %add_convert_fusion.query_ref.key_ref.value_ref), custom_call_target="tpu_custom_call" | custom-call | tf_op jit(solution)/shard_map/attend/pallas_call | solution.py:939
  149.9 9.2 %fusion.13 = (f32[1024,1536]{1,0:T(8,128)}, bf16[1024,1536]{1,0:T(8,128)(2,1)S(1)}) fusion(f32[1536]{0:T(1024)S(1)} %dynamic_slice.188, bf16[768,1536]{1,0:T(8,128)(2,1)S(1)} %copy-done.55, bf16[512,768]{1,0:T(8,128)(2,1)} %collective-permute-done.21, bf16[512,768]{1,0:T(8,128)(2,1)S(1)} %add_convert_fusion.1), kind=kOutput, calls=%fused_computation.16 | convolution fusion | flops 2458386432 | bytes 13375488 | tf_op jit(solution)/shard_map/dot_general | solution.py:33
  171.6 17.1 %collective-permute-done.25 = bf16[512,768]{1,0:T(8,128)(2,1)} collective-permute-done((bf16[512,768]{1,0:T(8,128)(2,1)}, bf16[512,768]{1,0:T(8,128)(2,1)}, u32[]{:S(2)}, u32[]{:S(2)}) %collective-permute-start.25) | collective-permute-done | bytes 786464 | tf_op jit(solution)/shard_map/ppermute | solution.py:1053
  195.1 63.3 %vocab_stats.1 = (f32[1024,12800]{1,0:T(8,128)}, f32[1024,12800]{1,0:T(8,128)}, f32[8,1024]{1,0:T(8,128)}) custom-call(s32[2]{0:T(128)} %pad_add_fusion.scalars_ref, bf16[4,512,768]{2,1,0:T(8,128)(2,1)} %pad_maximum_fusion.student_low_ref.student_high_ref.teacher_low_ref.teacher_high_ref, ...), custom_call_target="tpu_custom_call" | custom-call | tf_op jit(solution)/shard_map/vocab_stats/pallas_call | solution.py:782
  264.6 53.6 %vocab_grads.1 = (f32[2,512,768]{2,1,0:T(8,128)}, bf16[2,512,768]{2,1,0:T(8,128)(2,1)}, f32[8,1024]{1,0:T(8,128)}) custom-call(f32[1024,12800]{1,0:T(8,128)} %get-tuple-element.89.logit_student_ref, f32[1024,12800]{1,0:T(8,128)} %get-tuple-element.90.logit_teacher_ref, bf16[12576,768]{1,0:T(8,128)(2,1)} %embed_ref.3, f32[8,1024]{1,0:T(8,128)} %get-tuple-element.91.refs_0_, ...), custom_call_target="tpu_custom_call" | custom-call | tf_op jit(solution)/shard_map/vocab_grads/pallas_call | solution.py:878
  324.6 18.4 %collective-permute-done.31 = bf16[512,768]{1,0:T(8,128)(2,1)S(1)} collective-permute-done((bf16[512,768]{1,0:T(8,128)(2,1)S(1)}, bf16[512,768]{1,0:T(8,128)(2,1)S(1)}, u32[]{:S(2)}, u32[]{:S(2)}) %collective-permute-start.31) | collective-permute-done | bytes 786464 | tf_op jit(solution)/shard_map/ppermute | solution.py:1053
  349.2 4.7 convolution_convert_fusion.1
  356.2 4.8 convert_reduce_fusion
  361.1 4.4 convolution_convert_fusion
  383.3 20.8 %attend_grads.1 = (bf16[1024,384]{1,0:T(8,128)(2,1)}, bf16[1024,384]{1,0:T(8,128)(2,1)}, bf16[1024,384]{1,0:T(8,128)(2,1)}) custom-call(s32[1]{0:T(128)} %bitcast.43.length_ref, bf16[1024,1152]{1,0:T(8,128)(2,1)} %add_convert_fusion.query_ref.key_ref.value_ref, bf16[1024,1152]{1,0:T(8,128)(2,1)} %add_convert_fusion.query_ref.key_ref.value_ref, ...), custom_call_target="tpu_custom_call" | custom-call | tf_op jit(solution)/shard_map/attend_grads/pallas_call | solution.py:1008
  425.5 5.3 %collective-permute-done.39 = bf16[2,1,1,96,1536]{4,3,2,1,0:T(8,128)(2,1)} collective-permute-done((bf16[2,1,1,96,1536]{4,3,2,1,0:T(8,128)(2,1)}, bf16[2,1,1,96,1536]{4,3,2,1,0:T(8,128)(2,1)}, u32[]{:S(2)}, u32[]{:S(2)}) %collective-permute-start.39) | collective-permute-done | bytes 589856 | tf_op jit(solution)/shard_map/ppermute | solution.py:1053
  444.3 5.9 %collective-permute-done.50 = bf16[256,768]{1,0:T(8,128)(2,1)} collective-permute-done((bf16[256,768]{1,0:T(8,128)(2,1)}, bf16[256,768]{1,0:T(8,128)(2,1)}, u32[]{:S(2)}, u32[]{:S(2)}) %collective-permute-start.50) | collective-permute-done | bytes 393248 | tf_op jit(solution)/shard_map/ppermute | solution.py:1053
  451.4 5.3 %collective-permute-start.57 = (bf16[264,768]{1,0:T(8,128)(2,1)S(1)}, bf16[264,768]{1,0:T(8,128)(2,1)S(1)}, u32[]{:S(2)}, u32[]{:S(2)}) collective-permute-start(bf16[264,768]{1,0:T(8,128)(2,1)S(1)} %fusion.42), channel_id=1, source_target_pairs={{0,0},{1,16},{2,8},{3,24},{8,1},{9,17},{10,9},{11,25},{16,2},{17,1... | collective-permute-start | bytes 1216520 | tf_op jit(solution)/shard_map/ppermute | solution.py:1410
  459.6 9.0 %collective-permute-done.57 = bf16[264,768]{1,0:T(8,128)(2,1)S(1)} collective-permute-done((bf16[264,768]{1,0:T(8,128)(2,1)S(1)}, bf16[264,768]{1,0:T(8,128)(2,1)S(1)}, u32[]{:S(2)}, u32[]{:S(2)}) %collective-permute-start.57) | collective-permute-done | bytes 405536 | tf_op jit(solution)/shard_map/ppermute | solution.py:1410
  476.6 6.8 %collective-permute-done.52 = bf16[1,1,1,96,384]{4,3,2,1,0:T(8,128)(2,1)S(1)} collective-permute-done((bf16[1,1,1,96,384]{4,3,2,1,0:T(8,128)(2,1)S(1)}, bf16[1,1,1,96,384]{4,3,2,1,0:T(8,128)(2,1)S(1)}, u32[]{:S(2)}, u32[]{:S(2)}) %collective-permute-start.52) | collective-permute-done | bytes 73760 | tf_op jit(solution)/shard_map/ppermute | solution.py:1053
  483.4 8.8 %collective-permute-done.42 = bf16[2,1,1,104,1152]{4,3,2,1,0:T(8,128)(2,1)S(1)} collective-permute-done((bf16[2,1,1,104,1152]{4,3,2,1,0:T(8,128)(2,1)S(1)}, bf16[2,1,1,104,1152]{4,3,2,1,0:T(8,128)(2,1)S(1)}, u32[]{:S(2)}, u32[]{:S(2)}) %collective-permute-start.42) | collective-permute-done | bytes 479264 | tf_op jit(solution)/shard_map/ppermute | solution.py:1053
  496.2 4.5 collective-permute-done.54
  (488 shorter events, 198.4 us)
Async XLA Ops:
  15.3 15.8 %collective-permute-start.3 = (bf16[128,1152]{1,0:T(8,128)(2,1)S(1)}, bf16[128,1152]{1,0:T(8,128)(2,1)S(1)}, u32[]{:S(2)}, u32[]{:S(2)}) collective-permute-start(bf16[128,1152]{1,0:T(8,128)(2,1)S(1)} %get-tuple-element.74.refs_0_), channel_id=1, source_target_pairs={{0,16},{8,24},{16,0},{24,8},{1,17},{9,25},{17,1},{25,9},{2,18},{10... | collective-permute-start | bytes 884744 | tf_op jit(solution)/shard_map/ppermute | solution.py:1053
  31.1 26.3 %collective-permute-start.12 = (bf16[96,1920]{1,0:T(8,128)(2,1)S(1)}, bf16[96,1920]{1,0:T(8,128)(2,1)S(1)}, u32[]{:S(2)}, u32[]{:S(2)}) collective-permute-start(bf16[96,1920]{1,0:T(8,128)(2,1)S(1)} %constant_dynamic-update-slice_fusion.41.refs_0_), channel_id=1, source_target_pairs={{0,16},{8,24},{16,0},{24,8},{1,17},{9,25},{17,1},{25,9},{2,18},{10... | collective-permute-start | bytes 1105928 | tf_op jit(solution)/shard_map/ppermute | solution.py:1053
  31.1 27.1 %collective-permute-start.4 = (bf16[256,768]{1,0:T(8,128)(2,1)S(1)}, bf16[256,768]{1,0:T(8,128)(2,1)S(1)}, u32[]{:S(2)}, u32[]{:S(2)}) collective-permute-start(bf16[256,768]{1,0:T(8,128)(2,1)S(1)} %bitcast.380), channel_id=1, source_target_pairs={{0,0},{1,8},{2,16},{3,24},{8,1},{9,9},{10,17},{11,25},{16,2},{17,1... | collective-permute-start | bytes 1179656 | tf_op jit(solution)/shard_map/ppermute | solution.py:1257
  37.8 33.7 %collective-permute-start.8 = (bf16[256,1152]{1,0:T(8,128)(2,1)S(1)}, bf16[256,1152]{1,0:T(8,128)(2,1)S(1)}, u32[]{:S(2)}, u32[]{:S(2)}) collective-permute-start(bf16[256,1152]{1,0:T(8,128)(2,1)S(1)} %constant_dynamic-update-slice_fusion.8), channel_id=1, source_target_pairs={{0,8},{8,0},{16,24},{24,16},{1,9},{9,1},{17,25},{25,17},{2,10},{10... | collective-permute-start | bytes 1769480 | tf_op jit(solution)/shard_map/ppermute | solution.py:1053
  57.5 24.2 %collective-permute-start.14 = (bf16[192,1920]{1,0:T(8,128)(2,1)S(1)}, bf16[192,1920]{1,0:T(8,128)(2,1)S(1)}, u32[]{:S(2)}, u32[]{:S(2)}) collective-permute-start(bf16[192,1920]{1,0:T(8,128)(2,1)S(1)} %pad_maximum_fusion.10), channel_id=1, source_target_pairs={{0,4},{4,0},{1,5},{5,1},{2,6},{6,2},{3,7},{7,3},{8,12},{12,8},{9,1... | collective-permute-start | bytes 2211848 | tf_op jit(solution)/shard_map/ppermute | solution.py:1053
  58.3 22.5 %collective-permute-start.15 = (bf16[384,384]{1,0:T(8,128)(2,1)S(1)}, bf16[384,384]{1,0:T(8,128)(2,1)S(1)}, u32[]{:S(2)}, u32[]{:S(2)}) collective-permute-start(bf16[384,384]{1,0:T(8,128)(2,1)S(1)} %pad_maximum_fusion.15.refs_0_), channel_id=1, source_target_pairs={{0,16},{8,24},{16,0},{24,8},{1,17},{9,25},{17,1},{25,9},{2,18},{10... | collective-permute-start | bytes 884744 | tf_op jit(solution)/shard_map/ppermute | solution.py:1053
  69.9 14.0 %collective-permute-start.7 = (bf16[256,768]{1,0:T(8,128)(2,1)S(1)}, bf16[256,768]{1,0:T(8,128)(2,1)S(1)}, u32[]{:S(2)}, u32[]{:S(2)}) collective-permute-start(bf16[256,768]{1,0:T(8,128)(2,1)S(1)} %collective-permute-done.4), channel_id=1, source_target_pairs={{0,1},{1,0},{2,3},{3,2},{4,5},{5,4},{6,7},{7,6},{8,9},{9,8},{10,11... | collective-permute-start | bytes 1179656 | tf_op jit(solution)/shard_map/ppermute | solution.py:1053
  75.2 27.8 %collective-permute-start.13 = (bf16[512,1152]{1,0:T(8,128)(2,1)S(1)}, bf16[512,1152]{1,0:T(8,128)(2,1)}, u32[]{:S(2)}, u32[]{:S(2)}) collective-permute-start(bf16[512,1152]{1,0:T(8,128)(2,1)S(1)} %pad_maximum_fusion.6), channel_id=1, source_target_pairs={{0,4},{4,0},{1,5},{5,1},{2,6},{6,2},{3,7},{7,3},{8,12},{12,8},{9,1... | collective-permute-start | bytes 3538952 | tf_op jit(solution)/shard_map/ppermute | solution.py:1053
  83.0 43.2 %collective-permute-start.17 = (bf16[384,1920]{1,0:T(8,128)(2,1)}, bf16[384,1920]{1,0:T(8,128)(2,1)}, u32[]{:S(2)}, u32[]{:S(2)}) collective-permute-start(bf16[384,1920]{1,0:T(8,128)(2,1)} %pad_maximum_fusion.5), channel_id=1, source_target_pairs={{0,8},{8,0},{16,24},{24,16},{1,9},{9,1},{17,25},{25,17},{2,10},{10... | collective-permute-start | bytes 4423688 | tf_op jit(solution)/shard_map/ppermute | solution.py:1053
  95.9 37.4 %collective-permute-start.18 = (bf16[1536,384]{1,0:T(8,128)(2,1)}, bf16[1536,384]{1,0:T(8,128)(2,1)}, u32[]{:S(2)}, u32[]{:S(2)}) collective-permute-start(bf16[1536,384]{1,0:T(8,128)(2,1)} %pad_maximum_fusion.7), channel_id=1, source_target_pairs={{0,4},{4,0},{1,5},{5,1},{2,6},{6,2},{3,7},{7,3},{8,12},{12,8},{9,1... | collective-permute-start | bytes 3538952 | tf_op jit(solution)/shard_map/ppermute | solution.py:1053
  169.6 19.2 %collective-permute-start.25 = (bf16[512,768]{1,0:T(8,128)(2,1)}, bf16[512,768]{1,0:T(8,128)(2,1)}, u32[]{:S(2)}, u32[]{:S(2)}) collective-permute-start(bf16[512,768]{1,0:T(8,128)(2,1)} %multiply_convert_fusion.1), channel_id=1, source_target_pairs={{0,2},{1,3},{2,0},{3,1},{4,6},{5,7},{6,4},{7,5},{8,10},{9,11},{10,... | collective-permute-start | bytes 2359304 | tf_op jit(solution)/shard_map/ppermute | solution.py:1053
  171.0 19.8 %collective-permute-start.24 = (bf16[512,768]{1,0:T(8,128)(2,1)}, bf16[512,768]{1,0:T(8,128)(2,1)}, u32[]{:S(2)}, u32[]{:S(2)}) collective-permute-start(bf16[512,768]{1,0:T(8,128)(2,1)} %multiply_convert_fusion.1), channel_id=1, source_target_pairs={{0,1},{1,0},{2,3},{3,2},{4,5},{5,4},{6,7},{7,6},{8,9},{9,8},{10,11... | collective-permute-start | bytes 2359304 | tf_op jit(solution)/shard_map/ppermute | solution.py:1053
  324.3 18.8 %collective-permute-start.31 = (bf16[512,768]{1,0:T(8,128)(2,1)S(1)}, bf16[512,768]{1,0:T(8,128)(2,1)S(1)}, u32[]{:S(2)}, u32[]{:S(2)}) collective-permute-start(bf16[512,768]{1,0:T(8,128)(2,1)S(1)} %fusion.41), channel_id=1, source_target_pairs={{0,2},{1,3},{2,0},{3,1},{4,6},{5,7},{6,4},{7,5},{8,10},{9,11},{10,... | collective-permute-start | bytes 2359304 | tf_op jit(solution)/shard_map/ppermute | solution.py:1053
  369.7 34.4 %collective-permute-start.37 = (bf16[2,1,2,96,1536]{4,3,2,1,0:T(8,128)(2,1)}, bf16[2,1,2,96,1536]{4,3,2,1,0:T(8,128)(2,1)S(1)}, u32[]{:S(2)}, u32[]{:S(2)}) collective-permute-start(bf16[2,1,2,96,1536]{4,3,2,1,0:T(8,128)(2,1)} %constant_dynamic-slice_fusion.4), channel_id=1, source_target_pairs={{0,8},{8,0},{16,24},{24,16},{1,9},{9,1},{17,25},{25,17},{2,10},{10... | collective-permute-start | bytes 3538952 | tf_op jit(solution)/shard_map/ppermute | solution.py:1053
  371.6 32.5 %collective-permute-start.36 = (bf16[2,2,1,384,384]{4,3,2,1,0:T(8,128)(2,1)}, bf16[2,2,1,384,384]{4,3,2,1,0:T(8,128)(2,1)}, u32[]{:S(2)}, u32[]{:S(2)}) collective-permute-start(bf16[2,2,1,384,384]{4,3,2,1,0:T(8,128)(2,1)} %constant_dynamic-slice_fusion.5), channel_id=1, source_target_pairs={{0,4},{4,0},{1,5},{5,1},{2,6},{6,2},{3,7},{7,3},{8,12},{12,8},{9,1... | collective-permute-start | bytes 3538952 | tf_op jit(solution)/shard_map/ppermute | solution.py:1053
  415.8 14.9 %collective-permute-start.39 = (bf16[2,1,1,96,1536]{4,3,2,1,0:T(8,128)(2,1)}, bf16[2,1,1,96,1536]{4,3,2,1,0:T(8,128)(2,1)}, u32[]{:S(2)}, u32[]{:S(2)}) collective-permute-start(bf16[2,1,1,96,1536]{4,3,2,1,0:T(8,128)(2,1)} %dynamic-slice_convert_fusion.1), channel_id=1, source_target_pairs={{0,4},{4,0},{1,5},{5,1},{2,6},{6,2},{3,7},{7,3},{8,12},{12,8},{9,1... | collective-permute-start | bytes 1769480 | tf_op jit(solution)/shard_map/ppermute | solution.py:1053
  416.1 14.6 %collective-permute-start.38 = (bf16[2,1,1,384,384]{4,3,2,1,0:T(8,128)(2,1)}, bf16[2,1,1,384,384]{4,3,2,1,0:T(8,128)(2,1)}, u32[]{:S(2)}, u32[]{:S(2)}) collective-permute-start(bf16[2,1,1,384,384]{4,3,2,1,0:T(8,128)(2,1)} %dynamic-slice_convert_fusion.2), channel_id=1, source_target_pairs={{0,8},{8,0},{16,24},{24,16},{1,9},{9,1},{17,25},{25,17},{2,10},{10... | collective-permute-start | bytes 1769480 | tf_op jit(solution)/shard_map/ppermute | solution.py:1053
  433.4 23.8 %collective-permute-start.49 = (bf16[2,1,2,96,384]{4,3,2,1,0:T(8,128)(2,1)}, bf16[2,1,2,96,384]{4,3,2,1,0:T(8,128)(2,1)}, u32[]{:S(2)}, u32[]{:S(2)}) collective-permute-start(bf16[2,1,2,96,384]{4,3,2,1,0:T(8,128)(2,1)} %constant_dynamic-slice_fusion), channel_id=1, source_target_pairs={{0,8},{8,0},{16,24},{24,16},{1,9},{9,1},{17,25},{25,17},{2,10},{10... | collective-permute-start | bytes 884744 | tf_op jit(solution)/shard_map/ppermute | solution.py:1053
  436.9 55.4 %collective-permute-start.53 = (bf16[1,1,1,384,384]{4,3,2,1,0:T(8,128)(2,1)}, bf16[1,1,1,384,384]{4,3,2,1,0:T(8,128)(2,1)}, u32[]{:S(2)}, u32[]{:S(2)}) collective-permute-start(bf16[1,1,1,384,384]{4,3,2,1,0:T(8,128)(2,1)} %dynamic-slice_convert_fusion.4), channel_id=1, source_target_pairs={{0,16},{8,24},{16,0},{24,8},{1,17},{9,25},{17,1},{25,9},{2,18},{10... | collective-permute-start | bytes 884744 | tf_op jit(solution)/shard_map/ppermute | solution.py:1053
  443.8 25.8 %collective-permute-start.41 = (bf16[2,2,1,104,1152]{4,3,2,1,0:T(8,128)(2,1)S(1)}, bf16[2,2,1,104,1152]{4,3,2,1,0:T(8,128)(2,1)S(1)}, u32[]{:S(2)}, u32[]{:S(2)}) collective-permute-start(bf16[2,2,1,104,1152]{4,3,2,1,0:T(8,128)(2,1)S(1)} %fusion.38), channel_id=1, source_target_pairs={{0,4},{4,0},{1,5},{5,1},{2,6},{6,2},{3,7},{7,3},{8,12},{12,8},{9,1... | collective-permute-start | bytes 2875400 | tf_op jit(solution)/shard_map/ppermute | solution.py:1053
  451.4 17.2 %collective-permute-start.57 = (bf16[264,768]{1,0:T(8,128)(2,1)S(1)}, bf16[264,768]{1,0:T(8,128)(2,1)S(1)}, u32[]{:S(2)}, u32[]{:S(2)}) collective-permute-start(bf16[264,768]{1,0:T(8,128)(2,1)S(1)} %fusion.42), channel_id=1, source_target_pairs={{0,0},{1,16},{2,8},{3,24},{8,1},{9,17},{10,9},{11,25},{16,2},{17,1... | collective-permute-start | bytes 1216520 | tf_op jit(solution)/shard_map/ppermute | solution.py:1410
  456.8 36.5 %collective-permute-start.47 = (bf16[1,1,1,96,1536]{4,3,2,1,0:T(8,128)(2,1)S(1)}, bf16[1,1,1,96,1536]{4,3,2,1,0:T(8,128)(2,1)S(1)}, u32[]{:S(2)}, u32[]{:S(2)}) collective-permute-start(bf16[1,1,1,96,1536]{4,3,2,1,0:T(8,128)(2,1)S(1)} %dynamic-slice_convert_fusion.5), channel_id=1, source_target_pairs={{0,16},{8,24},{16,0},{24,8},{1,17},{9,25},{17,1},{25,9},{2,18},{10... | collective-permute-start | bytes 884744 | tf_op jit(solution)/shard_map/ppermute | solution.py:1053
  458.2 16.0 %collective-permute-start.51 = (bf16[2,1,1,96,384]{4,3,2,1,0:T(8,128)(2,1)S(1)}, bf16[2,1,1,96,384]{4,3,2,1,0:T(8,128)(2,1)S(1)}, u32[]{:S(2)}, u32[]{:S(2)}) collective-permute-start(bf16[2,1,1,96,384]{4,3,2,1,0:T(8,128)(2,1)S(1)} %dynamic-slice_convert_fusion.7), channel_id=1, source_target_pairs={{0,4},{4,0},{1,5},{5,1},{2,6},{6,2},{3,7},{7,3},{8,12},{12,8},{9,1... | collective-permute-start | bytes 442376 | tf_op jit(solution)/shard_map/ppermute | solution.py:1053
  469.9 22.4 %collective-permute-start.42 = (bf16[2,1,1,104,1152]{4,3,2,1,0:T(8,128)(2,1)S(1)}, bf16[2,1,1,104,1152]{4,3,2,1,0:T(8,128)(2,1)S(1)}, u32[]{:S(2)}, u32[]{:S(2)}) collective-permute-start(bf16[2,1,1,104,1152]{4,3,2,1,0:T(8,128)(2,1)S(1)} %dynamic-slice_convert_fusion.3), channel_id=1, source_target_pairs={{0,8},{8,0},{16,24},{24,16},{1,9},{9,1},{17,25},{25,17},{2,10},{10... | collective-permute-start | bytes 1437704 | tf_op jit(solution)/shard_map/ppermute | solution.py:1053
  (98 other events, 798.0 us)

commit v3 on v2

--- a/solution.py
+++ b/solution.py
@@ -637,6 +637,7 @@
 
 LANES = 128
 MARGIN = 16.0
+SEQUENCE_AT = (0, 2, 3, 1)
 VMEM_BYTES = 60 * 1024 * 1024
 
 
@@ -653,14 +654,16 @@
 
 def vocab_stats_kernel(
     scalars_ref,
-    student_low_ref,
-    student_high_ref,
-    teacher_low_ref,
-    teacher_high_ref,
+    mine_low_ref,
+    mine_high_ref,
+    far_low_ref,
+    far_high_ref,
     embed_ref,
     logit_student_ref,
     logit_teacher_ref,
     stats_ref,
+    student_ref,
+    teacher_ref,
     tile_max_s,
     tile_max_t,
     max_s,
@@ -671,20 +674,33 @@
     part_s,
     part_t,
     part_x,
+    low,
     *,
     tile,
     rows_block,
 ):
     step_index = pl.program_id(0)
     steps = pl.num_programs(0)
-    half_rows = student_low_ref.shape[1]
+    first = step_index == 0
+    half_rows = mine_low_ref.shape[0]
     rows = 2 * half_rows
+
+    def keep(student_parts, teacher_parts):
+        for kept, parts in ((student_ref, student_parts), (teacher_ref, teacher_parts)):
+            for place, part in enumerate(parts):
+                kept[place * half_rows : (place + 1) * half_rows, :] = part[...]
+
+    @pl.when((step_index == 0) & (scalars_ref[1] == 0))
+    def _():
+        keep((mine_low_ref, mine_high_ref), (far_low_ref, far_high_ref))
+
+    @pl.when((step_index == 0) & (scalars_ref[1] == 1))
+    def _():
+        keep((far_low_ref, far_high_ref), (mine_low_ref, mine_high_ref))
 
     @pl.when(step_index == 0)
     def _():
-        max_s[...] = jnp.full_like(max_s, -1e30)
-        max_t[...] = jnp.full_like(max_t, -1e30)
-        for total in (sum_s, sum_t, cross):
+        for total in (max_s, max_t, sum_s, sum_t, cross):
             total[...] = jnp.zeros_like(total)
 
     def sums(scaled_s, scaled_t, top_s, top_t):
@@ -703,11 +719,8 @@
         excess = None
         for start in range(0, rows, rows_block):
             here = pl.ds(start, rows_block)
-            source = pl.ds(start % half_rows, rows_block)
-            student_ref = student_low_ref if start < half_rows else student_high_ref
-            teacher_ref = teacher_low_ref if start < half_rows else teacher_high_ref
-            scaled_s = matmul_right_t(student_ref[0, source, :], embed_tile)
-            scaled_t = matmul_right_t(teacher_ref[0, source, :], embed_tile)
+            scaled_s = matmul_right_t(student_ref[here, :], embed_tile)
+            scaled_t = matmul_right_t(teacher_ref[here, :], embed_tile)
             if masked:
                 column = lax.broadcasted_iota(jnp.int32, (1, tile), 1) + step_index * tile
                 scaled_s = jnp.where(column < scalars_ref[0], scaled_s, -1e30)
@@ -726,19 +739,33 @@
             over = jnp.maximum(tops_s - old_s, tops_t - old_t)
             excess = over if excess is None else jnp.maximum(excess, over)
 
-        @pl.when(jnp.max(excess) > MARGIN)
+        low[0] = 0.0
+
+        @pl.when(first)
+        def _():
+            least_s = jnp.min(jnp.max(tile_max_s[...], axis=1, keepdims=True))
+            least_t = jnp.min(jnp.max(tile_max_t[...], axis=1, keepdims=True))
+            low[0] = -jnp.minimum(least_s, least_t)
+
+        @pl.when(jnp.maximum(jnp.max(excess), low[0]) > MARGIN)
         def _():
             def rescale(chunk, _):
                 here = pl.ds(pl.multiple_of(chunk * 64, 64), 64)
                 old_s = max_s[here, :]
                 old_t = max_t[here, :]
-                new_s = jnp.maximum(old_s, jnp.max(tile_max_s[here, :], axis=1, keepdims=True))
-                new_t = jnp.maximum(old_t, jnp.max(tile_max_t[here, :], axis=1, keepdims=True))
-                factor_t = jnp.exp(old_t - new_t)
+                top_s = jnp.max(tile_max_s[here, :], axis=1, keepdims=True)
+                top_t = jnp.max(tile_max_t[here, :], axis=1, keepdims=True)
+                new_s = jnp.broadcast_to(
+                    jnp.where(first, top_s, jnp.maximum(old_s[:, :1], top_s)), old_s.shape
+                )
+                new_t = jnp.broadcast_to(
+                    jnp.where(first, top_t, jnp.maximum(old_t[:, :1], top_t)), old_t.shape
+                )
+                factor_t = jnp.where(first, 0.0, jnp.exp(old_t - new_t))
                 moved = (old_t - old_s) - (new_t - new_s)
                 max_s[here, :] = new_s
                 max_t[here, :] = new_t
-                sum_s[here, :] = sum_s[here, :] * jnp.exp(old_s - new_s)
+                sum_s[here, :] = sum_s[here, :] * jnp.where(first, 0.0, jnp.exp(old_s - new_s))
                 cross[here, :] = (cross[here, :] + moved * sum_t[here, :]) * factor_t
                 sum_t[here, :] = sum_t[here, :] * factor_t
                 part_s[here, :], part_t[here, :], part_x[here, :] = sums(
@@ -771,34 +798,32 @@
 
 
 def vocab_stats(final_parts, is_teacher, embedding, valid_columns, tile=1280, rows_block=256):
-    _, half_rows, width = final_parts.shape
+    half_rows, width = final_parts[0].shape
     rows = 2 * half_rows
     steps = pl.cdiv(embedding.shape[0], tile)
     logits = jax.ShapeDtypeStruct((rows, steps * tile), jnp.float32)
-    part_spec = lambda teacher, second: pl.BlockSpec(
-        (1, half_rows, width),
-        lambda j, scalars: (2 * (scalars[1] ^ teacher) + second, 0, 0),
-    )
     return pl.pallas_call(
         functools.partial(vocab_stats_kernel, tile=tile, rows_block=rows_block),
         grid_spec=pltpu.PrefetchScalarGridSpec(
             num_scalar_prefetch=1,
             grid=(steps,),
-            in_specs=[part_spec(0, 0), part_spec(0, 1), part_spec(1, 0), part_spec(1, 1)]
+            in_specs=[whole_block((half_rows, width))] * 4
             + [pl.BlockSpec((tile, width), lambda j, *_: (j, 0))],
             out_specs=[
                 pl.BlockSpec((rows, tile), lambda j, *_: (0, j)),
                 pl.BlockSpec((rows, tile), lambda j, *_: (0, j)),
                 whole_block((8, rows)),
             ],
-            scratch_shapes=[pltpu.VMEM((rows, LANES), jnp.float32)] * 10,
+            scratch_shapes=[pltpu.VMEM((rows, width), jnp.bfloat16)] * 2
+            + [pltpu.VMEM((rows, LANES), jnp.float32)] * 10
+            + [pltpu.SMEM((1,), jnp.float32)],
         ),
         out_shape=[logits, logits, jax.ShapeDtypeStruct((8, rows), jnp.float32)],
         compiler_params=pltpu.CompilerParams(vmem_limit_bytes=VMEM_BYTES),
         name="vocab_stats",
     )(
         jnp.stack([valid_columns, is_teacher.astype(jnp.int32)]),
-        *[final_parts] * 4,
+        *final_parts,
         embedding,
     )
 
@@ -1226,8 +1251,8 @@
     front = exchange_models(front_slabs)
     back = exchange_models(after(back_slabs, front))
     length_parts = sum(
-        jnp.where(blk == source, front[source][shard_rows, LANES : LANES + 2], 0)
-        for source in range(size_vocab)
+        jnp.where(blk == place, front[source][shard_rows, LANES : LANES + 2], 0)
+        for place, source in enumerate(SEQUENCE_AT)
     ).astype(jnp.int32)
     seq_length = 32 * length_parts[0] + length_parts[1]
     front_block = jnp.concatenate(
@@ -1252,14 +1277,16 @@
     middle_held = double(((after(middle_block, front_held[0]),), ((0,),)), BLK, 1)
     reduce_held = double(((after(reduce_block, middle_held[0]),), ((0,),)), BLK, 1)
     turn = [
-        (a * size_vocab + b, b * size_vocab + a) for a in range(size_blk) for b in range(size_vocab)
+        (a * size_vocab + SEQUENCE_AT[b], b * size_vocab + a)
+        for a in range(size_blk)
+        for b in range(size_vocab)
     ]
+    front_held = double(front_held, BLK, 0)
     quarter = lax.ppermute(after(hidden[0], front_held[0]), crossing, turn)
     quarter_far = swap(quarter, VOCAB, 2)
     quarters = in_order(
         member, [quarter, swap(quarter, VOCAB, 1), quarter_far, swap(quarter_far, VOCAB, 1)]
     )
-    front_held = double(front_held, BLK, 0)
     front_held = double(held_after(front_held, middle_held[0]), BATCH, 0)
     middle_held = double(middle_held, BATCH, 0)
     reduce_held = double(reduce_held, BLK, 0)
@@ -1325,9 +1352,7 @@
     final_rows = (0.5 * layer_norm(block_out, gain_final, shift_final)).astype(jnp.bfloat16)
 
     final_far = swap(final_rows, VOCAB, 2)
-    final_parts = jnp.stack(
-        [final_rows, swap(final_rows, VOCAB, 1), final_far, swap(final_far, VOCAB, 1)]
-    )
+    final_parts = (final_rows, swap(final_rows, VOCAB, 1), final_far, swap(final_far, VOCAB, 1))
     vocab_local = embedding.shape[0]
     valid_columns = jnp.clip(VOCAB_REAL - member * vocab_local, 0, vocab_local)
     logit_student, logit_teacher, stats = vocab_stats(
@@ -1397,7 +1422,7 @@
     input_sum = jnp.where(is_teacher, grad_inputs[1], grad_inputs[0])
     input_sum += input_other.astype(jnp.float32)
     home = [
-        (a * size_vocab + 2 * m + h, (2 * h + m) * size_vocab + a)
+        (a * size_vocab + 2 * m + h, (2 * h + m) * size_vocab + SEQUENCE_AT[a])
         for a in range(size_blk)
         for m in (0, 1)
         for h in (0, 1)

time: 528 us -> 526 us (level)
  local copies, waits for them, and re-layouts: 33 us -> 43.2 us
  starting transfers between devices: 74.2 us -> 64.2 us
  waiting for transfers between devices: 157 us -> 151 us
    ppermute x56, waiting for transfers between devices: 148 us -> 126 us  [swap(): lax.ppermute(rows, axis, [(index, index ^ distance) for index in range(co...]
    ppermute x1, waiting for transfers between devices: 0.01 us -> 15.8 us  [shards_by_model(): quarter = lax.ppermute(after(hidden[0], front_held[0]), crossing, turn)]
    ppermute x56, starting transfers between devices: 62.2 us -> 55.9 us  [swap(): lax.ppermute(rows, axis, [(index, index ^ distance) for index in range(co...]
    concatenate x7, local copies, waits for them, and re-layouts: 0.72 us -> 6.46 us  [shards_by_model(): jnp.concatenate([v.reshape(shards_all, -1) for v in vector_parts], axis=1)]
    unnamed x175 -> x187, local copies, waits for them, and re-layouts: 10.4 us -> 10.6 us
  transfers between devices with their start and end apart: 58 -> 58, of which waited for: 31 -> 32; matrix products, arithmetic and copies ran while one was open for 13% -> 17% of each run, Pallas kernels for 8% -> 8%
where the time goes in v3:
time: 526 us; the launch traced here: 519 us
  Pallas kernels  156 us (30%)
  waiting for transfers between devices  151 us (29%)
  starting transfers between devices  64.2 us (12%)
  other arithmetic  51 us (10%)
  matrix products  48.5 us (9%)
  local copies, waits for them, and re-layouts  43.2 us (8%)
    ppermute x56, waiting for transfers between devices, swap(): lax.ppermute(rows, axis, [(index, index ^ distance) for index in range(co...  126 us
    pallas_call x1, Pallas kernels, vocab_stats(): pl.pallas_call(functools.partial(vocab_stats_kernel, tile=tile, rows_bloc...  59.8 us
    ppermute x56, starting transfers between devices, swap(): lax.ppermute(rows, axis, [(index, index ^ distance) for index in range(co...  55.9 us
    pallas_call x1, Pallas kernels, vocab_grads(): pl.pallas_call(functools.partial(vocab_grads_kernel, tile=tile, columns=c...  54 us
    pallas_call x1, Pallas kernels, attend_grads(): pl.pallas_call(functools.partial(attend_grads_kernel, block=block), grid_...  20.6 us
    dot_general x4, matrix products, matmul_plain(): return jnp.dot(left_side, right_side, preferred_element_type=jnp.float32)  17.4 us
    dot_general x4, matrix products, matmul_left_t(): lax.dot_general(left_side, right_side, (((0,), (0,)), ((), ())), preferre...  16 us
    ppermute x1, waiting for transfers between devices, shards_by_model(): quarter = lax.ppermute(after(hidden[0], front_held[0]), crossing, turn)  15.8 us
  transfers between devices with their start and end apart: 58, of which 32 were waited for; matrix products, arithmetic and copies ran while one was open for 17% of the time, Pallas kernels for 8%

profile of v3, /device:TPU:1, one launch (start us, length us, event | category | flops | bytes accessed | tf_op | source)
XLA Modules:
  0.0 518.8 jit_solution(17132589762175655732)
XLA Ops:
  18.6 4.3 collective-permute-done.9
  23.2 8.0 %collective-permute-done.3.refs_1_ = bf16[128,1152]{1,0:T(8,128)(2,1)S(1)} collective-permute-done((bf16[128,1152]{1,0:T(8,128)(2,1)S(1)}, bf16[128,1152]{1,0:T(8,128)(2,1)S(1)}, u32[]{:S(2)}, u32[]{:S(2)}) %collective-permute-start.3) | collective-permute-done | bytes 294944 | tf_op jit(solution)/shard_map/ppermute | solution.py:1078
  31.2 4.2 collective-permute-start.4
  35.5 13.6 %collective-permute-done.12.refs_1_ = bf16[96,1920]{1,0:T(8,128)(2,1)S(1)} collective-permute-done((bf16[96,1920]{1,0:T(8,128)(2,1)S(1)}, bf16[96,1920]{1,0:T(8,128)(2,1)S(1)}, u32[]{:S(2)}, u32[]{:S(2)}) %collective-permute-start.12) | collective-permute-done | bytes 368672 | tf_op jit(solution)/shard_map/ppermute | solution.py:1078
  50.7 8.2 %collective-permute-done.4.refs_2_ = bf16[256,1152]{1,0:T(8,128)(2,1)S(1)} collective-permute-done((bf16[256,1152]{1,0:T(8,128)(2,1)S(1)}, bf16[256,1152]{1,0:T(8,128)(2,1)S(1)}, u32[]{:S(2)}, u32[]{:S(2)}) %collective-permute-start.4) | collective-permute-done | bytes 589856 | tf_op jit(solution)/shard_map/ppermute | solution.py:1078
  67.7 15.8 %collective-permute-done.5 = bf16[256,768]{1,0:T(8,128)(2,1)} collective-permute-done((bf16[256,768]{1,0:T(8,128)(2,1)}, bf16[256,768]{1,0:T(8,128)(2,1)}, u32[]{:S(2)}, u32[]{:S(2)}) %collective-permute-start.5) | collective-permute-done | bytes 393248 | tf_op jit(solution)/shard_map/ppermute | solution.py:1285
  84.9 4.0 collective-permute-done.16.refs_2_
  90.8 7.2 %collective-permute-start.7 = (bf16[256,768]{1,0:T(8,128)(2,1)S(1)}, bf16[256,768]{1,0:T(8,128)(2,1)S(1)}, u32[]{:S(2)}, u32[]{:S(2)}) collective-permute-start(bf16[256,768]{1,0:T(8,128)(2,1)S(1)} %collective-permute-done.6), channel_id=1, source_target_pairs={{0,1},{1,0},{2,3},{3,2},{4,5},{5,4},{6,7},{7,6},{8,9},{9,8},{10,11... | collective-permute-start | bytes 1179656 | tf_op jit(solution)/shard_map/ppermute | solution.py:1078
  109.4 11.8 %attend.1 = bf16[1024,384]{1,0:T(8,128)(2,1)} custom-call(s32[1]{0:T(128)} %bitcast.43.length_ref, bf16[1024,1152]{1,0:T(8,128)(2,1)} %add_convert_fusion.query_ref.key_ref.value_ref, bf16[1024,1152]{1,0:T(8,128)(2,1)} %add_convert_fusion.query_ref.key_ref.value_ref, bf16[1024,1152]{1,0:T(8,128)(2,1)} %add_convert_fusion.query_ref.key_ref.value_ref), custom_call_target="tpu_custom_call" | custom-call | tf_op jit(solution)/shard_map/attend/pallas_call | solution.py:964
  146.7 10.2 %fusion.13 = (f32[1024,1536]{1,0:T(8,128)}, bf16[1024,1536]{1,0:T(8,128)(2,1)S(1)}) fusion(f32[1536]{0:T(1024)S(1)} %dynamic_slice.188, bf16[768,1536]{1,0:T(8,128)(2,1)S(1)} %copy-done.62, bf16[512,768]{1,0:T(8,128)(2,1)} %collective-permute-done.21, bf16[512,768]{1,0:T(8,128)(2,1)} %add_convert_fusion.1), kind=kOutput, calls=%fused_computation.16 | convolution fusion | flops 2458386432 | bytes 13375488 | tf_op jit(solution)/shard_map/dot_general | solution.py:33
  168.7 19.1 %collective-permute-done.25.far_low_ref = bf16[512,768]{1,0:T(8,128)(2,1)} collective-permute-done((bf16[512,768]{1,0:T(8,128)(2,1)}, bf16[512,768]{1,0:T(8,128)(2,1)}, u32[]{:S(2)}, u32[]{:S(2)}) %collective-permute-start.25) | collective-permute-done | bytes 786464 | tf_op jit(solution)/shard_map/ppermute | solution.py:1078
  191.0 59.8 %vocab_stats.1 = (f32[1024,12800]{1,0:T(8,128)}, f32[1024,12800]{1,0:T(8,128)}, f32[8,1024]{1,0:T(8,128)}) custom-call(s32[2]{0:T(128)} %pad_add_fusion.scalars_ref, bf16[512,768]{1,0:T(8,128)(2,1)} %multiply_convert_fusion.1.mine_low_ref, bf16[512,768]{1,0:T(8,128)(2,1)} %collective-permute-done.24.mine_high_ref, ...), custom_call_target="tpu_custom_call" | custom-call | tf_op jit(solution)/shard_map/vocab_stats/pallas_call | solution.py:805
  250.8 5.2 %collective-permute-start.27 = (f32[8,1024]{1,0:T(8,128)}, f32[8,1024]{1,0:T(8,128)S(1)}, u32[]{:S(2)}, u32[]{:S(2)}) collective-permute-start(f32[8,1024]{1,0:T(8,128)} %get-tuple-element.91.refs_0_), channel_id=1, source_target_pairs={{0,1},{1,0},{2,3},{3,2},{4,5},{5,4},{6,7},{7,6},{8,9},{9,8},{10,11... | collective-permute-start | bytes 98312 | tf_op jit(solution)/shard_map/ppermute | solution.py:1078
  260.7 54.0 %vocab_grads.1 = (f32[2,512,768]{2,1,0:T(8,128)}, bf16[2,512,768]{2,1,0:T(8,128)(2,1)}, f32[8,1024]{1,0:T(8,128)}) custom-call(f32[1024,12800]{1,0:T(8,128)} %get-tuple-element.89.logit_student_ref, f32[1024,12800]{1,0:T(8,128)} %get-tuple-element.90.logit_teacher_ref, bf16[12576,768]{1,0:T(8,128)(2,1)} %embed_ref.3, f32[8,1024]{1,0:T(8,128)} %get-tuple-element.91.refs_0_, ...), custom_call_target="tpu_custom_call" | custom-call | tf_op jit(solution)/shard_map/vocab_grads/pallas_call | solution.py:903
  321.9 17.8 %collective-permute-done.31 = bf16[512,768]{1,0:T(8,128)(2,1)S(1)} collective-permute-done((bf16[512,768]{1,0:T(8,128)(2,1)S(1)}, bf16[512,768]{1,0:T(8,128)(2,1)S(1)}, u32[]{:S(2)}, u32[]{:S(2)}) %collective-permute-start.31) | collective-permute-done | bytes 786464 | tf_op jit(solution)/shard_map/ppermute | solution.py:1078
  345.8 5.0 convolution_convert_fusion.1
  353.3 4.8 convert_reduce_fusion
  358.1 4.7 convolution_convert_fusion
  381.3 20.6 %attend_grads.1 = (bf16[1024,384]{1,0:T(8,128)(2,1)}, bf16[1024,384]{1,0:T(8,128)(2,1)}, bf16[1024,384]{1,0:T(8,128)(2,1)}) custom-call(s32[1]{0:T(128)} %bitcast.43.length_ref, bf16[1024,1152]{1,0:T(8,128)(2,1)} %add_convert_fusion.query_ref.key_ref.value_ref, bf16[1024,1152]{1,0:T(8,128)(2,1)} %add_convert_fusion.query_ref.key_ref.value_ref, ...), custom_call_target="tpu_custom_call" | custom-call | tf_op jit(solution)/shard_map/attend_grads/pallas_call | solution.py:1033
  450.0 5.2 collective-permute-start.57
  456.7 8.7 %collective-permute-done.57 = bf16[264,768]{1,0:T(8,128)(2,1)S(1)} collective-permute-done((bf16[264,768]{1,0:T(8,128)(2,1)S(1)}, bf16[264,768]{1,0:T(8,128)(2,1)S(1)}, u32[]{:S(2)}, u32[]{:S(2)}) %collective-permute-start.57) | collective-permute-done | bytes 405536 | tf_op jit(solution)/shard_map/ppermute | solution.py:1435
  470.4 5.5 %collective-permute-start.42 = (bf16[2,1,1,104,1152]{4,3,2,1,0:T(8,128)(2,1)S(1)}, bf16[2,1,1,104,1152]{4,3,2,1,0:T(8,128)(2,1)S(1)}, u32[]{:S(2)}, u32[]{:S(2)}) collective-permute-start(bf16[2,1,1,104,1152]{4,3,2,1,0:T(8,128)(2,1)S(1)} %dynamic-slice_convert_fusion.3), channel_id=1, source_target_pairs={{0,8},{8,0},{16,24},{24,16},{1,9},{9,1},{17,25},{25,17},{2,10},{10... | collective-permute-start | bytes 1437704 | tf_op jit(solution)/shard_map/ppermute | solution.py:1078
  476.6 9.5 %collective-permute-done.52 = bf16[1,1,1,96,384]{4,3,2,1,0:T(8,128)(2,1)S(1)} collective-permute-done((bf16[1,1,1,96,384]{4,3,2,1,0:T(8,128)(2,1)S(1)}, bf16[1,1,1,96,384]{4,3,2,1,0:T(8,128)(2,1)S(1)}, u32[]{:S(2)}, u32[]{:S(2)}) %collective-permute-start.52) | collective-permute-done | bytes 73760 | tf_op jit(solution)/shard_map/ppermute | solution.py:1078
  493.9 4.4 collective-permute-done.54
  (498 shorter events, 202.5 us)
Async XLA Ops:
  15.4 15.8 %collective-permute-start.3 = (bf16[128,1152]{1,0:T(8,128)(2,1)S(1)}, bf16[128,1152]{1,0:T(8,128)(2,1)S(1)}, u32[]{:S(2)}, u32[]{:S(2)}) collective-permute-start(bf16[128,1152]{1,0:T(8,128)(2,1)S(1)} %get-tuple-element.74.refs_0_), channel_id=1, source_target_pairs={{0,16},{8,24},{16,0},{24,8},{1,17},{9,25},{17,1},{25,9},{2,18},{10... | collective-permute-start | bytes 884744 | tf_op jit(solution)/shard_map/ppermute | solution.py:1078
  31.2 17.9 %collective-permute-start.12 = (bf16[96,1920]{1,0:T(8,128)(2,1)S(1)}, bf16[96,1920]{1,0:T(8,128)(2,1)S(1)}, u32[]{:S(2)}, u32[]{:S(2)}) collective-permute-start(bf16[96,1920]{1,0:T(8,128)(2,1)S(1)} %constant_dynamic-update-slice_fusion.41.refs_0_), channel_id=1, source_target_pairs={{0,16},{8,24},{16,0},{24,8},{1,17},{9,25},{17,1},{25,9},{2,18},{10... | collective-permute-start | bytes 1105928 | tf_op jit(solution)/shard_map/ppermute | solution.py:1078
  31.2 27.7 %collective-permute-start.4 = (bf16[256,1152]{1,0:T(8,128)(2,1)S(1)}, bf16[256,1152]{1,0:T(8,128)(2,1)S(1)}, u32[]{:S(2)}, u32[]{:S(2)}) collective-permute-start(bf16[256,1152]{1,0:T(8,128)(2,1)S(1)} %constant_dynamic-update-slice_fusion.8), channel_id=1, source_target_pairs={{0,8},{8,0},{16,24},{24,16},{1,9},{9,1},{17,25},{25,17},{2,10},{10... | collective-permute-start | bytes 1769480 | tf_op jit(solution)/shard_map/ppermute | solution.py:1078
  49.1 15.8 %collective-permute-start.15 = (bf16[384,384]{1,0:T(8,128)(2,1)S(1)}, bf16[384,384]{1,0:T(8,128)(2,1)S(1)}, u32[]{:S(2)}, u32[]{:S(2)}) collective-permute-start(bf16[384,384]{1,0:T(8,128)(2,1)S(1)} %pad_maximum_fusion.14.refs_0_), channel_id=1, source_target_pairs={{0,16},{8,24},{16,0},{24,8},{1,17},{9,25},{17,1},{25,9},{2,18},{10... | collective-permute-start | bytes 884744 | tf_op jit(solution)/shard_map/ppermute | solution.py:1078
  50.1 33.5 %collective-permute-start.14 = (bf16[192,1920]{1,0:T(8,128)(2,1)}, bf16[192,1920]{1,0:T(8,128)(2,1)S(1)}, u32[]{:S(2)}, u32[]{:S(2)}) collective-permute-start(bf16[192,1920]{1,0:T(8,128)(2,1)} %pad_maximum_fusion.9), channel_id=1, source_target_pairs={{0,4},{4,0},{1,5},{5,1},{2,6},{6,2},{3,7},{7,3},{8,12},{12,8},{9,1... | collective-permute-start | bytes 2211848 | tf_op jit(solution)/shard_map/ppermute | solution.py:1078
  60.2 37.7 %collective-permute-start.13 = (bf16[512,1152]{1,0:T(8,128)(2,1)}, bf16[512,1152]{1,0:T(8,128)(2,1)}, u32[]{:S(2)}, u32[]{:S(2)}) collective-permute-start(bf16[512,1152]{1,0:T(8,128)(2,1)} %pad_maximum_fusion.5), channel_id=1, source_target_pairs={{0,4},{4,0},{1,5},{5,1},{2,6},{6,2},{3,7},{7,3},{8,12},{12,8},{9,1... | collective-permute-start | bytes 3538952 | tf_op jit(solution)/shard_map/ppermute | solution.py:1078
  61.8 21.8 %collective-permute-start.5 = (bf16[256,768]{1,0:T(8,128)(2,1)}, bf16[256,768]{1,0:T(8,128)(2,1)}, u32[]{:S(2)}, u32[]{:S(2)}) collective-permute-start(bf16[256,768]{1,0:T(8,128)(2,1)} %bitcast.375), channel_id=1, source_target_pairs={{0,0},{2,8},{3,16},{1,24},{8,1},{10,9},{11,17},{9,25},{16,2},{18,1... | collective-permute-start | bytes 1179656 | tf_op jit(solution)/shard_map/ppermute | solution.py:1285
  65.0 23.9 %collective-permute-start.16 = (bf16[768,384]{1,0:T(8,128)(2,1)S(1)}, bf16[768,384]{1,0:T(8,128)(2,1)S(1)}, u32[]{:S(2)}, u32[]{:S(2)}) collective-permute-start(bf16[768,384]{1,0:T(8,128)(2,1)S(1)} %pad_maximum_fusion.12), channel_id=1, source_target_pairs={{0,8},{8,0},{16,24},{24,16},{1,9},{9,1},{17,25},{25,17},{2,10},{10... | collective-permute-start | bytes 1769480 | tf_op jit(solution)/shard_map/ppermute | solution.py:1078
  83.5 18.5 %collective-permute-start.8 = (bf16[256,768]{1,0:T(8,128)(2,1)}, bf16[256,768]{1,0:T(8,128)(2,1)S(1)}, u32[]{:S(2)}, u32[]{:S(2)}) collective-permute-start(bf16[256,768]{1,0:T(8,128)(2,1)} %collective-permute-done.5), channel_id=1, source_target_pairs={{0,1},{1,0},{2,3},{3,2},{4,5},{5,4},{6,7},{7,6},{8,9},{9,8},{10,11... | collective-permute-start | bytes 1179656 | tf_op jit(solution)/shard_map/ppermute | solution.py:1078
  84.9 36.2 %collective-permute-start.17 = (bf16[384,1920]{1,0:T(8,128)(2,1)}, bf16[384,1920]{1,0:T(8,128)(2,1)}, u32[]{:S(2)}, u32[]{:S(2)}) collective-permute-start(bf16[384,1920]{1,0:T(8,128)(2,1)} %pad_maximum_fusion.4), channel_id=1, source_target_pairs={{0,8},{8,0},{16,24},{24,16},{1,9},{9,1},{17,25},{25,17},{2,10},{10... | collective-permute-start | bytes 4423688 | tf_op jit(solution)/shard_map/ppermute | solution.py:1078
  90.1 39.2 %collective-permute-start.18 = (bf16[1536,384]{1,0:T(8,128)(2,1)}, bf16[1536,384]{1,0:T(8,128)(2,1)}, u32[]{:S(2)}, u32[]{:S(2)}) collective-permute-start(bf16[1536,384]{1,0:T(8,128)(2,1)} %pad_maximum_fusion.6), channel_id=1, source_target_pairs={{0,4},{4,0},{1,5},{5,1},{2,6},{6,2},{3,7},{7,3},{8,12},{12,8},{9,1... | collective-permute-start | bytes 3538952 | tf_op jit(solution)/shard_map/ppermute | solution.py:1078
  168.5 19.3 %collective-permute-start.25 = (bf16[512,768]{1,0:T(8,128)(2,1)}, bf16[512,768]{1,0:T(8,128)(2,1)}, u32[]{:S(2)}, u32[]{:S(2)}) collective-permute-start(bf16[512,768]{1,0:T(8,128)(2,1)} %multiply_convert_fusion.1.mine_low_ref), channel_id=1, source_target_pairs={{0,2},{1,3},{2,0},{3,1},{4,6},{5,7},{6,4},{7,5},{8,10},{9,11},{10,... | collective-permute-start | bytes 2359304 | tf_op jit(solution)/shard_map/ppermute | solution.py:1078
  168.5 20.9 %collective-permute-start.24 = (bf16[512,768]{1,0:T(8,128)(2,1)}, bf16[512,768]{1,0:T(8,128)(2,1)}, u32[]{:S(2)}, u32[]{:S(2)}) collective-permute-start(bf16[512,768]{1,0:T(8,128)(2,1)} %multiply_convert_fusion.1.mine_low_ref), channel_id=1, source_target_pairs={{0,1},{1,0},{2,3},{3,2},{4,5},{5,4},{6,7},{7,6},{8,9},{9,8},{10,11... | collective-permute-start | bytes 2359304 | tf_op jit(solution)/shard_map/ppermute | solution.py:1078
  320.8 18.8 %collective-permute-start.31 = (bf16[512,768]{1,0:T(8,128)(2,1)S(1)}, bf16[512,768]{1,0:T(8,128)(2,1)S(1)}, u32[]{:S(2)}, u32[]{:S(2)}) collective-permute-start(bf16[512,768]{1,0:T(8,128)(2,1)S(1)} %fusion.41), channel_id=1, source_target_pairs={{0,2},{1,3},{2,0},{3,1},{4,6},{5,7},{6,4},{7,5},{8,10},{9,11},{10,... | collective-permute-start | bytes 2359304 | tf_op jit(solution)/shard_map/ppermute | solution.py:1078
  367.0 35.0 %collective-permute-start.37 = (bf16[2,1,2,96,1536]{4,3,2,1,0:T(8,128)(2,1)}, bf16[2,1,2,96,1536]{4,3,2,1,0:T(8,128)(2,1)}, u32[]{:S(2)}, u32[]{:S(2)}) collective-permute-start(bf16[2,1,2,96,1536]{4,3,2,1,0:T(8,128)(2,1)} %constant_dynamic-slice_fusion.4), channel_id=1, source_target_pairs={{0,8},{8,0},{16,24},{24,16},{1,9},{9,1},{17,25},{25,17},{2,10},{10... | collective-permute-start | bytes 3538952 | tf_op jit(solution)/shard_map/ppermute | solution.py:1078
  368.9 33.1 %collective-permute-start.36 = (bf16[2,2,1,384,384]{4,3,2,1,0:T(8,128)(2,1)}, bf16[2,2,1,384,384]{4,3,2,1,0:T(8,128)(2,1)}, u32[]{:S(2)}, u32[]{:S(2)}) collective-permute-start(bf16[2,2,1,384,384]{4,3,2,1,0:T(8,128)(2,1)} %constant_dynamic-slice_fusion.5), channel_id=1, source_target_pairs={{0,4},{4,0},{1,5},{5,1},{2,6},{6,2},{3,7},{7,3},{8,12},{12,8},{9,1... | collective-permute-start | bytes 3538952 | tf_op jit(solution)/shard_map/ppermute | solution.py:1078
  415.4 15.3 %collective-permute-start.38 = (bf16[2,1,1,384,384]{4,3,2,1,0:T(8,128)(2,1)S(1)}, bf16[2,1,1,384,384]{4,3,2,1,0:T(8,128)(2,1)}, u32[]{:S(2)}, u32[]{:S(2)}) collective-permute-start(bf16[2,1,1,384,384]{4,3,2,1,0:T(8,128)(2,1)S(1)} %dynamic-slice_convert_fusion.2), channel_id=1, source_target_pairs={{0,8},{8,0},{16,24},{24,16},{1,9},{9,1},{17,25},{25,17},{2,10},{10... | collective-permute-start | bytes 1769480 | tf_op jit(solution)/shard_map/ppermute | solution.py:1078
  433.3 22.0 %collective-permute-start.49 = (bf16[2,1,2,96,384]{4,3,2,1,0:T(8,128)(2,1)}, bf16[2,1,2,96,384]{4,3,2,1,0:T(8,128)(2,1)}, u32[]{:S(2)}, u32[]{:S(2)}) collective-permute-start(bf16[2,1,2,96,384]{4,3,2,1,0:T(8,128)(2,1)} %constant_dynamic-slice_fusion), channel_id=1, source_target_pairs={{0,8},{8,0},{16,24},{24,16},{1,9},{9,1},{17,25},{25,17},{2,10},{10... | collective-permute-start | bytes 884744 | tf_op jit(solution)/shard_map/ppermute | solution.py:1078
  436.8 53.1 %collective-permute-start.53 = (bf16[1,1,1,384,384]{4,3,2,1,0:T(8,128)(2,1)}, bf16[1,1,1,384,384]{4,3,2,1,0:T(8,128)(2,1)}, u32[]{:S(2)}, u32[]{:S(2)}) collective-permute-start(bf16[1,1,1,384,384]{4,3,2,1,0:T(8,128)(2,1)} %dynamic-slice_convert_fusion.4), channel_id=1, source_target_pairs={{0,16},{8,24},{16,0},{24,8},{1,17},{9,25},{17,1},{25,9},{2,18},{10... | collective-permute-start | bytes 884744 | tf_op jit(solution)/shard_map/ppermute | solution.py:1078
  447.9 22.3 %collective-permute-start.41 = (bf16[2,2,1,104,1152]{4,3,2,1,0:T(8,128)(2,1)S(1)}, bf16[2,2,1,104,1152]{4,3,2,1,0:T(8,128)(2,1)S(1)}, u32[]{:S(2)}, u32[]{:S(2)}) collective-permute-start(bf16[2,2,1,104,1152]{4,3,2,1,0:T(8,128)(2,1)S(1)} %fusion.38), channel_id=1, source_target_pairs={{0,4},{4,0},{1,5},{5,1},{2,6},{6,2},{3,7},{7,3},{8,12},{12,8},{9,1... | collective-permute-start | bytes 2875400 | tf_op jit(solution)/shard_map/ppermute | solution.py:1078
  450.0 15.4 %collective-permute-start.57 = (bf16[264,768]{1,0:T(8,128)(2,1)S(1)}, bf16[264,768]{1,0:T(8,128)(2,1)S(1)}, u32[]{:S(2)}, u32[]{:S(2)}) collective-permute-start(bf16[264,768]{1,0:T(8,128)(2,1)S(1)} %fusion.42), channel_id=1, source_target_pairs={{0,0},{1,16},{2,8},{3,24},{8,2},{9,18},{10,10},{11,26},{16,3},{17,... | collective-permute-start | bytes 1216520 | tf_op jit(solution)/shard_map/ppermute | solution.py:1435
  455.2 35.7 %collective-permute-start.47 = (bf16[1,1,1,96,1536]{4,3,2,1,0:T(8,128)(2,1)S(1)}, bf16[1,1,1,96,1536]{4,3,2,1,0:T(8,128)(2,1)S(1)}, u32[]{:S(2)}, u32[]{:S(2)}) collective-permute-start(bf16[1,1,1,96,1536]{4,3,2,1,0:T(8,128)(2,1)S(1)} %dynamic-slice_convert_fusion.5), channel_id=1, source_target_pairs={{0,16},{8,24},{16,0},{24,8},{1,17},{9,25},{17,1},{25,9},{2,18},{10... | collective-permute-start | bytes 884744 | tf_op jit(solution)/shard_map/ppermute | solution.py:1078
  456.4 19.5 %collective-permute-start.51 = (bf16[2,1,1,96,384]{4,3,2,1,0:T(8,128)(2,1)S(1)}, bf16[2,1,1,96,384]{4,3,2,1,0:T(8,128)(2,1)S(1)}, u32[]{:S(2)}, u32[]{:S(2)}) collective-permute-start(bf16[2,1,1,96,384]{4,3,2,1,0:T(8,128)(2,1)S(1)} %dynamic-slice_convert_fusion.7), channel_id=1, source_target_pairs={{0,4},{4,0},{1,5},{5,1},{2,6},{6,2},{3,7},{7,3},{8,12},{12,8},{9,1... | collective-permute-start | bytes 442376 | tf_op jit(solution)/shard_map/ppermute | solution.py:1078
  470.4 19.5 %collective-permute-start.42 = (bf16[2,1,1,104,1152]{4,3,2,1,0:T(8,128)(2,1)S(1)}, bf16[2,1,1,104,1152]{4,3,2,1,0:T(8,128)(2,1)S(1)}, u32[]{:S(2)}, u32[]{:S(2)}) collective-permute-start(bf16[2,1,1,104,1152]{4,3,2,1,0:T(8,128)(2,1)S(1)} %dynamic-slice_convert_fusion.3), channel_id=1, source_target_pairs={{0,8},{8,0},{16,24},{24,16},{1,9},{9,1},{17,25},{25,17},{2,10},{10... | collective-permute-start | bytes 1437704 | tf_op jit(solution)/shard_map/ppermute | solution.py:1078
  (104 other events, 759.5 us)

commit v4 on v3

--- a/solution.py
+++ b/solution.py
@@ -1339,7 +1339,9 @@
     normed_two = jnp.concatenate([normed_own, swap(normed_own, VOCAB, 1)], axis=0)
     inner_rows = matmul_plain(normed_two, expand_weight) + expand_bias
     active = gelu_tanh(inner_rows).astype(jnp.bfloat16)
-    active, slope = lax.optimization_barrier((active, gelu_slope(inner_rows)))
+    active, slope = lax.optimization_barrier(
+        (active, gelu_slope(inner_rows).astype(jnp.bfloat16))
+    )
     (reduce_columns,) = place_blocks(reduce_held, plane, ((0, reduce_rows, 0, part),))
     reduce_weight = in_pair(
         is_second,
@@ -1383,7 +1385,7 @@
     grid = (2, 2, 2)
     grad_reduce = grad_reduce.reshape(grid + (reduce_rows, part))
     grad_active = matmul_right_t(branch_low, reduce_weight)
-    inner_grad = (grad_active * slope).astype(jnp.bfloat16)
+    inner_grad = (grad_active * slope.astype(jnp.float32)).astype(jnp.bfloat16)
     grad_normed = matmul_right_t(after(inner_grad, reduce_other), expand_weight)
     grad_normed_own = grad_normed[:own_rows] + swap_low(grad_normed[own_rows:])
     middle_part, grad_second_gain, grad_second_shift = norm_back(

time: 526 us -> 525 us (level)
    unnamed x187 -> x189, local copies, waits for them, and re-layouts: 10.6 us -> 11.3 us
  transfers between devices with their start and end apart: 58 -> 58, of which waited for: 32 -> 32; matrix products, arithmetic and copies ran while one was open for 17% -> 16% of each run, Pallas kernels for 8% -> 8%
where the time goes in v4:
time: 525 us; the launch traced here: 517 us
  Pallas kernels  161 us (31%)
  waiting for transfers between devices  150 us (29%)
  starting transfers between devices  60.3 us (11%)
  other arithmetic  50.9 us (10%)
  matrix products  46.2 us (9%)
  local copies, waits for them, and re-layouts  43.7 us (8%)
    ppermute x56, waiting for transfers between devices, swap(): lax.ppermute(rows, axis, [(index, index ^ distance) for index in range(co...  126 us
    pallas_call x1, Pallas kernels, vocab_stats(): pl.pallas_call(functools.partial(vocab_stats_kernel, tile=tile, rows_bloc...  64.5 us
    pallas_call x1, Pallas kernels, vocab_grads(): pl.pallas_call(functools.partial(vocab_grads_kernel, tile=tile, columns=c...  53.8 us
    ppermute x56, starting transfers between devices, swap(): lax.ppermute(rows, axis, [(index, index ^ distance) for index in range(co...  52 us
    pallas_call x1, Pallas kernels, attend_grads(): pl.pallas_call(functools.partial(attend_grads_kernel, block=block), grid_...  20.6 us
    dot_general x4, matrix products, matmul_plain(): return jnp.dot(left_side, right_side, preferred_element_type=jnp.float32)  17.1 us
    dot_general x4, matrix products, matmul_left_t(): lax.dot_general(left_side, right_side, (((0,), (0,)), ((), ())), preferre...  15.9 us
    ppermute x1, waiting for transfers between devices, shards_by_model(): quarter = lax.ppermute(after(hidden[0], front_held[0]), crossing, turn)  15.8 us
  transfers between devices with their start and end apart: 58, of which 32 were waited for; matrix products, arithmetic and copies ran while one was open for 16% of the time, Pallas kernels for 8%

profile of v4, /device:TPU:1, one launch (start us, length us, event | category | flops | bytes accessed | tf_op | source)
XLA Modules:
  0.0 516.9 jit_solution(110924880969530609)
XLA Ops:
  18.6 4.3 collective-permute-done.9
  23.2 8.0 %collective-permute-done.3.refs_1_ = bf16[128,1152]{1,0:T(8,128)(2,1)S(1)} collective-permute-done((bf16[128,1152]{1,0:T(8,128)(2,1)S(1)}, bf16[128,1152]{1,0:T(8,128)(2,1)S(1)}, u32[]{:S(2)}, u32[]{:S(2)}) %collective-permute-start.3) | collective-permute-done | bytes 294944 | tf_op jit(solution)/shard_map/ppermute | solution.py:1078
  31.2 4.2 collective-permute-start.4
  35.5 13.6 %collective-permute-done.12.refs_1_ = bf16[96,1920]{1,0:T(8,128)(2,1)S(1)} collective-permute-done((bf16[96,1920]{1,0:T(8,128)(2,1)S(1)}, bf16[96,1920]{1,0:T(8,128)(2,1)S(1)}, u32[]{:S(2)}, u32[]{:S(2)}) %collective-permute-start.12) | collective-permute-done | bytes 368672 | tf_op jit(solution)/shard_map/ppermute | solution.py:1078
  50.7 8.2 %collective-permute-done.4.refs_2_ = bf16[256,1152]{1,0:T(8,128)(2,1)S(1)} collective-permute-done((bf16[256,1152]{1,0:T(8,128)(2,1)S(1)}, bf16[256,1152]{1,0:T(8,128)(2,1)S(1)}, u32[]{:S(2)}, u32[]{:S(2)}) %collective-permute-start.4) | collective-permute-done | bytes 589856 | tf_op jit(solution)/shard_map/ppermute | solution.py:1078
  67.7 15.8 %collective-permute-done.5 = bf16[256,768]{1,0:T(8,128)(2,1)} collective-permute-done((bf16[256,768]{1,0:T(8,128)(2,1)}, bf16[256,768]{1,0:T(8,128)(2,1)}, u32[]{:S(2)}, u32[]{:S(2)}) %collective-permute-start.5) | collective-permute-done | bytes 393248 | tf_op jit(solution)/shard_map/ppermute | solution.py:1285
  84.9 4.0 collective-permute-done.16.refs_2_
  90.7 7.2 %collective-permute-start.7 = (bf16[256,768]{1,0:T(8,128)(2,1)S(1)}, bf16[256,768]{1,0:T(8,128)(2,1)S(1)}, u32[]{:S(2)}, u32[]{:S(2)}) collective-permute-start(bf16[256,768]{1,0:T(8,128)(2,1)S(1)} %collective-permute-done.6), channel_id=1, source_target_pairs={{0,1},{1,0},{2,3},{3,2},{4,5},{5,4},{6,7},{7,6},{8,9},{9,8},{10,11... | collective-permute-start | bytes 1179656 | tf_op jit(solution)/shard_map/ppermute | solution.py:1078
  109.3 11.8 %attend.1 = bf16[1024,384]{1,0:T(8,128)(2,1)} custom-call(s32[1]{0:T(128)} %bitcast.43.length_ref, bf16[1024,1152]{1,0:T(8,128)(2,1)} %add_convert_fusion.query_ref.key_ref.value_ref, bf16[1024,1152]{1,0:T(8,128)(2,1)} %add_convert_fusion.query_ref.key_ref.value_ref, bf16[1024,1152]{1,0:T(8,128)(2,1)} %add_convert_fusion.query_ref.key_ref.value_ref), custom_call_target="tpu_custom_call" | custom-call | tf_op jit(solution)/shard_map/attend/pallas_call | solution.py:964
  146.6 9.8 %fusion.14 = (bf16[1024,1536]{1,0:T(8,128)(2,1)}, bf16[1024,1536]{1,0:T(8,128)(2,1)S(1)}) fusion(f32[1536]{0:T(1024)S(1)} %dynamic_slice.188, bf16[768,1536]{1,0:T(8,128)(2,1)S(1)} %copy-done.62, bf16[512,768]{1,0:T(8,128)(2,1)} %collective-permute-done.21, bf16[512,768]{1,0:T(8,128)(2,1)} %add_convert_fusion.1), kind=kOutput, calls=%fused_computation.17 | convolution fusion | flops 2459959296 | bytes 10229760 | tf_op jit(solution)/shard_map/dot_general | solution.py:33
  168.2 19.1 %collective-permute-done.25.far_low_ref = bf16[512,768]{1,0:T(8,128)(2,1)} collective-permute-done((bf16[512,768]{1,0:T(8,128)(2,1)}, bf16[512,768]{1,0:T(8,128)(2,1)}, u32[]{:S(2)}, u32[]{:S(2)}) %collective-permute-start.25) | collective-permute-done | bytes 786464 | tf_op jit(solution)/shard_map/ppermute | solution.py:1078
  190.5 64.5 %vocab_stats.1 = (f32[1024,12800]{1,0:T(8,128)}, f32[1024,12800]{1,0:T(8,128)}, f32[8,1024]{1,0:T(8,128)}) custom-call(s32[2]{0:T(128)} %pad_add_fusion.scalars_ref, bf16[512,768]{1,0:T(8,128)(2,1)} %multiply_convert_fusion.1.mine_low_ref, bf16[512,768]{1,0:T(8,128)(2,1)} %collective-permute-done.24.mine_high_ref, ...), custom_call_target="tpu_custom_call" | custom-call | tf_op jit(solution)/shard_map/vocab_stats/pallas_call | solution.py:805
  260.0 53.8 %vocab_grads.1 = (f32[2,512,768]{2,1,0:T(8,128)}, bf16[2,512,768]{2,1,0:T(8,128)(2,1)}, f32[8,1024]{1,0:T(8,128)}) custom-call(f32[1024,12800]{1,0:T(8,128)} %get-tuple-element.89.logit_student_ref, f32[1024,12800]{1,0:T(8,128)} %get-tuple-element.90.logit_teacher_ref, bf16[12576,768]{1,0:T(8,128)(2,1)} %embed_ref.3, f32[8,1024]{1,0:T(8,128)} %get-tuple-element.91.refs_0_, ...), custom_call_target="tpu_custom_call" | custom-call | tf_op jit(solution)/shard_map/vocab_grads/pallas_call | solution.py:903
  321.4 17.3 %collective-permute-done.31 = bf16[512,768]{1,0:T(8,128)(2,1)S(1)} collective-permute-done((bf16[512,768]{1,0:T(8,128)(2,1)S(1)}, bf16[512,768]{1,0:T(8,128)(2,1)S(1)}, u32[]{:S(2)}, u32[]{:S(2)}) %collective-permute-start.31) | collective-permute-done | bytes 786464 | tf_op jit(solution)/shard_map/ppermute | solution.py:1078
  344.9 5.0 convolution_convert_fusion.1
  356.0 4.7 convolution_convert_fusion
  379.1 20.6 %attend_grads.1 = (bf16[1024,384]{1,0:T(8,128)(2,1)}, bf16[1024,384]{1,0:T(8,128)(2,1)}, bf16[1024,384]{1,0:T(8,128)(2,1)}) custom-call(s32[1]{0:T(128)} %bitcast.43.length_ref, bf16[1024,1152]{1,0:T(8,128)(2,1)} %add_convert_fusion.query_ref.key_ref.value_ref, bf16[1024,1152]{1,0:T(8,128)(2,1)} %add_convert_fusion.query_ref.key_ref.value_ref, ...), custom_call_target="tpu_custom_call" | custom-call | tf_op jit(solution)/shard_map/attend_grads/pallas_call | solution.py:1033
  407.6 3.9 fusion.97
  447.8 5.2 %collective-permute-start.57 = (bf16[264,768]{1,0:T(8,128)(2,1)S(1)}, bf16[264,768]{1,0:T(8,128)(2,1)S(1)}, u32[]{:S(2)}, u32[]{:S(2)}) collective-permute-start(bf16[264,768]{1,0:T(8,128)(2,1)S(1)} %fusion.43), channel_id=1, source_target_pairs={{0,0},{1,16},{2,8},{3,24},{8,2},{9,18},{10,10},{11,26},{16,3},{17,... | collective-permute-start | bytes 1216520 | tf_op jit(solution)/shard_map/ppermute | solution.py:1437
  454.6 8.6 %collective-permute-done.57 = bf16[264,768]{1,0:T(8,128)(2,1)S(1)} collective-permute-done((bf16[264,768]{1,0:T(8,128)(2,1)S(1)}, bf16[264,768]{1,0:T(8,128)(2,1)S(1)}, u32[]{:S(2)}, u32[]{:S(2)}) %collective-permute-start.57) | collective-permute-done | bytes 405536 | tf_op jit(solution)/shard_map/ppermute | solution.py:1437
  464.2 4.2 collective-permute-done.41
  468.6 5.2 %collective-permute-start.42 = (bf16[2,1,1,104,1152]{4,3,2,1,0:T(8,128)(2,1)S(1)}, bf16[2,1,1,104,1152]{4,3,2,1,0:T(8,128)(2,1)S(1)}, u32[]{:S(2)}, u32[]{:S(2)}) collective-permute-start(bf16[2,1,1,104,1152]{4,3,2,1,0:T(8,128)(2,1)S(1)} %dynamic-slice_convert_fusion.3), channel_id=1, source_target_pairs={{0,8},{8,0},{16,24},{24,16},{1,9},{9,1},{17,25},{25,17},{2,10},{10... | collective-permute-start | bytes 1437704 | tf_op jit(solution)/shard_map/ppermute | solution.py:1078
  474.6 9.8 %collective-permute-done.52 = bf16[1,1,1,96,384]{4,3,2,1,0:T(8,128)(2,1)S(1)} collective-permute-done((bf16[1,1,1,96,384]{4,3,2,1,0:T(8,128)(2,1)S(1)}, bf16[1,1,1,96,384]{4,3,2,1,0:T(8,128)(2,1)S(1)}, u32[]{:S(2)}, u32[]{:S(2)}) %collective-permute-start.52) | collective-permute-done | bytes 73760 | tf_op jit(solution)/shard_map/ppermute | solution.py:1078
  492.0 4.4 collective-permute-done.54
  (500 shorter events, 198.9 us)
Async XLA Ops:
  15.4 15.8 %collective-permute-start.3 = (bf16[128,1152]{1,0:T(8,128)(2,1)S(1)}, bf16[128,1152]{1,0:T(8,128)(2,1)S(1)}, u32[]{:S(2)}, u32[]{:S(2)}) collective-permute-start(bf16[128,1152]{1,0:T(8,128)(2,1)S(1)} %get-tuple-element.74.refs_0_), channel_id=1, source_target_pairs={{0,16},{8,24},{16,0},{24,8},{1,17},{9,25},{17,1},{25,9},{2,18},{10... | collective-permute-start | bytes 884744 | tf_op jit(solution)/shard_map/ppermute | solution.py:1078
  31.2 17.9 %collective-permute-start.12 = (bf16[96,1920]{1,0:T(8,128)(2,1)S(1)}, bf16[96,1920]{1,0:T(8,128)(2,1)S(1)}, u32[]{:S(2)}, u32[]{:S(2)}) collective-permute-start(bf16[96,1920]{1,0:T(8,128)(2,1)S(1)} %constant_dynamic-update-slice_fusion.41.refs_0_), channel_id=1, source_target_pairs={{0,16},{8,24},{16,0},{24,8},{1,17},{9,25},{17,1},{25,9},{2,18},{10... | collective-permute-start | bytes 1105928 | tf_op jit(solution)/shard_map/ppermute | solution.py:1078
  31.2 27.7 %collective-permute-start.4 = (bf16[256,1152]{1,0:T(8,128)(2,1)S(1)}, bf16[256,1152]{1,0:T(8,128)(2,1)S(1)}, u32[]{:S(2)}, u32[]{:S(2)}) collective-permute-start(bf16[256,1152]{1,0:T(8,128)(2,1)S(1)} %constant_dynamic-update-slice_fusion.8), channel_id=1, source_target_pairs={{0,8},{8,0},{16,24},{24,16},{1,9},{9,1},{17,25},{25,17},{2,10},{10... | collective-permute-start | bytes 1769480 | tf_op jit(solution)/shard_map/ppermute | solution.py:1078
  49.1 15.8 %collective-permute-start.15 = (bf16[384,384]{1,0:T(8,128)(2,1)S(1)}, bf16[384,384]{1,0:T(8,128)(2,1)S(1)}, u32[]{:S(2)}, u32[]{:S(2)}) collective-permute-start(bf16[384,384]{1,0:T(8,128)(2,1)S(1)} %pad_maximum_fusion.14.refs_0_), channel_id=1, source_target_pairs={{0,16},{8,24},{16,0},{24,8},{1,17},{9,25},{17,1},{25,9},{2,18},{10... | collective-permute-start | bytes 884744 | tf_op jit(solution)/shard_map/ppermute | solution.py:1078
  50.1 33.4 %collective-permute-start.14 = (bf16[192,1920]{1,0:T(8,128)(2,1)}, bf16[192,1920]{1,0:T(8,128)(2,1)S(1)}, u32[]{:S(2)}, u32[]{:S(2)}) collective-permute-start(bf16[192,1920]{1,0:T(8,128)(2,1)} %pad_maximum_fusion.9), channel_id=1, source_target_pairs={{0,4},{4,0},{1,5},{5,1},{2,6},{6,2},{3,7},{7,3},{8,12},{12,8},{9,1... | collective-permute-start | bytes 2211848 | tf_op jit(solution)/shard_map/ppermute | solution.py:1078
  60.2 37.7 %collective-permute-start.13 = (bf16[512,1152]{1,0:T(8,128)(2,1)}, bf16[512,1152]{1,0:T(8,128)(2,1)}, u32[]{:S(2)}, u32[]{:S(2)}) collective-permute-start(bf16[512,1152]{1,0:T(8,128)(2,1)} %pad_maximum_fusion.5), channel_id=1, source_target_pairs={{0,4},{4,0},{1,5},{5,1},{2,6},{6,2},{3,7},{7,3},{8,12},{12,8},{9,1... | collective-permute-start | bytes 3538952 | tf_op jit(solution)/shard_map/ppermute | solution.py:1078
  61.7 21.8 %collective-permute-start.5 = (bf16[256,768]{1,0:T(8,128)(2,1)}, bf16[256,768]{1,0:T(8,128)(2,1)}, u32[]{:S(2)}, u32[]{:S(2)}) collective-permute-start(bf16[256,768]{1,0:T(8,128)(2,1)} %bitcast.375), channel_id=1, source_target_pairs={{0,0},{2,8},{3,16},{1,24},{8,1},{10,9},{11,17},{9,25},{16,2},{18,1... | collective-permute-start | bytes 1179656 | tf_op jit(solution)/shard_map/ppermute | solution.py:1285
  65.0 23.9 %collective-permute-start.16 = (bf16[768,384]{1,0:T(8,128)(2,1)S(1)}, bf16[768,384]{1,0:T(8,128)(2,1)S(1)}, u32[]{:S(2)}, u32[]{:S(2)}) collective-permute-start(bf16[768,384]{1,0:T(8,128)(2,1)S(1)} %pad_maximum_fusion.12), channel_id=1, source_target_pairs={{0,8},{8,0},{16,24},{24,16},{1,9},{9,1},{17,25},{25,17},{2,10},{10... | collective-permute-start | bytes 1769480 | tf_op jit(solution)/shard_map/ppermute | solution.py:1078
  83.5 18.5 %collective-permute-start.8 = (bf16[256,768]{1,0:T(8,128)(2,1)}, bf16[256,768]{1,0:T(8,128)(2,1)S(1)}, u32[]{:S(2)}, u32[]{:S(2)}) collective-permute-start(bf16[256,768]{1,0:T(8,128)(2,1)} %collective-permute-done.5), channel_id=1, source_target_pairs={{0,1},{1,0},{2,3},{3,2},{4,5},{5,4},{6,7},{7,6},{8,9},{9,8},{10,11... | collective-permute-start | bytes 1179656 | tf_op jit(solution)/shard_map/ppermute | solution.py:1078
  84.9 36.2 %collective-permute-start.17 = (bf16[384,1920]{1,0:T(8,128)(2,1)}, bf16[384,1920]{1,0:T(8,128)(2,1)}, u32[]{:S(2)}, u32[]{:S(2)}) collective-permute-start(bf16[384,1920]{1,0:T(8,128)(2,1)} %pad_maximum_fusion.4), channel_id=1, source_target_pairs={{0,8},{8,0},{16,24},{24,16},{1,9},{9,1},{17,25},{25,17},{2,10},{10... | collective-permute-start | bytes 4423688 | tf_op jit(solution)/shard_map/ppermute | solution.py:1078
  90.1 39.2 %collective-permute-start.18 = (bf16[1536,384]{1,0:T(8,128)(2,1)}, bf16[1536,384]{1,0:T(8,128)(2,1)}, u32[]{:S(2)}, u32[]{:S(2)}) collective-permute-start(bf16[1536,384]{1,0:T(8,128)(2,1)} %pad_maximum_fusion.6), channel_id=1, source_target_pairs={{0,4},{4,0},{1,5},{5,1},{2,6},{6,2},{3,7},{7,3},{8,12},{12,8},{9,1... | collective-permute-start | bytes 3538952 | tf_op jit(solution)/shard_map/ppermute | solution.py:1078
  168.0 19.3 %collective-permute-start.25 = (bf16[512,768]{1,0:T(8,128)(2,1)}, bf16[512,768]{1,0:T(8,128)(2,1)}, u32[]{:S(2)}, u32[]{:S(2)}) collective-permute-start(bf16[512,768]{1,0:T(8,128)(2,1)} %multiply_convert_fusion.1.mine_low_ref), channel_id=1, source_target_pairs={{0,2},{1,3},{2,0},{3,1},{4,6},{5,7},{6,4},{7,5},{8,10},{9,11},{10,... | collective-permute-start | bytes 2359304 | tf_op jit(solution)/shard_map/ppermute | solution.py:1078
  168.0 20.9 %collective-permute-start.24 = (bf16[512,768]{1,0:T(8,128)(2,1)}, bf16[512,768]{1,0:T(8,128)(2,1)}, u32[]{:S(2)}, u32[]{:S(2)}) collective-permute-start(bf16[512,768]{1,0:T(8,128)(2,1)} %multiply_convert_fusion.1.mine_low_ref), channel_id=1, source_target_pairs={{0,1},{1,0},{2,3},{3,2},{4,5},{5,4},{6,7},{7,6},{8,9},{9,8},{10,11... | collective-permute-start | bytes 2359304 | tf_op jit(solution)/shard_map/ppermute | solution.py:1078
  319.8 18.8 %collective-permute-start.31 = (bf16[512,768]{1,0:T(8,128)(2,1)S(1)}, bf16[512,768]{1,0:T(8,128)(2,1)S(1)}, u32[]{:S(2)}, u32[]{:S(2)}) collective-permute-start(bf16[512,768]{1,0:T(8,128)(2,1)S(1)} %fusion.42), channel_id=1, source_target_pairs={{0,2},{1,3},{2,0},{3,1},{4,6},{5,7},{6,4},{7,5},{8,10},{9,11},{10,... | collective-permute-start | bytes 2359304 | tf_op jit(solution)/shard_map/ppermute | solution.py:1078
  365.0 34.8 %collective-permute-start.37 = (bf16[2,1,2,96,1536]{4,3,2,1,0:T(8,128)(2,1)}, bf16[2,1,2,96,1536]{4,3,2,1,0:T(8,128)(2,1)}, u32[]{:S(2)}, u32[]{:S(2)}) collective-permute-start(bf16[2,1,2,96,1536]{4,3,2,1,0:T(8,128)(2,1)} %constant_dynamic-slice_fusion.4), channel_id=1, source_target_pairs={{0,8},{8,0},{16,24},{24,16},{1,9},{9,1},{17,25},{25,17},{2,10},{10... | collective-permute-start | bytes 3538952 | tf_op jit(solution)/shard_map/ppermute | solution.py:1078
  366.9 32.9 %collective-permute-start.36 = (bf16[2,2,1,384,384]{4,3,2,1,0:T(8,128)(2,1)}, bf16[2,2,1,384,384]{4,3,2,1,0:T(8,128)(2,1)}, u32[]{:S(2)}, u32[]{:S(2)}) collective-permute-start(bf16[2,2,1,384,384]{4,3,2,1,0:T(8,128)(2,1)} %constant_dynamic-slice_fusion.5), channel_id=1, source_target_pairs={{0,4},{4,0},{1,5},{5,1},{2,6},{6,2},{3,7},{7,3},{8,12},{12,8},{9,1... | collective-permute-start | bytes 3538952 | tf_op jit(solution)/shard_map/ppermute | solution.py:1078
  413.2 15.2 %collective-permute-start.38 = (bf16[2,1,1,384,384]{4,3,2,1,0:T(8,128)(2,1)S(1)}, bf16[2,1,1,384,384]{4,3,2,1,0:T(8,128)(2,1)}, u32[]{:S(2)}, u32[]{:S(2)}) collective-permute-start(bf16[2,1,1,384,384]{4,3,2,1,0:T(8,128)(2,1)S(1)} %dynamic-slice_convert_fusion.2), channel_id=1, source_target_pairs={{0,8},{8,0},{16,24},{24,16},{1,9},{9,1},{17,25},{25,17},{2,10},{10... | collective-permute-start | bytes 1769480 | tf_op jit(solution)/shard_map/ppermute | solution.py:1078
  431.1 22.1 %collective-permute-start.49 = (bf16[2,1,2,96,384]{4,3,2,1,0:T(8,128)(2,1)}, bf16[2,1,2,96,384]{4,3,2,1,0:T(8,128)(2,1)}, u32[]{:S(2)}, u32[]{:S(2)}) collective-permute-start(bf16[2,1,2,96,384]{4,3,2,1,0:T(8,128)(2,1)} %constant_dynamic-slice_fusion), channel_id=1, source_target_pairs={{0,8},{8,0},{16,24},{24,16},{1,9},{9,1},{17,25},{25,17},{2,10},{10... | collective-permute-start | bytes 884744 | tf_op jit(solution)/shard_map/ppermute | solution.py:1078
  434.6 53.5 %collective-permute-start.53 = (bf16[1,1,1,384,384]{4,3,2,1,0:T(8,128)(2,1)}, bf16[1,1,1,384,384]{4,3,2,1,0:T(8,128)(2,1)}, u32[]{:S(2)}, u32[]{:S(2)}) collective-permute-start(bf16[1,1,1,384,384]{4,3,2,1,0:T(8,128)(2,1)} %dynamic-slice_convert_fusion.4), channel_id=1, source_target_pairs={{0,16},{8,24},{16,0},{24,8},{1,17},{9,25},{17,1},{25,9},{2,18},{10... | collective-permute-start | bytes 884744 | tf_op jit(solution)/shard_map/ppermute | solution.py:1078
  446.1 22.3 %collective-permute-start.41 = (bf16[2,2,1,104,1152]{4,3,2,1,0:T(8,128)(2,1)S(1)}, bf16[2,2,1,104,1152]{4,3,2,1,0:T(8,128)(2,1)S(1)}, u32[]{:S(2)}, u32[]{:S(2)}) collective-permute-start(bf16[2,2,1,104,1152]{4,3,2,1,0:T(8,128)(2,1)S(1)} %fusion.39), channel_id=1, source_target_pairs={{0,4},{4,0},{1,5},{5,1},{2,6},{6,2},{3,7},{7,3},{8,12},{12,8},{9,1... | collective-permute-start | bytes 2875400 | tf_op jit(solution)/shard_map/ppermute | solution.py:1078
  447.8 15.4 %collective-permute-start.57 = (bf16[264,768]{1,0:T(8,128)(2,1)S(1)}, bf16[264,768]{1,0:T(8,128)(2,1)S(1)}, u32[]{:S(2)}, u32[]{:S(2)}) collective-permute-start(bf16[264,768]{1,0:T(8,128)(2,1)S(1)} %fusion.43), channel_id=1, source_target_pairs={{0,0},{1,16},{2,8},{3,24},{8,2},{9,18},{10,10},{11,26},{16,3},{17,... | collective-permute-start | bytes 1216520 | tf_op jit(solution)/shard_map/ppermute | solution.py:1437
  453.0 36.1 %collective-permute-start.47 = (bf16[1,1,1,96,1536]{4,3,2,1,0:T(8,128)(2,1)S(1)}, bf16[1,1,1,96,1536]{4,3,2,1,0:T(8,128)(2,1)S(1)}, u32[]{:S(2)}, u32[]{:S(2)}) collective-permute-start(bf16[1,1,1,96,1536]{4,3,2,1,0:T(8,128)(2,1)S(1)} %dynamic-slice_convert_fusion.5), channel_id=1, source_target_pairs={{0,16},{8,24},{16,0},{24,8},{1,17},{9,25},{17,1},{25,9},{2,18},{10... | collective-permute-start | bytes 884744 | tf_op jit(solution)/shard_map/ppermute | solution.py:1078
  454.3 19.6 %collective-permute-start.51 = (bf16[2,1,1,96,384]{4,3,2,1,0:T(8,128)(2,1)S(1)}, bf16[2,1,1,96,384]{4,3,2,1,0:T(8,128)(2,1)S(1)}, u32[]{:S(2)}, u32[]{:S(2)}) collective-permute-start(bf16[2,1,1,96,384]{4,3,2,1,0:T(8,128)(2,1)S(1)} %dynamic-slice_convert_fusion.7), channel_id=1, source_target_pairs={{0,4},{4,0},{1,5},{5,1},{2,6},{6,2},{3,7},{7,3},{8,12},{12,8},{9,1... | collective-permute-start | bytes 442376 | tf_op jit(solution)/shard_map/ppermute | solution.py:1078
  468.6 19.4 %collective-permute-start.42 = (bf16[2,1,1,104,1152]{4,3,2,1,0:T(8,128)(2,1)S(1)}, bf16[2,1,1,104,1152]{4,3,2,1,0:T(8,128)(2,1)S(1)}, u32[]{:S(2)}, u32[]{:S(2)}) collective-permute-start(bf16[2,1,1,104,1152]{4,3,2,1,0:T(8,128)(2,1)S(1)} %dynamic-slice_convert_fusion.3), channel_id=1, source_target_pairs={{0,8},{8,0},{16,24},{24,16},{1,9},{9,1},{17,25},{25,17},{2,10},{10... | collective-permute-start | bytes 1437704 | tf_op jit(solution)/shard_map/ppermute | solution.py:1078
  (105 other events, 756.6 us)
